TPU v7x, 128 devices: a whole 4x4x4 slice. The times are simulated.
128 devices in a mesh: ha: 8 (over z, core), wa: 16 (over y, x).
Axes of the slice: x: 4, y: 4, z: 4, core: 2. Of those that a mesh axis runs over, the one named last changes fastest.
Arguments:
- frames_in: bfloat16 [1, 240, 640, 128], P(None, 'ha', 'wa'), may hold values from -6 to 6
- cache_in: bfloat16 [2, 240, 640, 128], P(None, 'ha', 'wa'), may hold values from -6 to 6
- cache_mid: bfloat16 [2, 240, 640, 128], P(None, 'ha', 'wa'), may hold values from -6 to 6
- w_first: bfloat16 [3, 3, 3, 128, 128], replicated, may hold values from -0.109375 to 0.109375
- w_second: bfloat16 [3, 3, 3, 128, 128], replicated, may hold values from -0.109375 to 0.109375
- scale_first: float32 [1, 128], replicated, may hold values from -0.5 to 0.5
- shift_first: float32 [1, 128], replicated, may hold values from -3 to 3
- scale_second: float32 [1, 128], replicated, may hold values from -0.5 to 0.5
- shift_second: float32 [1, 128], replicated, may hold values from -3 to 3
- cotangent: bfloat16 [1, 240, 640, 128], P(None, 'ha', 'wa'), may hold values from -6 to 6
Outputs:
- grad_input: bfloat16 [1, 240, 640, 128], P(None, 'ha', 'wa')
- grad_first: float32 [3, 3, 3, 128, 128], replicated
- grad_second: float32 [3, 3, 3, 128, 128], replicated
All inputs are finite; a program needn't handle non-finite values.
Results may differ from a plain program's by a relative error of at most 0.0058.
Values may be sent and summed in bfloat16 or wider, within the bound.
No kernel may reach another device: no remote copies, remote signals or barrier semaphores. Data moves between devices by JAX's collectives and lax.ppermute only.
A program may use at most 128 MiB of HBM per device.

v0:
```python
import jax
import jax.numpy as jnp
from jax import lax
from jax.experimental import pallas as pl
from jax.experimental.pallas import tpu as pltpu
from jax.sharding import PartitionSpec as P

BF = jnp.bfloat16
F32 = jnp.float32
RIM = 4
BOTH = ("ha", "wa")


def swaps(axis):
    count = lax.axis_size(axis)
    first = [(i, i ^ 1) for i in range(count)]
    second = [(i, i + 1 if i % 2 else i - 1) for i in range(1, count - 1)]
    return first, second


def trade(axis, near, far):
    first, second = swaps(axis)
    return lax.ppermute(near, axis, first), lax.ppermute(far, axis, second)


def is_odd(axis):
    return lax.axis_index(axis) % 2 == 1


def slope(value):
    sig = jax.nn.sigmoid(value)
    return sig * (1.0 + value * (1.0 - sig))


def flat(value):
    return value.reshape(-1, value.shape[-1])


def turn(value, step):
    return pltpu.roll(value, step % value.shape[1], 1)


def join(block, near, far):
    high, _, lanes = block[0].shape
    odd = is_odd("wa")
    near, far = near.astype(F32), far.astype(F32)
    left = jnp.where(odd, near, far).reshape(high, 3, 2 * RIM, lanes)
    right = jnp.where(odd, far, near).reshape(high, 3, 2 * RIM, lanes)
    lower = lax.broadcasted_iota(jnp.int32, (high, 2 * RIM, lanes), 1) < RIM
    frames = []
    for frame in range(6):
        one, other = right[:, frame // 2], left[:, frame // 2]
        if frame % 2 == 0:
            rim = jnp.where(lower, one, pltpu.roll(other, RIM, 1))
        else:
            rim = jnp.where(lower, pltpu.roll(one, RIM, 1), other)
        frames.append(jnp.concatenate([block[frame].astype(F32), rim], axis=1).astype(BF))
    return frames


class Rows:
    def __init__(self, *pieces):
        self.pieces = pieces

    def get(self, start, count):
        out = []
        for first, ref, size in self.pieces:
            low, high = max(start, first), min(start + count, first + size)
            if low < high:
                out.append(ref[low - first : high - first])
        return out[0] if len(out) == 1 else jnp.concatenate(out, axis=0)


class Frame:
    def __init__(self, ref, index):
        self.ref, self.index = ref, index

    def __getitem__(self, key):
        return self.ref[self.index, key]


def forward(frames, weight, blocks):
    lhs = jnp.concatenate(
        [
            jnp.concatenate(
                [flat(frames[a].get(start - 1 + b, count)) for start, count in blocks], axis=0
            )
            for a in range(3)
            for b in range(3)
        ],
        axis=1,
    )
    out = jnp.dot(lhs, weight[...], preferred_element_type=F32)
    return gather_columns(out, 1)


def backward(field, weight, start, count):
    lhs = jnp.concatenate([flat(field.get(start + 1 - b, count)) for b in range(3)], axis=1)
    out = lax.dot_general(lhs, weight[...], (((1,), (1,)), ((), ())), preferred_element_type=F32)
    return gather_columns(out, -1)


def gather_columns(out, step):
    lanes = out.shape[-1] // 3
    out = out.reshape(-1, FULL[0], 3 * lanes)
    return (
        turn(out[..., :lanes], step)
        + out[..., lanes : 2 * lanes]
        + turn(out[..., 2 * lanes :], -step)
    )


FULL = [0]


def in_image(rows, cols, lanes, blocks):
    full = cols + 2 * RIM
    image_rows, image_cols = rows * lax.axis_size("ha"), cols * lax.axis_size("wa")
    col = lax.broadcasted_iota(jnp.int32, (1, full, lanes), 1)
    place = jnp.where(col < cols + RIM, col, col - full) + lax.axis_index("wa") * cols
    col_in = (place >= 0) & (place < image_cols)
    out = []
    for start, count in blocks:
        row = lax.broadcasted_iota(jnp.int32, (count, full, lanes), 0)
        row = row + (start - RIM) + lax.axis_index("ha") * rows
        out.append((row >= 0) & (row < image_rows) & col_in)
    return jnp.concatenate(out, axis=0) if len(out) > 1 else out[0]


def first_layer(rows, cols, frames, weight, affine, blocks):
    lanes = affine.shape[-1]
    gain, bias = (affine[i : i + 1, :].reshape(1, 1, lanes) for i in (0, 1))
    m_one = forward(frames, weight, blocks) * gain + bias
    sig = jax.nn.sigmoid(m_one)
    inside = in_image(rows, cols, lanes, blocks)
    a_one = jnp.where(inside, m_one * sig, 0.0).astype(BF)
    slope_one = jnp.where(inside, sig * (1.0 + m_one * (1.0 - sig)) * gain, 0.0)
    return a_one, slope_one


def second_layer(frames, cot, weight, affine, blocks):
    lanes = affine.shape[-1]
    gain, bias = (affine[i : i + 1, :].reshape(1, 1, lanes) for i in (2, 3))
    m_two = forward(frames, weight, blocks) * gain + bias
    pulled = [cot.get(start, count) for start, count in blocks]
    pulled = jnp.concatenate(pulled, axis=0) if len(pulled) > 1 else pulled[0]
    return pulled.astype(F32) * slope(m_two) * gain


def spread(cols, value):
    own = lax.broadcasted_iota(jnp.int32, (1,) + value.shape[1:], 1) < cols
    kept = jnp.where(own, value, 0.0)
    return jnp.concatenate([turn(kept, -1), kept, turn(kept, 1)], axis=2).astype(BF)


def cut(start, stop, parts):
    step = -(-(stop - start) // parts)
    return [(at, min(step, stop - at)) for at in range(start, stop, step)]


def pack_kernel(
    rows, cols, cache_in_at, frames_in_at, cache_mid_at, cot_at, row_near, row_far, col_near, col_far,
    cache_in, frames_in, cache_mid, cot, sems,
):
    copies = [
        pltpu.make_async_copy(source, target, sems.at[i])
        for i, (source, target) in enumerate(
            (
                (cache_in_at, cache_in),
                (frames_in_at, frames_in),
                (cache_mid_at, cache_mid),
                (cot_at, cot),
            )
        )
    ]
    for copy in copies:
        copy.start()
    for copy in copies:
        copy.wait()
    odd_row, odd_col = is_odd("ha"), is_odd("wa")
    sources = (
        (cache_in, 0), (cache_in, 1), (frames_in, 0), (cache_mid, 0), (cache_mid, 1), (cot, 0)
    )
    last = rows - RIM
    near_at, far_at = jnp.where(odd_row, 0, last), jnp.where(odd_row, last, 0)
    for frame, (ref, i) in enumerate(sources):
        row_near[frame] = ref[i, pl.ds(near_at, RIM)]
        row_far[frame] = ref[i, pl.ds(far_at, RIM)]
    lanes = col_near.shape[-1]
    lower = lax.broadcasted_iota(jnp.int32, (rows, 2 * RIM, lanes), 1) < RIM

    def edges(frame):
        ref, i = sources[frame]
        value = ref[i].astype(F32)
        return value[:, : 2 * RIM], pltpu.roll(value[:, cols - 2 * RIM :], RIM, 1)

    near, far = [], []
    for pair in range(3):
        (head, tail), (head_b, tail_b) = edges(2 * pair), edges(2 * pair + 1)
        heads = jnp.where(lower, head, pltpu.roll(head_b, RIM, 1))
        tails = jnp.where(lower, tail, pltpu.roll(tail_b, RIM, 1))
        near.append(jnp.where(odd_col, heads, tails))
        far.append(jnp.where(odd_col, tails, heads))
    col_near[...] = jnp.stack(near, axis=1).reshape(-1, lanes).astype(BF)
    col_far[...] = jnp.stack(far, axis=1).reshape(-1, lanes).astype(BF)


def ready_kernel(
    w_one, w_two, sc_one, sh_one, sc_two, sh_two, ahead_one, ahead_two, back_one, back_two, affine
):
    lanes = affine.shape[-1]
    for weight, ahead, back in ((w_one, ahead_one, back_one), (w_two, ahead_two, back_two)):
        for a in range(3):
            for b in range(3):
                for c in range(3):
                    at = (a * 3 + b) * lanes
                    ahead[at : at + lanes, c * lanes : (c + 1) * lanes] = weight[a, b, c]
        for b in range(3):
            for c in range(3):
                back[c * lanes : (c + 1) * lanes, b * lanes : (b + 1) * lanes] = weight[2, b, c]
    affine[...] = jnp.concatenate(
        [1.0 + sc_one[...], sh_one[...], 1.0 + sc_two[...], sh_two[...]] * 2, axis=0
    )


def middle_kernel(
    rows, cols, cache_in, frames_in, cache_mid, cot, col_near, col_far, ahead_one, ahead_two, affine,
    field, slope_mid, a_mid, d_mid, moved_mid,
):
    block = [cache_in[0], cache_in[1], frames_in[0], cache_mid[0], cache_mid[1], cot[0]]
    for frame, value in enumerate(join(block, col_near[...], col_far[...])):
        field[frame] = value
    own = [Rows((RIM, Frame(field, i), rows)) for i in range(6)]
    first = RIM + 1
    for start, count in cut(first, RIM + rows - 1, 2):
        a_one, slope_one = first_layer(rows, cols, own[:3], ahead_one, affine, [(start, count)])
        a_mid[start - first : start - first + count] = a_one
        slope_mid[start - first : start - first + count] = slope_one
    frames = own[3:5] + [Rows((first, a_mid, rows - 2))]
    second = RIM + 2
    for start, count in cut(second, RIM + rows - 2, 2):
        value = second_layer(frames, own[5], ahead_two, affine, [(start, count)])
        d_mid[start - second : start - second + count] = value.astype(BF)
        moved_mid[start - second : start - second + count] = spread(cols, value)


def rim_kernel(
    rows, cols, field, slope_mid, a_mid, d_mid, moved_mid, row_near, row_far, corner_near, corner_far,
    ahead_one, ahead_two, back_two, affine, keep, send, d_one,
    top, bottom, slope_rim, a_rim, d_rim, moved_rim, moved_one, grads, sems,
):
    lanes = affine.shape[-1]
    tall = rows + 2 * RIM
    half = corner_near.shape[0] // 2

    def assemble(target, block, corner):
        parts = join([block[i] for i in range(6)], corner[:half], corner[half:])
        for frame, value in enumerate(parts):
            target[frame] = value

    @pl.when(is_odd("ha"))
    def _():
        assemble(top, row_near, corner_near)
        assemble(bottom, row_far, corner_far)

    @pl.when(jnp.logical_not(is_odd("ha")))
    def _():
        assemble(top, row_far, corner_far)
        assemble(bottom, row_near, corner_near)

    whole = [
        Rows(
            (0, Frame(top, i), RIM),
            (RIM, Frame(field, i), rows),
            (RIM + rows, Frame(bottom, i), RIM),
        )
        for i in range(6)
    ]

    def around(rim, mid, first, count):
        size = mid.shape[0]
        return Rows(
            (first, rim, count),
            (first + count, mid, size),
            (first + count + size, Shifted(rim, count), count),
        )

    used = 27 * lanes
    if grads.shape[1] > used:
        grads[:, used:, :] = jnp.zeros((2, grads.shape[1] - used, lanes), BF)
    edge = jnp.zeros((2,) + moved_rim.shape[1:], BF)
    moved_rim[0:2] = edge
    moved_rim[6:8] = edge
    moved_one[0:2] = edge
    moved_one[rows + 2 : rows + 4] = edge

    def gradient(which, frames, moved):
        lhs = jnp.concatenate([flat(frames[a].get(RIM - 1, rows + 2)) for a in range(3)], axis=1)
        for b in range(3):
            rhs = flat(moved.get(RIM - b, rows + 2))
            out = lax.dot_general(lhs, rhs, (((0,), (0,)), ((), ())), preferred_element_type=F32)
            for a in range(3):
                for c in range(3):
                    at = ((a * 3 + b) * 3 + c) * lanes
                    grads[which, at : at + lanes, :] = out[
                        a * lanes : (a + 1) * lanes, c * lanes : (c + 1) * lanes
                    ].astype(BF)

    blocks = [(1, 4), (tall - 5, 4)]
    a_value, slope_value = first_layer(rows, cols, whole[:3], ahead_one, affine, blocks)
    a_rim[...] = a_value
    slope_rim[...] = slope_value
    a_all = around(a_rim, a_mid, 1, 4)
    slope_all = around(slope_rim, slope_mid, 1, 4)

    frames = whole[3:5] + [a_all]
    value = second_layer(frames, whole[5], ahead_two, affine, [(2, 4), (tall - 6, 4)])
    d_rim[...] = value.astype(BF)
    moved_rim[2:6] = spread(cols, value[2:6])
    d_all = around(d_rim, d_mid, 2, 4)
    gradient(1, frames, around(moved_rim, moved_mid, 2, 4))

    for start, count in cut(3, tall - 3, 2):
        value = backward(d_all, back_two, start, count) * slope_all.get(start, count)
        d_one[start - 3 : start - 3 + count] = value.astype(BF)
        low, high = max(start, RIM), min(start + count, RIM + rows)
        moved_one[low - 2 : high - 2] = spread(cols, value[low - start : high - start])
    gradient(0, whole[:3], Rows((2, moved_one, rows + 4)))

    core = lax.axis_index("ha") % 2
    copies = [
        pltpu.make_async_copy(grads.at[core], keep, sems.at[0]),
        pltpu.make_async_copy(grads.at[1 - core], send, sems.at[1]),
    ]
    for copy in copies:
        copy.start()
    for copy in copies:
        copy.wait()


class Shifted:
    def __init__(self, ref, by):
        self.ref, self.by = ref, by

    def __getitem__(self, key):
        return self.ref[key.start + self.by : key.stop + self.by]


def input_kernel(rows, cols, d_one, back_one, gin):
    field = Rows((RIM - 1, d_one, rows + 2))
    for start, count in cut(RIM, RIM + rows, 2):
        value = backward(field, back_one, start, count)
        gin[0, start - RIM : start - RIM + count] = value[:, :cols].astype(BF)


def per_device(
    frames_in, cache_in, cache_mid, w_first, w_second,
    scale_first, shift_first, scale_second, shift_second, cotangent,
):
    _, rows, cols, chans = frames_in.shape
    devices = lax.axis_size("ha") * lax.axis_size("wa")
    factor = 1.0 / (rows * cols * devices) ** 0.5
    full, tall = cols + 2 * RIM, rows + 2 * RIM
    FULL[0] = full
    chips = devices // 2
    total = 27 * chans
    share = -(-total // (8 * chips)) * 8
    inner = pl.BlockSpec(memory_space=pltpu.VMEM)
    anywhere = pl.BlockSpec(memory_space=pl.ANY)

    def shaped(*shape, dtype=BF):
        return jax.ShapeDtypeStruct(shape, dtype)

    def call(kernel, name, out_shape, mebibytes, flops, args, sizes=True, **kwargs):
        def body(*refs):
            kernel(rows, cols, *refs) if sizes else kernel(*refs)

        count = len(out_shape)
        kwargs.setdefault("in_specs", [inner] * len(args))
        kwargs.setdefault("out_specs", (inner,) * count)
        return pl.pallas_call(
            body,
            out_shape=tuple(out_shape),
            cost_estimate=pl.CostEstimate(
                flops=int(flops), bytes_accessed=8 * 10**6, transcendentals=0
            ),
            compiler_params=pltpu.CompilerParams(vmem_limit_bytes=mebibytes * 2**20),
            name=name,
            **kwargs,
        )(*args)

    fields = (cache_in, frames_in, cache_mid, cotangent)
    rim_rows, rim_cols = shaped(6, RIM, cols, chans), shaped(6 * rows * RIM, chans)
    row_near, row_far, col_near, col_far = call(
        pack_kernel, "pack", (rim_rows, rim_rows, rim_cols, rim_cols), 60, 1e9, fields,
        in_specs=[anywhere] * 4,
        scratch_shapes=[pltpu.VMEM(v.shape, BF) for v in fields] + [pltpu.SemaphoreType.DMA((4,))],
    )
    ahead, back = shaped(9 * chans, 3 * chans), shaped(3 * chans, 3 * chans)
    ahead_one, ahead_two, back_one, back_two, affine = call(
        ready_kernel, "ready", (ahead, ahead, back, back, shaped(8, chans, dtype=F32)), 16, 2e9,
        (w_first, w_second, scale_first, shift_first, scale_second, shift_second), sizes=False,
    )
    col_near, col_far = trade("wa", col_near, col_far)
    row_near, row_far = trade("ha", row_near, row_far)
    size = 6 * RIM * RIM
    head = jnp.concatenate([col_near[:size], col_far[:size]], axis=0)
    tail = jnp.concatenate([col_near[-size:], col_far[-size:]], axis=0)
    odd = is_odd("ha")
    corner_near, corner_far = trade("ha", jnp.where(odd, head, tail), jnp.where(odd, tail, head))

    field, slope_mid, a_mid, d_mid, moved_mid = call(
        middle_kernel, "middle",
        (
            shaped(6, rows, full, chans),
            shaped(rows - 2, full, chans, dtype=F32),
            shaped(rows - 2, full, chans),
            shaped(rows - 4, full, chans),
            shaped(rows - 4, full, 3 * chans),
        ),
        28, 5e9, (*fields, col_near, col_far, ahead_one, ahead_two, affine),
    )
    keep, send, d_one = call(
        rim_kernel, "rim",
        (shaped(share * chips, chans), shaped(share * chips, chans), shaped(rows + 2, full, chans)),
        28, 5e9,
        (
            field, slope_mid, a_mid, d_mid, moved_mid, row_near, row_far, corner_near, corner_far,
            ahead_one, ahead_two, back_two, affine,
        ),
        out_specs=(anywhere, anywhere, inner),
        scratch_shapes=[
            pltpu.VMEM((6, RIM, full, chans), BF),
            pltpu.VMEM((6, RIM, full, chans), BF),
            pltpu.VMEM((8, full, chans), F32),
            pltpu.VMEM((8, full, chans), BF),
            pltpu.VMEM((8, full, chans), BF),
            pltpu.VMEM((8, full, 3 * chans), BF),
            pltpu.VMEM((rows + 4, full, 3 * chans), BF),
            pltpu.VMEM((2, share * chips, chans), BF),
            pltpu.SemaphoreType.DMA((2,)),
        ],
    )

    pairs, _ = swaps("ha")
    got = lax.ppermute(send, "ha", pairs)
    (grad_input,) = call(
        input_kernel, "input", (shaped(1, rows, cols, chans),), 28, 1e9, (d_one, back_one)
    )
    chip_sum = (keep.astype(F32) + got.astype(F32)).astype(BF)
    cores = [[c for c in range(devices) if (c // lax.axis_size("wa")) % 2 == k] for k in range(2)]

    def spread_out(value):
        return lax.all_to_all(
            value.reshape(chips, share, chans), BOTH, 0, 0, axis_index_groups=cores, tiled=True
        )

    mine = (jnp.sum(spread_out(chip_sum).astype(F32), axis=0) * factor).astype(BF)
    one = spread_out(jnp.broadcast_to(mine[None], (chips, share, chans))).reshape(-1, chans)
    other = lax.ppermute(one, "ha", pairs)
    even = jnp.logical_not(odd)
    shape = (3, 3, 3, chans, chans)
    one, other = one[:total].astype(F32), other[:total].astype(F32)
    grad_first = jnp.where(even, one, other).reshape(shape)
    grad_second = jnp.where(even, other, one).reshape(shape)
    return (grad_input, grad_first, grad_second)


def solution(mesh):
    tiled = P(None, "ha", "wa", None)
    return jax.shard_map(
        per_device,
        mesh=mesh,
        in_specs=(tiled, tiled, tiled, P(), P(), P(), P(), P(), P(), tiled),
        out_specs=(tiled, P(), P()),
        check_vma=False,
    )
```

profile of v0, /device:TPU:1, one launch (start us, length us, event | category | flops | bytes accessed | tf_op | source)
XLA Modules:
  0.0 88.8 jit_solution(16696382629480637965)
XLA Ops:
  0.6 0.0 copy-start.9
  0.6 0.0 copy-start.8
  0.7 0.0 copy-start.7
  0.7 0.0 copy-start.6
  0.7 0.0 copy-start.1
  0.7 0.0 copy-start
  0.7 2.5 %pack.1 = (bf16[6,4,40,128]{3,2,1,0:T(8,128)(2,1)}, bf16[6,4,40,128]{3,2,1,0:T(8,128)(2,1)}, bf16[720,128]{1,0:T(8,128)(2,1)}, bf16[720,128]{1,0:T(8,128)(2,1)}) custom-call(bf16[2,30,40,128]{3,2,1,0:T(8,128)(2,1)} %refs_0_.5, bf16[1,30,40,128]{3,2,1,0:T(8,128)(2,1)} %refs_1_.5, bf16[2,30,40,128]{3,2,1,0:T(8,128)(2,1)} %refs_2_.5, ...), custom_call_target="tpu_custom_call" | custom-call | flops 1000000000 | bytes 8000000 | tf_op jit(solution)/shard_map/pack/pallas_call | solution.py:381
  3.2 2.1 %collective-permute-start = (bf16[720,128]{1,0:T(8,128)(2,1)}, bf16[720,128]{1,0:T(8,128)(2,1)S(1)}, u32[]{:S(2)}, u32[]{:S(2)}) collective-permute-start(bf16[720,128]{1,0:T(8,128)(2,1)} %get-tuple-element.20), channel_id=1, source_target_pairs={{0,1},{1,0},{2,3},{3,2},{4,5},{5,4},{6,7},{7,6},{8,9},{9,8},{10,11... | collective-permute-start | bytes 552968 | tf_op jit(solution)/shard_map/ppermute | solution.py:23
  5.4 0.7 collective-permute-start.1
  6.0 1.0 %collective-permute-start.2 = (bf16[6,4,40,128]{3,2,1,0:T(8,128)(2,1)}, bf16[6,4,40,128]{3,2,1,0:T(8,128)(2,1)S(1)}, u32[]{:S(2)}, u32[]{:S(2)}) collective-permute-start(bf16[6,4,40,128]{3,2,1,0:T(8,128)(2,1)} %get-tuple-element.30), channel_id=1, source_target_pairs={{0,16},{16,0},{32,48},{48,32},{64,80},{80,64},{96,112},{112,96},{1... | collective-permute-start | bytes 737288 | tf_op jit(solution)/shard_map/ppermute | solution.py:23
  7.1 3.4 %collective-permute-start.3 = (bf16[6,4,40,128]{3,2,1,0:T(8,128)(2,1)}, bf16[6,4,40,128]{3,2,1,0:T(8,128)(2,1)S(1)}, u32[]{:S(2)}, u32[]{:S(2)}) collective-permute-start(bf16[6,4,40,128]{3,2,1,0:T(8,128)(2,1)} %get-tuple-element.31), channel_id=1, source_target_pairs={{16,32},{32,16},{48,64},{64,48},{80,96},{96,80},{17,33},{33,17},{4... | collective-permute-start | bytes 737288 | tf_op jit(solution)/shard_map/ppermute | solution.py:23
  10.5 0.0 copy-done.9
  10.5 0.0 copy-done.8
  10.5 0.0 copy-done.7
  10.5 0.0 copy-done.6
  10.6 0.0 copy-done.1
  10.6 0.0 copy-done
  10.6 0.0 copy-start.2
  10.6 0.0 copy-start.3
  10.6 0.0 copy-start.4
  10.6 0.0 copy-start.5
  10.6 0.4 ready.1
  11.0 0.0 collective-permute-done.refs_4_
  11.0 0.0 collective-permute-done.1.refs_5_
  11.1 3.8 %collective-permute-start.5 = (bf16[192,128]{1,0:T(8,128)(2,1)S(1)}, bf16[192,128]{1,0:T(8,128)(2,1)S(1)}, u32[]{:S(2)}, u32[]{:S(2)}) collective-permute-start(bf16[192,128]{1,0:T(8,128)(2,1)S(1)} %get-tuple-element.43), channel_id=1, source_target_pairs={{16,32},{32,16},{48,64},{64,48},{80,96},{96,80},{17,33},{33,17},{4... | collective-permute-start | bytes 147464 | tf_op jit(solution)/shard_map/ppermute | solution.py:23
  14.9 0.1 collective-permute-start.4
  15.0 0.0 copy-done.2
  15.0 0.0 copy-done.3
  15.0 0.0 copy-done.4
  15.0 0.0 copy-done.5
  15.0 4.2 %middle.1 = (bf16[6,30,48,128]{3,2,1,0:T(8,128)(2,1)S(1)}, f32[28,48,128]{2,1,0:T(8,128)S(1)}, bf16[28,48,128]{2,1,0:T(8,128)(2,1)S(1)}, bf16[26,48,128]{2,1,0:T(8,128)(2,1)S(1)}, bf16[26,48,384]{2,1,0:T(8,128)(2,1)S(1)}) custom-call(bf16[2,30,40,128]{3,2,1,0:T(8,128)(2,1)S(1)} %copy-done.2, bf16[1,30,40,128]{3,2,1,0:T(8,128)(2,1)S(1)} %copy-done.4, ...), custom_call_target="tpu_custom_call" | custom-call | flops 5000000000 | bytes 8000000 | tf_op jit(solution)/shard_map/middle/pallas_call | solution.py:381
  19.2 0.0 collective-permute-done.5.refs_8_
  19.2 0.0 collective-permute-done.4.refs_7_
  19.2 0.0 collective-permute-done.2.refs_5_
  19.2 0.0 collective-permute-done.3.refs_6_
  19.2 6.5 %rim.1 = (bf16[3584,128]{1,0:T(8,128)(2,1)S(1)}, bf16[3584,128]{1,0:T(8,128)(2,1)S(1)}, bf16[32,48,128]{2,1,0:T(8,128)(2,1)S(1)}) custom-call(bf16[6,30,48,128]{3,2,1,0:T(8,128)(2,1)S(1)} %get-tuple-element.25.refs_0_, f32[28,48,128]{2,1,0:T(8,128)S(1)} %get-tuple-element.26.refs_1_, bf16[28,48,128]{2,1,0:T(8,128)(2,1)S(1)} %get-tuple-element.27.refs_2_, ...), custom_call_target="tpu_custom_call" | custom-call | flops 5000000000 | bytes 8000000 | tf_op jit(solution)/shard_map/rim/pallas_call | solution.py:381
  25.7 0.5 collective-permute-start.6
  26.3 2.1 %collective-permute-done.6 = bf16[3584,128]{1,0:T(8,128)(2,1)S(1)} collective-permute-done((bf16[3584,128]{1,0:T(8,128)(2,1)S(1)}, bf16[3584,128]{1,0:T(8,128)(2,1)S(1)}, u32[]{:S(2)}, u32[]{:S(2)}) %collective-permute-start.6) | collective-permute-done | bytes 917536 | tf_op jit(solution)/shard_map/ppermute | solution.py:446
  28.4 0.2 add_convert_fusion
  28.6 31.4 %all_to_all.10 = bf16[64,56,128]{2,1,0:T(8,128)(2,1)S(1)} all-to-all(bf16[64,56,128]{2,1,0:T(8,128)(2,1)S(1)} %bitcast.4), channel_id=1, replica_groups={{0,1,2,3,4,5,6,7,8,9,10,11,12,13,14,15,32,33,34,35,36,37,38,39,40,41,42..., dimensions={0} | all-to-all | bytes 1835008 | tf_op jit(solution)/shard_map/all_to_all | solution.py:454
  60.0 0.2 convert_reduce_fusion
  60.2 0.1 broadcast_in_dim.2
  60.3 19.9 %all_to_all.11 = bf16[64,56,128]{2,1,0:T(8,128)(2,1)} all-to-all(bf16[64,56,128]{2,1,0:T(8,128)(2,1)S(1)} %broadcast_in_dim.2), channel_id=1, replica_groups={{0,1,2,3,4,5,6,7,8,9,10,11,12,13,14,15,32,33,34,35,36,37,38,39,40,41,42..., dimensions={0} | all-to-all | bytes 1835008 | tf_op jit(solution)/shard_map/all_to_all | solution.py:454
  80.2 3.1 %collective-permute-start.7 = (bf16[3584,128]{1,0:T(8,128)(2,1)}, bf16[3584,128]{1,0:T(8,128)(2,1)S(1)}, u32[]{:S(2)}, u32[]{:S(2)}) collective-permute-start(bf16[3584,128]{1,0:T(8,128)(2,1)} %bitcast.1), channel_id=1, source_target_pairs={{0,16},{16,0},{32,48},{48,32},{64,80},{80,64},{96,112},{112,96},{1... | collective-permute-start | bytes 2752520 | tf_op jit(solution)/shard_map/ppermute | solution.py:460
  83.3 1.7 %input.1 = bf16[1,30,40,128]{3,2,1,0:T(8,128)(2,1)} custom-call(bf16[32,48,128]{2,1,0:T(8,128)(2,1)S(1)} %get-tuple-element.33.refs_0_, bf16[384,384]{1,0:T(8,128)(2,1)S(1)} %get-tuple-element.34.refs_1_), custom_call_target="tpu_custom_call" | custom-call | flops 1000000000 | bytes 8000000 | tf_op jit(solution)/shard_map/input/pallas_call | solution.py:381
  84.9 0.7 collective-permute-done.7
  85.6 3.2 %convert_select_fusion = (f32[3456,128]{1,0:T(8,128)}, f32[3456,128]{1,0:T(8,128)}) fusion(pred[]{:T(512)S(6)} %not.3, bf16[3584,128]{1,0:T(8,128)(2,1)S(1)} %collective-permute-done.7, bf16[3584,128]{1,0:T(8,128)(2,1)} %bitcast.1), kind=kLoop, calls=%fused_computation | loop fusion | flops 1769472 | bytes 5308417 | tf_op jit(solution)/shard_map/jit(_where)/select_n | solution.py:465
  (4 shorter events, 0.0 us)
Async XLA Ops:
  0.6 9.9 %copy-start.9 = (f32[1,128]{1,0:T(1,128)S(1)}, f32[1,128]{1,0:T(1,128)}, u32[]{:S(2)}) copy-start(f32[1,128]{1,0:T(1,128)} %refs_5_.1) | copy-start | bytes 1540
  0.6 9.9 %copy-start.8 = (f32[1,128]{1,0:T(1,128)S(1)}, f32[1,128]{1,0:T(1,128)}, u32[]{:S(2)}) copy-start(f32[1,128]{1,0:T(1,128)} %refs_4_.1) | copy-start | bytes 1540
  0.7 9.9 %copy-start.7 = (f32[1,128]{1,0:T(1,128)S(1)}, f32[1,128]{1,0:T(1,128)}, u32[]{:S(2)}) copy-start(f32[1,128]{1,0:T(1,128)} %refs_3_.4) | copy-start | bytes 1540
  0.7 9.9 %copy-start.6 = (f32[1,128]{1,0:T(1,128)S(1)}, f32[1,128]{1,0:T(1,128)}, u32[]{:S(2)}) copy-start(f32[1,128]{1,0:T(1,128)} %refs_2_.4) | copy-start | bytes 1540
  0.7 9.9 %copy-start.1 = (bf16[3,3,3,128,128]{4,3,2,1,0:T(8,128)(2,1)S(1)}, bf16[3,3,3,128,128]{4,3,2,1,0:T(8,128)(2,1)}, u32[]{:S(2)}) copy-start(bf16[3,3,3,128,128]{4,3,2,1,0:T(8,128)(2,1)} %refs_1_.4) | copy-start | bytes 2654212
  0.7 9.9 %copy-start = (bf16[3,3,3,128,128]{4,3,2,1,0:T(8,128)(2,1)S(1)}, bf16[3,3,3,128,128]{4,3,2,1,0:T(8,128)(2,1)}, u32[]{:S(2)}) copy-start(bf16[3,3,3,128,128]{4,3,2,1,0:T(8,128)(2,1)} %refs_0_.4) | copy-start | bytes 2654212
  3.2 7.8 %collective-permute-start = (bf16[720,128]{1,0:T(8,128)(2,1)}, bf16[720,128]{1,0:T(8,128)(2,1)S(1)}, u32[]{:S(2)}, u32[]{:S(2)}) collective-permute-start(bf16[720,128]{1,0:T(8,128)(2,1)} %get-tuple-element.20), channel_id=1, source_target_pairs={{0,1},{1,0},{2,3},{3,2},{4,5},{5,4},{6,7},{7,6},{8,9},{9,8},{10,11... | collective-permute-start | bytes 552968 | tf_op jit(solution)/shard_map/ppermute | solution.py:23
  5.4 5.7 %collective-permute-start.1 = (bf16[720,128]{1,0:T(8,128)(2,1)}, bf16[720,128]{1,0:T(8,128)(2,1)S(1)}, u32[]{:S(2)}, u32[]{:S(2)}) collective-permute-start(bf16[720,128]{1,0:T(8,128)(2,1)} %get-tuple-element.21), channel_id=1, source_target_pairs={{1,2},{2,1},{3,4},{4,3},{5,6},{6,5},{7,8},{8,7},{9,10},{10,9},{11,... | collective-permute-start | bytes 552968 | tf_op jit(solution)/shard_map/ppermute | solution.py:23
  6.0 13.2 %collective-permute-start.2 = (bf16[6,4,40,128]{3,2,1,0:T(8,128)(2,1)}, bf16[6,4,40,128]{3,2,1,0:T(8,128)(2,1)S(1)}, u32[]{:S(2)}, u32[]{:S(2)}) collective-permute-start(bf16[6,4,40,128]{3,2,1,0:T(8,128)(2,1)} %get-tuple-element.30), channel_id=1, source_target_pairs={{0,16},{16,0},{32,48},{48,32},{64,80},{80,64},{96,112},{112,96},{1... | collective-permute-start | bytes 737288 | tf_op jit(solution)/shard_map/ppermute | solution.py:23
  7.1 12.2 %collective-permute-start.3 = (bf16[6,4,40,128]{3,2,1,0:T(8,128)(2,1)}, bf16[6,4,40,128]{3,2,1,0:T(8,128)(2,1)S(1)}, u32[]{:S(2)}, u32[]{:S(2)}) collective-permute-start(bf16[6,4,40,128]{3,2,1,0:T(8,128)(2,1)} %get-tuple-element.31), channel_id=1, source_target_pairs={{16,32},{32,16},{48,64},{64,48},{80,96},{96,80},{17,33},{33,17},{4... | collective-permute-start | bytes 737288 | tf_op jit(solution)/shard_map/ppermute | solution.py:23
  10.6 4.4 %copy-start.2 = (bf16[2,30,40,128]{3,2,1,0:T(8,128)(2,1)S(1)}, bf16[2,30,40,128]{3,2,1,0:T(8,128)(2,1)}, u32[]{:S(2)}) copy-start(bf16[2,30,40,128]{3,2,1,0:T(8,128)(2,1)} %refs_0_.5) | copy-start | bytes 1843204
  10.6 4.4 %copy-start.3 = (bf16[2,30,40,128]{3,2,1,0:T(8,128)(2,1)S(1)}, bf16[2,30,40,128]{3,2,1,0:T(8,128)(2,1)}, u32[]{:S(2)}) copy-start(bf16[2,30,40,128]{3,2,1,0:T(8,128)(2,1)} %refs_2_.5) | copy-start | bytes 1843204
  10.6 4.4 %copy-start.4 = (bf16[1,30,40,128]{3,2,1,0:T(8,128)(2,1)S(1)}, bf16[1,30,40,128]{3,2,1,0:T(8,128)(2,1)}, u32[]{:S(2)}) copy-start(bf16[1,30,40,128]{3,2,1,0:T(8,128)(2,1)} %refs_1_.5) | copy-start | bytes 921604
  10.6 4.4 %copy-start.5 = (bf16[1,30,40,128]{3,2,1,0:T(8,128)(2,1)S(1)}, bf16[1,30,40,128]{3,2,1,0:T(8,128)(2,1)}, u32[]{:S(2)}) copy-start(bf16[1,30,40,128]{3,2,1,0:T(8,128)(2,1)} %refs_3_.5) | copy-start | bytes 921604
  11.1 8.1 %collective-permute-start.5 = (bf16[192,128]{1,0:T(8,128)(2,1)S(1)}, bf16[192,128]{1,0:T(8,128)(2,1)S(1)}, u32[]{:S(2)}, u32[]{:S(2)}) collective-permute-start(bf16[192,128]{1,0:T(8,128)(2,1)S(1)} %get-tuple-element.43), channel_id=1, source_target_pairs={{16,32},{32,16},{48,64},{64,48},{80,96},{96,80},{17,33},{33,17},{4... | collective-permute-start | bytes 147464 | tf_op jit(solution)/shard_map/ppermute | solution.py:23
  14.9 4.3 %collective-permute-start.4 = (bf16[192,128]{1,0:T(8,128)(2,1)S(1)}, bf16[192,128]{1,0:T(8,128)(2,1)S(1)}, u32[]{:S(2)}, u32[]{:S(2)}) collective-permute-start(bf16[192,128]{1,0:T(8,128)(2,1)S(1)} %get-tuple-element.44), channel_id=1, source_target_pairs={{0,16},{16,0},{32,48},{48,32},{64,80},{80,64},{96,112},{112,96},{1... | collective-permute-start | bytes 147464 | tf_op jit(solution)/shard_map/ppermute | solution.py:23
  25.7 2.6 %collective-permute-start.6 = (bf16[3584,128]{1,0:T(8,128)(2,1)S(1)}, bf16[3584,128]{1,0:T(8,128)(2,1)S(1)}, u32[]{:S(2)}, u32[]{:S(2)}) collective-permute-start(bf16[3584,128]{1,0:T(8,128)(2,1)S(1)} %get-tuple-element.36), channel_id=1, source_target_pairs={{0,16},{16,0},{32,48},{48,32},{64,80},{80,64},{96,112},{112,96},{1... | collective-permute-start | bytes 2752520 | tf_op jit(solution)/shard_map/ppermute | solution.py:446
  80.2 5.4 %collective-permute-start.7 = (bf16[3584,128]{1,0:T(8,128)(2,1)}, bf16[3584,128]{1,0:T(8,128)(2,1)S(1)}, u32[]{:S(2)}, u32[]{:S(2)}) collective-permute-start(bf16[3584,128]{1,0:T(8,128)(2,1)} %bitcast.1), channel_id=1, source_target_pairs={{0,16},{16,0},{32,48},{48,32},{64,80},{80,64},{96,112},{112,96},{1... | collective-permute-start | bytes 2752520 | tf_op jit(solution)/shard_map/ppermute | solution.py:460
where the time goes:
time: 89 us; the launch traced here: 88.8 us
  blocking collectives  51.3 us (58%)
  Pallas kernels  15.2 us (17%)
  starting transfers between devices  14.8 us (17%)
  other arithmetic  3.62 us (4%)
  waiting for transfers between devices  2.77 us (3%)
  between operations  0.95 us (1%)
    all_to_all x2, blocking collectives, spread_out(): lax.all_to_all(value.reshape(chips, share, chans), BOTH, 0, 0, axis_index...  51.3 us
    pallas_call x5, Pallas kernels, call(): pl.pallas_call(body, out_shape=tuple(out_shape), cost_estimate=pl.CostEst...  15.2 us
    ppermute x6, starting transfers between devices, trade(): return (lax.ppermute(near, axis, first), lax.ppermute(far, axis, second))  11.2 us
    select_n x1, other arithmetic, per_device(): grad_second = jnp.where(even, other, one).reshape(shape)  3.19 us
    ppermute x1, starting transfers between devices, per_device(): other = lax.ppermute(one, 'ha', pairs)  3.06 us
    ppermute x1, waiting for transfers between devices, per_device(): got = lax.ppermute(send, 'ha', pairs)  2.1 us
  transfers between devices with their start and end apart: 8, of which 2 were waited for; matrix products, arithmetic and copies ran while one was open for 0% of the time, Pallas kernels for 7%

commit v1 on v0

--- a/solution.py
+++ b/solution.py
@@ -251,6 +251,7 @@
 ):
     lanes = affine.shape[-1]
     tall = rows + 2 * RIM
+    core = lax.axis_index("ha") % 2
     half = corner_near.shape[0] // 2
 
     def assemble(target, block, corner):
@@ -306,6 +307,14 @@
                         a * lanes : (a + 1) * lanes, c * lanes : (c + 1) * lanes
                     ].astype(BF)
 
+        @pl.when(core == which)
+        def _():
+            pltpu.make_async_copy(grads.at[which], keep, sems.at[0]).start()
+
+        @pl.when(core != which)
+        def _():
+            pltpu.make_async_copy(grads.at[which], send, sems.at[1]).start()
+
     blocks = [(1, 4), (tall - 5, 4)]
     a_value, slope_value = first_layer(rows, cols, whole[:3], ahead_one, affine, blocks)
     a_rim[...] = a_value
@@ -327,15 +336,8 @@
         moved_one[low - 2 : high - 2] = spread(cols, value[low - start : high - start])
     gradient(0, whole[:3], Rows((2, moved_one, rows + 4)))
 
-    core = lax.axis_index("ha") % 2
-    copies = [
-        pltpu.make_async_copy(grads.at[core], keep, sems.at[0]),
-        pltpu.make_async_copy(grads.at[1 - core], send, sems.at[1]),
-    ]
-    for copy in copies:
-        copy.start()
-    for copy in copies:
-        copy.wait()
+    pltpu.make_async_copy(grads.at[core], keep, sems.at[0]).wait()
+    pltpu.make_async_copy(grads.at[1 - core], send, sems.at[1]).wait()
 
 
 class Shifted:
@@ -351,6 +353,28 @@
     for start, count in cut(RIM, RIM + rows, 2):
         value = backward(field, back_one, start, count)
         gin[0, start - RIM : start - RIM + count] = value[:, :cols].astype(BF)
+
+
+def place_kernel(parts, first, source, *refs):
+    one, other, wide, sems = refs[-4:]
+    size = wide.shape[0] // parts
+    own_first = jnp.logical_not(is_odd("ha"))
+    to_one = own_first if first else jnp.logical_not(own_first)
+    for part in range(parts):
+        at = pl.ds(part * size, size)
+        wide[at, :] = source[at, :].astype(F32)
+
+        @pl.when(to_one)
+        def _():
+            pltpu.make_async_copy(wide.at[at], one.at[at], sems.at[part]).start()
+
+        @pl.when(jnp.logical_not(to_one))
+        def _():
+            pltpu.make_async_copy(wide.at[at], other.at[at], sems.at[part]).start()
+
+    for part in range(parts):
+        at = pl.ds(part * size, size)
+        pltpu.make_async_copy(wide.at[at], one.at[at], sems.at[part]).wait()
 
 
 def per_device(
@@ -445,8 +469,9 @@
     pairs, _ = swaps("ha")
     got = lax.ppermute(send, "ha", pairs)
     (grad_input,) = call(
-        input_kernel, "input", (shaped(1, rows, cols, chans),), 28, 1e9, (d_one, back_one)
-    )
+        input_kernel, "input", (shaped(1, rows, cols, chans),), 12, 1e9, (d_one, back_one)
+    )
+    got, grad_input = lax.optimization_barrier((got, grad_input))
     chip_sum = (keep.astype(F32) + got.astype(F32)).astype(BF)
     cores = [[c for c in range(devices) if (c // lax.axis_size("wa")) % 2 == k] for k in range(2)]
 
@@ -458,12 +483,23 @@
     mine = (jnp.sum(spread_out(chip_sum).astype(F32), axis=0) * factor).astype(BF)
     one = spread_out(jnp.broadcast_to(mine[None], (chips, share, chans))).reshape(-1, chans)
     other = lax.ppermute(one, "ha", pairs)
-    even = jnp.logical_not(odd)
     shape = (3, 3, 3, chans, chans)
-    one, other = one[:total].astype(F32), other[:total].astype(F32)
-    grad_first = jnp.where(even, one, other).reshape(shape)
-    grad_second = jnp.where(even, other, one).reshape(shape)
-    return (grad_input, grad_first, grad_second)
+    parts = 4
+
+    def place(source, *given):
+        return call(
+            lambda *refs: place_kernel(parts, not given, *refs), "place",
+            [shaped(total, chans, dtype=F32)] * 2, 8, 2e9, (source, *given), sizes=False,
+            in_specs=[inner] + [anywhere] * len(given),
+            out_specs=(anywhere, anywhere),
+            scratch_shapes=[
+                pltpu.VMEM((total, chans), F32), pltpu.SemaphoreType.DMA((parts,))
+            ],
+            input_output_aliases={1: 0, 2: 1} if given else {},
+        )
+
+    grad_first, grad_second = place(other, *place(one))
+    return (grad_input, grad_first.reshape(shape), grad_second.reshape(shape))
 
 
 def solution(mesh):

time: 89 us -> 86.7 us (0.974)
  other arithmetic: 3.62 us -> 0.43 us
  Pallas kernels: 15.2 us -> 17.8 us
  waiting for transfers between devices: 2.77 us -> 1.29 us
    select_n x1 -> x0, other arithmetic: 3.19 us -> none  [per_device(): grad_second = jnp.where(even, other, one).reshape(shape)]
    pallas_call x5 -> x7, Pallas kernels: 15.2 us -> 17.8 us  [call(): pl.pallas_call(body, out_shape=tuple(out_shape), cost_estimate=pl.CostEst...]
    ppermute x1, waiting for transfers between devices: 2.1 us -> 0.45 us  [per_device(): got = lax.ppermute(send, 'ha', pairs)]
  transfers between devices with their start and end apart: 8 -> 8, of which waited for: 2 -> 2; matrix products, arithmetic and copies ran while one was open for 0% -> 0% of each run, Pallas kernels for 7% -> 9%
where the time goes in v1:
time: 86.7 us; the launch traced here: 86.5 us
  blocking collectives  50.8 us (59%)
  Pallas kernels  17.8 us (21%)
  starting transfers between devices  14.9 us (17%)
  waiting for transfers between devices  1.29 us (1%)
  between operations  0.96 us (1%)
    all_to_all x2, blocking collectives, spread_out(): lax.all_to_all(value.reshape(chips, share, chans), BOTH, 0, 0, axis_index...  50.8 us
    pallas_call x7, Pallas kernels, call(): pl.pallas_call(body, out_shape=tuple(out_shape), cost_estimate=pl.CostEst...  17.8 us
    ppermute x6, starting transfers between devices, trade(): return (lax.ppermute(near, axis, first), lax.ppermute(far, axis, second))  11.2 us
    ppermute x1, starting transfers between devices, per_device(): other = lax.ppermute(one, 'ha', pairs)  3.19 us
  transfers between devices with their start and end apart: 8, of which 2 were waited for; matrix products, arithmetic and copies ran while one was open for 0% of the time, Pallas kernels for 9%

profile of v1, /device:TPU:1, one launch (start us, length us, event | category | flops | bytes accessed | tf_op | source)
XLA Modules:
  0.0 86.5 jit_solution(12791243887460669429)
XLA Ops:
  0.6 0.0 copy-start.9
  0.6 0.0 copy-start.8
  0.7 0.0 copy-start.7
  0.7 0.0 copy-start.6
  0.7 0.0 copy-start.1
  0.7 0.0 copy-start
  0.7 2.5 %pack.1 = (bf16[6,4,40,128]{3,2,1,0:T(8,128)(2,1)}, bf16[6,4,40,128]{3,2,1,0:T(8,128)(2,1)}, bf16[720,128]{1,0:T(8,128)(2,1)}, bf16[720,128]{1,0:T(8,128)(2,1)}) custom-call(bf16[2,30,40,128]{3,2,1,0:T(8,128)(2,1)} %refs_0_.5, bf16[1,30,40,128]{3,2,1,0:T(8,128)(2,1)} %refs_1_.5, bf16[2,30,40,128]{3,2,1,0:T(8,128)(2,1)} %refs_2_.5, ...), custom_call_target="tpu_custom_call" | custom-call | flops 1000000000 | bytes 8000000 | tf_op jit(solution)/shard_map/pack/pallas_call | solution.py:405
  3.2 2.1 %collective-permute-start = (bf16[720,128]{1,0:T(8,128)(2,1)}, bf16[720,128]{1,0:T(8,128)(2,1)S(1)}, u32[]{:S(2)}, u32[]{:S(2)}) collective-permute-start(bf16[720,128]{1,0:T(8,128)(2,1)} %get-tuple-element.26), channel_id=1, source_target_pairs={{0,1},{1,0},{2,3},{3,2},{4,5},{5,4},{6,7},{7,6},{8,9},{9,8},{10,11... | collective-permute-start | bytes 552968 | tf_op jit(solution)/shard_map/ppermute | solution.py:23
  5.4 0.7 collective-permute-start.1
  6.0 1.0 %collective-permute-start.2 = (bf16[6,4,40,128]{3,2,1,0:T(8,128)(2,1)}, bf16[6,4,40,128]{3,2,1,0:T(8,128)(2,1)S(1)}, u32[]{:S(2)}, u32[]{:S(2)}) collective-permute-start(bf16[6,4,40,128]{3,2,1,0:T(8,128)(2,1)} %get-tuple-element.36), channel_id=1, source_target_pairs={{0,16},{16,0},{32,48},{48,32},{64,80},{80,64},{96,112},{112,96},{1... | collective-permute-start | bytes 737288 | tf_op jit(solution)/shard_map/ppermute | solution.py:23
  7.1 3.4 %collective-permute-start.3 = (bf16[6,4,40,128]{3,2,1,0:T(8,128)(2,1)}, bf16[6,4,40,128]{3,2,1,0:T(8,128)(2,1)S(1)}, u32[]{:S(2)}, u32[]{:S(2)}) collective-permute-start(bf16[6,4,40,128]{3,2,1,0:T(8,128)(2,1)} %get-tuple-element.37), channel_id=1, source_target_pairs={{16,32},{32,16},{48,64},{64,48},{80,96},{96,80},{17,33},{33,17},{4... | collective-permute-start | bytes 737288 | tf_op jit(solution)/shard_map/ppermute | solution.py:23
  10.5 0.0 copy-done.9
  10.5 0.0 copy-done.8
  10.5 0.0 copy-done.7
  10.6 0.0 copy-done.6
  10.6 0.0 copy-done.1
  10.6 0.0 copy-done
  10.6 0.0 copy-start.2
  10.6 0.0 copy-start.3
  10.6 0.0 copy-start.4
  10.6 0.0 copy-start.5
  10.6 0.4 ready.1
  11.0 0.0 collective-permute-done.refs_4_
  11.0 0.0 collective-permute-done.1.refs_5_
  11.1 3.8 %collective-permute-start.5 = (bf16[192,128]{1,0:T(8,128)(2,1)S(1)}, bf16[192,128]{1,0:T(8,128)(2,1)S(1)}, u32[]{:S(2)}, u32[]{:S(2)}) collective-permute-start(bf16[192,128]{1,0:T(8,128)(2,1)S(1)} %get-tuple-element.53), channel_id=1, source_target_pairs={{16,32},{32,16},{48,64},{64,48},{80,96},{96,80},{17,33},{33,17},{4... | collective-permute-start | bytes 147464 | tf_op jit(solution)/shard_map/ppermute | solution.py:23
  14.9 0.1 collective-permute-start.4
  15.0 0.0 copy-done.2
  15.0 0.0 copy-done.3
  15.0 0.0 copy-done.4
  15.0 0.0 copy-done.5
  15.0 4.2 %middle.1 = (bf16[6,30,48,128]{3,2,1,0:T(8,128)(2,1)S(1)}, f32[28,48,128]{2,1,0:T(8,128)S(1)}, bf16[28,48,128]{2,1,0:T(8,128)(2,1)S(1)}, bf16[26,48,128]{2,1,0:T(8,128)(2,1)S(1)}, bf16[26,48,384]{2,1,0:T(8,128)(2,1)S(1)}) custom-call(bf16[2,30,40,128]{3,2,1,0:T(8,128)(2,1)S(1)} %copy-done.2, bf16[1,30,40,128]{3,2,1,0:T(8,128)(2,1)S(1)} %copy-done.4, ...), custom_call_target="tpu_custom_call" | custom-call | flops 5000000000 | bytes 8000000 | tf_op jit(solution)/shard_map/middle/pallas_call | solution.py:405
  19.2 0.0 collective-permute-done.5.refs_8_
  19.2 0.0 collective-permute-done.4.refs_7_
  19.2 0.0 collective-permute-done.2.refs_5_
  19.2 0.0 collective-permute-done.3.refs_6_
  19.2 6.6 %rim.1 = (bf16[3584,128]{1,0:T(8,128)(2,1)S(1)}, bf16[3584,128]{1,0:T(8,128)(2,1)S(1)}, bf16[32,48,128]{2,1,0:T(8,128)(2,1)S(1)}) custom-call(bf16[6,30,48,128]{3,2,1,0:T(8,128)(2,1)S(1)} %get-tuple-element.31.refs_0_, f32[28,48,128]{2,1,0:T(8,128)S(1)} %get-tuple-element.32.refs_1_, bf16[28,48,128]{2,1,0:T(8,128)(2,1)S(1)} %get-tuple-element.33.refs_2_, ...), custom_call_target="tpu_custom_call" | custom-call | flops 5000000000 | bytes 8000000 | tf_op jit(solution)/shard_map/rim/pallas_call | solution.py:405
  25.9 0.6 collective-permute-start.6
  26.4 1.7 %input.1 = bf16[1,30,40,128]{3,2,1,0:T(8,128)(2,1)} custom-call(bf16[32,48,128]{2,1,0:T(8,128)(2,1)S(1)} %get-tuple-element.40.refs_0_, bf16[384,384]{1,0:T(8,128)(2,1)S(1)} %get-tuple-element.41.refs_1_), custom_call_target="tpu_custom_call" | custom-call | flops 1000000000 | bytes 8000000 | tf_op jit(solution)/shard_map/input/pallas_call | solution.py:405
  28.1 0.4 collective-permute-done.6
  28.5 0.2 add_convert_fusion
  28.8 31.4 %all_to_all.10 = bf16[64,56,128]{2,1,0:T(8,128)(2,1)S(1)} all-to-all(bf16[64,56,128]{2,1,0:T(8,128)(2,1)S(1)} %bitcast.6), channel_id=1, replica_groups={{0,1,2,3,4,5,6,7,8,9,10,11,12,13,14,15,32,33,34,35,36,37,38,39,40,41,42..., dimensions={0} | all-to-all | bytes 1835008 | tf_op jit(solution)/shard_map/all_to_all | solution.py:479
  60.1 0.2 convert_reduce_fusion
  60.3 0.1 broadcast_in_dim.2
  60.4 19.5 %all_to_all.11 = bf16[64,56,128]{2,1,0:T(8,128)(2,1)S(1)} all-to-all(bf16[64,56,128]{2,1,0:T(8,128)(2,1)S(1)} %broadcast_in_dim.2), channel_id=1, replica_groups={{0,1,2,3,4,5,6,7,8,9,10,11,12,13,14,15,32,33,34,35,36,37,38,39,40,41,42..., dimensions={0} | all-to-all | bytes 1835008 | tf_op jit(solution)/shard_map/all_to_all | solution.py:479
  79.9 3.2 %collective-permute-start.7 = (bf16[3584,128]{1,0:T(8,128)(2,1)S(1)}, bf16[3584,128]{1,0:T(8,128)(2,1)S(1)}, u32[]{:S(2)}, u32[]{:S(2)}) collective-permute-start(bf16[3584,128]{1,0:T(8,128)(2,1)S(1)} %bitcast.4), channel_id=1, source_target_pairs={{0,16},{16,0},{32,48},{48,32},{64,80},{80,64},{96,112},{112,96},{1... | collective-permute-start | bytes 2752520 | tf_op jit(solution)/shard_map/ppermute | solution.py:485
  83.1 1.3 %place.2 = (f32[3456,128]{1,0:T(8,128)}, f32[3456,128]{1,0:T(8,128)}) custom-call(bf16[3584,128]{1,0:T(8,128)(2,1)S(1)} %bitcast.5), custom_call_target="tpu_custom_call" | custom-call | flops 2000000000 | bytes 8000000 | tf_op jit(solution)/shard_map/place/pallas_call | solution.py:405
  84.4 0.8 collective-permute-done.7.refs_0_
  85.2 1.3 %place.3 = (f32[3456,128]{1,0:T(8,128)}, f32[3456,128]{1,0:T(8,128)}) custom-call(bf16[3584,128]{1,0:T(8,128)(2,1)S(1)} %collective-permute-done.7.refs_0_, f32[3456,128]{1,0:T(8,128)} %get-tuple-element.45.refs_1_, f32[3456,128]{1,0:T(8,128)} %get-tuple-element.46.refs_2_), custom_call_target="tpu_custom_call", output_to_operand_aliasing={{0}: (1, {}), {1}: (2, {})} | custom-call | flops 2000000000 | bytes 8000000 | tf_op jit(solution)/shard_map/place/pallas_call | solution.py:405
  (4 shorter events, 0.0 us)
Async XLA Ops:
  0.6 9.9 %copy-start.9 = (f32[1,128]{1,0:T(1,128)S(1)}, f32[1,128]{1,0:T(1,128)}, u32[]{:S(2)}) copy-start(f32[1,128]{1,0:T(1,128)} %refs_5_.1) | copy-start | bytes 1540
  0.6 9.9 %copy-start.8 = (f32[1,128]{1,0:T(1,128)S(1)}, f32[1,128]{1,0:T(1,128)}, u32[]{:S(2)}) copy-start(f32[1,128]{1,0:T(1,128)} %refs_4_.1) | copy-start | bytes 1540
  0.7 9.9 %copy-start.7 = (f32[1,128]{1,0:T(1,128)S(1)}, f32[1,128]{1,0:T(1,128)}, u32[]{:S(2)}) copy-start(f32[1,128]{1,0:T(1,128)} %refs_3_.4) | copy-start | bytes 1540
  0.7 9.9 %copy-start.6 = (f32[1,128]{1,0:T(1,128)S(1)}, f32[1,128]{1,0:T(1,128)}, u32[]{:S(2)}) copy-start(f32[1,128]{1,0:T(1,128)} %refs_2_.4) | copy-start | bytes 1540
  0.7 9.9 %copy-start.1 = (bf16[3,3,3,128,128]{4,3,2,1,0:T(8,128)(2,1)S(1)}, bf16[3,3,3,128,128]{4,3,2,1,0:T(8,128)(2,1)}, u32[]{:S(2)}) copy-start(bf16[3,3,3,128,128]{4,3,2,1,0:T(8,128)(2,1)} %refs_1_.4) | copy-start | bytes 2654212
  0.7 9.9 %copy-start = (bf16[3,3,3,128,128]{4,3,2,1,0:T(8,128)(2,1)S(1)}, bf16[3,3,3,128,128]{4,3,2,1,0:T(8,128)(2,1)}, u32[]{:S(2)}) copy-start(bf16[3,3,3,128,128]{4,3,2,1,0:T(8,128)(2,1)} %refs_0_.4) | copy-start | bytes 2654212
  3.2 7.8 %collective-permute-start = (bf16[720,128]{1,0:T(8,128)(2,1)}, bf16[720,128]{1,0:T(8,128)(2,1)S(1)}, u32[]{:S(2)}, u32[]{:S(2)}) collective-permute-start(bf16[720,128]{1,0:T(8,128)(2,1)} %get-tuple-element.26), channel_id=1, source_target_pairs={{0,1},{1,0},{2,3},{3,2},{4,5},{5,4},{6,7},{7,6},{8,9},{9,8},{10,11... | collective-permute-start | bytes 552968 | tf_op jit(solution)/shard_map/ppermute | solution.py:23
  5.4 5.7 %collective-permute-start.1 = (bf16[720,128]{1,0:T(8,128)(2,1)}, bf16[720,128]{1,0:T(8,128)(2,1)S(1)}, u32[]{:S(2)}, u32[]{:S(2)}) collective-permute-start(bf16[720,128]{1,0:T(8,128)(2,1)} %get-tuple-element.27), channel_id=1, source_target_pairs={{1,2},{2,1},{3,4},{4,3},{5,6},{6,5},{7,8},{8,7},{9,10},{10,9},{11,... | collective-permute-start | bytes 552968 | tf_op jit(solution)/shard_map/ppermute | solution.py:23
  6.0 13.2 %collective-permute-start.2 = (bf16[6,4,40,128]{3,2,1,0:T(8,128)(2,1)}, bf16[6,4,40,128]{3,2,1,0:T(8,128)(2,1)S(1)}, u32[]{:S(2)}, u32[]{:S(2)}) collective-permute-start(bf16[6,4,40,128]{3,2,1,0:T(8,128)(2,1)} %get-tuple-element.36), channel_id=1, source_target_pairs={{0,16},{16,0},{32,48},{48,32},{64,80},{80,64},{96,112},{112,96},{1... | collective-permute-start | bytes 737288 | tf_op jit(solution)/shard_map/ppermute | solution.py:23
  7.1 12.2 %collective-permute-start.3 = (bf16[6,4,40,128]{3,2,1,0:T(8,128)(2,1)}, bf16[6,4,40,128]{3,2,1,0:T(8,128)(2,1)S(1)}, u32[]{:S(2)}, u32[]{:S(2)}) collective-permute-start(bf16[6,4,40,128]{3,2,1,0:T(8,128)(2,1)} %get-tuple-element.37), channel_id=1, source_target_pairs={{16,32},{32,16},{48,64},{64,48},{80,96},{96,80},{17,33},{33,17},{4... | collective-permute-start | bytes 737288 | tf_op jit(solution)/shard_map/ppermute | solution.py:23
  10.6 4.4 %copy-start.2 = (bf16[2,30,40,128]{3,2,1,0:T(8,128)(2,1)S(1)}, bf16[2,30,40,128]{3,2,1,0:T(8,128)(2,1)}, u32[]{:S(2)}) copy-start(bf16[2,30,40,128]{3,2,1,0:T(8,128)(2,1)} %refs_0_.5) | copy-start | bytes 1843204
  10.6 4.4 %copy-start.3 = (bf16[2,30,40,128]{3,2,1,0:T(8,128)(2,1)S(1)}, bf16[2,30,40,128]{3,2,1,0:T(8,128)(2,1)}, u32[]{:S(2)}) copy-start(bf16[2,30,40,128]{3,2,1,0:T(8,128)(2,1)} %refs_2_.5) | copy-start | bytes 1843204
  10.6 4.4 %copy-start.4 = (bf16[1,30,40,128]{3,2,1,0:T(8,128)(2,1)S(1)}, bf16[1,30,40,128]{3,2,1,0:T(8,128)(2,1)}, u32[]{:S(2)}) copy-start(bf16[1,30,40,128]{3,2,1,0:T(8,128)(2,1)} %refs_1_.5) | copy-start | bytes 921604
  10.6 4.4 %copy-start.5 = (bf16[1,30,40,128]{3,2,1,0:T(8,128)(2,1)S(1)}, bf16[1,30,40,128]{3,2,1,0:T(8,128)(2,1)}, u32[]{:S(2)}) copy-start(bf16[1,30,40,128]{3,2,1,0:T(8,128)(2,1)} %refs_3_.5) | copy-start | bytes 921604
  11.1 8.1 %collective-permute-start.5 = (bf16[192,128]{1,0:T(8,128)(2,1)S(1)}, bf16[192,128]{1,0:T(8,128)(2,1)S(1)}, u32[]{:S(2)}, u32[]{:S(2)}) collective-permute-start(bf16[192,128]{1,0:T(8,128)(2,1)S(1)} %get-tuple-element.53), channel_id=1, source_target_pairs={{16,32},{32,16},{48,64},{64,48},{80,96},{96,80},{17,33},{33,17},{4... | collective-permute-start | bytes 147464 | tf_op jit(solution)/shard_map/ppermute | solution.py:23
  14.9 4.3 %collective-permute-start.4 = (bf16[192,128]{1,0:T(8,128)(2,1)S(1)}, bf16[192,128]{1,0:T(8,128)(2,1)S(1)}, u32[]{:S(2)}, u32[]{:S(2)}) collective-permute-start(bf16[192,128]{1,0:T(8,128)(2,1)S(1)} %get-tuple-element.54), channel_id=1, source_target_pairs={{0,16},{16,0},{32,48},{48,32},{64,80},{80,64},{96,112},{112,96},{1... | collective-permute-start | bytes 147464 | tf_op jit(solution)/shard_map/ppermute | solution.py:23
  25.9 2.7 %collective-permute-start.6 = (bf16[3584,128]{1,0:T(8,128)(2,1)S(1)}, bf16[3584,128]{1,0:T(8,128)(2,1)S(1)}, u32[]{:S(2)}, u32[]{:S(2)}) collective-permute-start(bf16[3584,128]{1,0:T(8,128)(2,1)S(1)} %get-tuple-element.39), channel_id=1, source_target_pairs={{0,16},{16,0},{32,48},{48,32},{64,80},{80,64},{96,112},{112,96},{1... | collective-permute-start | bytes 2752520 | tf_op jit(solution)/shard_map/ppermute | solution.py:470
  79.9 5.3 %collective-permute-start.7 = (bf16[3584,128]{1,0:T(8,128)(2,1)S(1)}, bf16[3584,128]{1,0:T(8,128)(2,1)S(1)}, u32[]{:S(2)}, u32[]{:S(2)}) collective-permute-start(bf16[3584,128]{1,0:T(8,128)(2,1)S(1)} %bitcast.4), channel_id=1, source_target_pairs={{0,16},{16,0},{32,48},{48,32},{64,80},{80,64},{96,112},{112,96},{1... | collective-permute-start | bytes 2752520 | tf_op jit(solution)/shard_map/ppermute | solution.py:485

commit v2 on v1

--- a/solution.py
+++ b/solution.py
@@ -47,7 +47,7 @@
     left = jnp.where(odd, near, far).reshape(high, 3, 2 * RIM, lanes)
     right = jnp.where(odd, far, near).reshape(high, 3, 2 * RIM, lanes)
     lower = lax.broadcasted_iota(jnp.int32, (high, 2 * RIM, lanes), 1) < RIM
-    frames = []
+    frames, rims = [], []
     for frame in range(6):
         one, other = right[:, frame // 2], left[:, frame // 2]
         if frame % 2 == 0:
@@ -55,7 +55,8 @@
         else:
             rim = jnp.where(lower, pltpu.roll(one, RIM, 1), other)
         frames.append(jnp.concatenate([block[frame].astype(F32), rim], axis=1).astype(BF))
-    return frames
+        rims.append(rim)
+    return frames, rims
 
 
 class Rows:
@@ -85,13 +86,44 @@
             jnp.concatenate(
                 [flat(frames[a].get(start - 1 + b, count)) for start, count in blocks], axis=0
             )
-            for a in range(3)
+            for a in range(len(frames))
             for b in range(3)
         ],
         axis=1,
     )
-    out = jnp.dot(lhs, weight[...], preferred_element_type=F32)
+    out = jnp.dot(lhs, weight, preferred_element_type=F32)
     return gather_columns(out, 1)
+
+
+def rim_forward(rims, weight, start, count, cols):
+    lhs = jnp.concatenate(
+        [
+            flat(rim[start - 1 + b - RIM : start - 1 + b - RIM + count])
+            for rim in rims
+            for b in range(3)
+        ],
+        axis=1,
+    ).astype(BF)
+    out = jnp.dot(lhs, weight, preferred_element_type=F32)
+    lanes = out.shape[-1] // 3
+    out = out.reshape(count, 2 * RIM, 3 * lanes)
+    place = lax.broadcasted_iota(jnp.int32, (count, 2 * RIM, lanes), 1)
+    last = 2 * RIM - 1
+    from_left, from_right = turn(out[..., :lanes], 1), turn(out[..., 2 * lanes :], -1)
+    here = (
+        out[..., lanes : 2 * lanes]
+        + jnp.where(place > 0, from_left, 0.0)
+        + jnp.where(place < last, from_right, 0.0)
+    )
+    return jnp.concatenate(
+        [
+            jnp.where(place == 0, from_left, 0.0),
+            jnp.zeros((count, cols - 4 * RIM, lanes), F32),
+            jnp.where(place == last, from_right, 0.0),
+            here,
+        ],
+        axis=1,
+    )
 
 
 def backward(field, weight, start, count):
@@ -127,10 +159,10 @@
     return jnp.concatenate(out, axis=0) if len(out) > 1 else out[0]
 
 
-def first_layer(rows, cols, frames, weight, affine, blocks):
+def first_layer(rows, cols, conv, affine, blocks):
     lanes = affine.shape[-1]
     gain, bias = (affine[i : i + 1, :].reshape(1, 1, lanes) for i in (0, 1))
-    m_one = forward(frames, weight, blocks) * gain + bias
+    m_one = conv * gain + bias
     sig = jax.nn.sigmoid(m_one)
     inside = in_image(rows, cols, lanes, blocks)
     a_one = jnp.where(inside, m_one * sig, 0.0).astype(BF)
@@ -138,10 +170,10 @@
     return a_one, slope_one
 
 
-def second_layer(frames, cot, weight, affine, blocks):
+def second_layer(conv, cot, affine, blocks):
     lanes = affine.shape[-1]
     gain, bias = (affine[i : i + 1, :].reshape(1, 1, lanes) for i in (2, 3))
-    m_two = forward(frames, weight, blocks) * gain + bias
+    m_two = conv * gain + bias
     pulled = [cot.get(start, count) for start, count in blocks]
     pulled = jnp.concatenate(pulled, axis=0) if len(pulled) > 1 else pulled[0]
     return pulled.astype(F32) * slope(m_two) * gain
@@ -173,19 +205,29 @@
             )
         )
     ]
+    odd_row, odd_col = is_odd("ha"), is_odd("wa")
+    last = rows - RIM
+    near_at, far_at = jnp.where(odd_row, 0, last), jnp.where(odd_row, last, 0)
     for copy in copies:
         copy.start()
+    straight, frame = [], 0
+    for source in (cache_in_at, frames_in_at, cache_mid_at, cot_at):
+        size = source.shape[0]
+        for start, target in ((near_at, row_near), (far_at, row_far)):
+            straight.append(
+                pltpu.make_async_copy(
+                    source.at[:, pl.ds(start, RIM)],
+                    target.at[frame : frame + size],
+                    sems.at[4 + len(straight)],
+                )
+            )
+            straight[-1].start()
+        frame += size
     for copy in copies:
         copy.wait()
-    odd_row, odd_col = is_odd("ha"), is_odd("wa")
     sources = (
         (cache_in, 0), (cache_in, 1), (frames_in, 0), (cache_mid, 0), (cache_mid, 1), (cot, 0)
     )
-    last = rows - RIM
-    near_at, far_at = jnp.where(odd_row, 0, last), jnp.where(odd_row, last, 0)
-    for frame, (ref, i) in enumerate(sources):
-        row_near[frame] = ref[i, pl.ds(near_at, RIM)]
-        row_far[frame] = ref[i, pl.ds(far_at, RIM)]
     lanes = col_near.shape[-1]
     lower = lax.broadcasted_iota(jnp.int32, (rows, 2 * RIM, lanes), 1) < RIM
 
@@ -203,6 +245,8 @@
         far.append(jnp.where(odd_col, tails, heads))
     col_near[...] = jnp.stack(near, axis=1).reshape(-1, lanes).astype(BF)
     col_far[...] = jnp.stack(far, axis=1).reshape(-1, lanes).astype(BF)
+    for copy in straight:
+        copy.wait()
 
 
 def ready_kernel(
@@ -223,25 +267,49 @@
     )
 
 
+def own_kernel(
+    rows, cols, cache_in, frames_in, cache_mid, ahead_one, ahead_two, part_one, part_two, field
+):
+    block = [cache_in[0], cache_in[1], frames_in[0], cache_mid[0], cache_mid[1]]
+    none = jnp.zeros((rows, 2 * RIM, block[0].shape[-1]), F32)
+    for i, value in enumerate(block):
+        field[i] = jnp.concatenate([value.astype(F32), none], axis=1).astype(BF)
+    own = [Rows((RIM, Frame(field, i), rows)) for i in range(5)]
+    split = 6 * none.shape[-1]
+    for frames, weight, part, first in (
+        (own[:3], ahead_one[...], part_one, RIM + 1),
+        (own[3:], ahead_two[:split], part_two, RIM + 2),
+    ):
+        for start, count in cut(first, 2 * RIM + rows - first, 2):
+            part[start - first : start - first + count] = forward(frames, weight, [(start, count)])
+
+
 def middle_kernel(
-    rows, cols, cache_in, frames_in, cache_mid, cot, col_near, col_far, ahead_one, ahead_two, affine,
-    field, slope_mid, a_mid, d_mid, moved_mid,
+    rows, cols, cache_in, frames_in, cache_mid, cot, col_near, col_far, part_one, part_two,
+    ahead_one, ahead_two, affine, field, slope_mid, a_mid, d_mid, moved_mid,
 ):
     block = [cache_in[0], cache_in[1], frames_in[0], cache_mid[0], cache_mid[1], cot[0]]
-    for frame, value in enumerate(join(block, col_near[...], col_far[...])):
+    frames, rims = join(block, col_near[...], col_far[...])
+    for frame, value in enumerate(frames):
         field[frame] = value
-    own = [Rows((RIM, Frame(field, i), rows)) for i in range(6)]
+    split = 6 * affine.shape[-1]
     first = RIM + 1
     for start, count in cut(first, RIM + rows - 1, 2):
-        a_one, slope_one = first_layer(rows, cols, own[:3], ahead_one, affine, [(start, count)])
-        a_mid[start - first : start - first + count] = a_one
-        slope_mid[start - first : start - first + count] = slope_one
-    frames = own[3:5] + [Rows((first, a_mid, rows - 2))]
+        at = slice(start - first, start - first + count)
+        conv = part_one[at] + rim_forward(rims[:3], ahead_one[...], start, count, cols)
+        a_mid[at], slope_mid[at] = first_layer(rows, cols, conv, affine, [(start, count)])
+    a_one, cotangent = Rows((first, a_mid, rows - 2)), Rows((RIM, Frame(field, 5), rows))
     second = RIM + 2
     for start, count in cut(second, RIM + rows - 2, 2):
-        value = second_layer(frames, own[5], ahead_two, affine, [(start, count)])
-        d_mid[start - second : start - second + count] = value.astype(BF)
-        moved_mid[start - second : start - second + count] = spread(cols, value)
+        at = slice(start - second, start - second + count)
+        conv = (
+            part_two[at]
+            + forward([a_one], ahead_two[split:], [(start, count)])
+            + rim_forward(rims[3:5], ahead_two[:split], start, count, cols)
+        )
+        value = second_layer(conv, cotangent, affine, [(start, count)])
+        d_mid[at] = value.astype(BF)
+        moved_mid[at] = spread(cols, value)
 
 
 def rim_kernel(
@@ -255,7 +323,7 @@
     half = corner_near.shape[0] // 2
 
     def assemble(target, block, corner):
-        parts = join([block[i] for i in range(6)], corner[:half], corner[half:])
+        parts, _ = join([block[i] for i in range(6)], corner[:half], corner[half:])
         for frame, value in enumerate(parts):
             target[frame] = value
 
@@ -316,14 +384,16 @@
             pltpu.make_async_copy(grads.at[which], send, sems.at[1]).start()
 
     blocks = [(1, 4), (tall - 5, 4)]
-    a_value, slope_value = first_layer(rows, cols, whole[:3], ahead_one, affine, blocks)
+    conv = forward(whole[:3], ahead_one[...], blocks)
+    a_value, slope_value = first_layer(rows, cols, conv, affine, blocks)
     a_rim[...] = a_value
     slope_rim[...] = slope_value
     a_all = around(a_rim, a_mid, 1, 4)
     slope_all = around(slope_rim, slope_mid, 1, 4)
 
     frames = whole[3:5] + [a_all]
-    value = second_layer(frames, whole[5], ahead_two, affine, [(2, 4), (tall - 6, 4)])
+    blocks = [(2, 4), (tall - 6, 4)]
+    value = second_layer(forward(frames, ahead_two[...], blocks), whole[5], affine, blocks)
     d_rim[...] = value.astype(BF)
     moved_rim[2:6] = spread(cols, value[2:6])
     d_all = around(d_rim, d_mid, 2, 4)
@@ -418,12 +488,22 @@
     row_near, row_far, col_near, col_far = call(
         pack_kernel, "pack", (rim_rows, rim_rows, rim_cols, rim_cols), 60, 1e9, fields,
         in_specs=[anywhere] * 4,
-        scratch_shapes=[pltpu.VMEM(v.shape, BF) for v in fields] + [pltpu.SemaphoreType.DMA((4,))],
+        out_specs=(anywhere, anywhere, inner, inner),
+        scratch_shapes=[pltpu.VMEM(v.shape, BF) for v in fields] + [pltpu.SemaphoreType.DMA((12,))],
     )
     ahead, back = shaped(9 * chans, 3 * chans), shaped(3 * chans, 3 * chans)
     ahead_one, ahead_two, back_one, back_two, affine = call(
         ready_kernel, "ready", (ahead, ahead, back, back, shaped(8, chans, dtype=F32)), 16, 2e9,
         (w_first, w_second, scale_first, shift_first, scale_second, shift_second), sizes=False,
+    )
+    part_one, part_two = call(
+        own_kernel, "own",
+        (
+            shaped(rows - 2, full, chans, dtype=F32),
+            shaped(rows - 4, full, chans, dtype=F32),
+        ),
+        24, 4e9, (cache_in, frames_in, cache_mid, ahead_one, ahead_two),
+        scratch_shapes=[pltpu.VMEM((5, rows, full, chans), BF)],
     )
     col_near, col_far = trade("wa", col_near, col_far)
     row_near, row_far = trade("ha", row_near, row_far)
@@ -442,7 +522,7 @@
             shaped(rows - 4, full, chans),
             shaped(rows - 4, full, 3 * chans),
         ),
-        28, 5e9, (*fields, col_near, col_far, ahead_one, ahead_two, affine),
+        28, 3e9, (*fields, col_near, col_far, part_one, part_two, ahead_one, ahead_two, affine),
     )
     keep, send, d_one = call(
         rim_kernel, "rim",

time: 86.7 us -> 106 us (1.22)
  Pallas kernels: 17.8 us -> 34.1 us
  local copies, waits for them, and re-layouts: 0.18 us -> 5.89 us
  starting transfers between devices: 14.9 us -> 13.4 us
  blocking collectives: 50.8 us -> 49.5 us
    pallas_call x7 -> x8, Pallas kernels: 17.8 us -> 34.1 us  [call(): pl.pallas_call(body, out_shape=tuple(out_shape), cost_estimate=pl.CostEst...]
    unnamed x20 -> x46, local copies, waits for them, and re-layouts: 0.05 us -> 5.76 us
    ppermute x6, starting transfers between devices: 11.2 us -> 9.6 us  [trade(): return (lax.ppermute(near, axis, first), lax.ppermute(far, axis, second))]
    all_to_all x2, blocking collectives: 50.8 us -> 49.5 us  [spread_out(): lax.all_to_all(value.reshape(chips, share, chans), BOTH, 0, 0, axis_index...]
  transfers between devices with their start and end apart: 8 -> 8, of which waited for: 2 -> 2; matrix products, arithmetic and copies ran while one was open for 0% -> 0% of each run, Pallas kernels for 9% -> 8%
where the time goes in v2:
time: 106 us
  blocking collectives  49.5 us (47%)
  Pallas kernels  34.1 us (32%)
  starting transfers between devices  13.4 us (13%)
  local copies, waits for them, and re-layouts  5.89 us (6%)
  waiting for transfers between devices  1.28 us (1%)
  between operations  1.16 us (1%)
    all_to_all x2, blocking collectives, spread_out(): lax.all_to_all(value.reshape(chips, share, chans), BOTH, 0, 0, axis_index...  49.5 us
    pallas_call x8, Pallas kernels, call(): pl.pallas_call(body, out_shape=tuple(out_shape), cost_estimate=pl.CostEst...  34.1 us
    ppermute x6, starting transfers between devices, trade(): return (lax.ppermute(near, axis, first), lax.ppermute(far, axis, second))  9.6 us
    unnamed x46, local copies, waits for them, and re-layouts  5.76 us
    ppermute x1, starting transfers between devices, per_device(): other = lax.ppermute(one, 'ha', pairs)  3.06 us
  transfers between devices with their start and end apart: 8, of which 2 were waited for; matrix products, arithmetic and copies ran while one was open for 0% of the time, Pallas kernels for 8%

profile of v2, /device:TPU:1, one launch (start us, length us, event | category | flops | bytes accessed | tf_op | source)
XLA Modules:
  0.0 105.8 jit_solution(9717761775281850161)
XLA Ops:
  0.6 0.0 copy-start.10
  0.6 0.0 copy-start.9
  0.7 0.0 copy-start.8
  0.7 0.0 copy-start.7
  0.7 0.0 copy-start.1
  0.7 0.0 copy-start
  0.7 16.9 %pack.1 = (bf16[6,4,40,128]{3,2,1,0:T(8,128)(2,1)}, bf16[6,4,40,128]{3,2,1,0:T(8,128)(2,1)}, bf16[720,128]{1,0:T(8,128)(2,1)}, bf16[720,128]{1,0:T(8,128)(2,1)}) custom-call(bf16[2,30,40,128]{3,2,1,0:T(8,128)(2,1)} %refs_0_.7, bf16[1,30,40,128]{3,2,1,0:T(8,128)(2,1)} %refs_1_.7, bf16[2,30,40,128]{3,2,1,0:T(8,128)(2,1)} %refs_2_.7, ...), custom_call_target="tpu_custom_call" | custom-call | flops 1000000000 | bytes 8000000 | tf_op jit(solution)/shard_map/pack/pallas_call | solution.py:475
  17.6 2.1 %collective-permute-start = (bf16[720,128]{1,0:T(8,128)(2,1)}, bf16[720,128]{1,0:T(8,128)(2,1)S(1)}, u32[]{:S(2)}, u32[]{:S(2)}) collective-permute-start(bf16[720,128]{1,0:T(8,128)(2,1)} %get-tuple-element.28), channel_id=1, source_target_pairs={{0,1},{1,0},{2,3},{3,2},{4,5},{5,4},{6,7},{7,6},{8,9},{9,8},{10,11... | collective-permute-start | bytes 552968 | tf_op jit(solution)/shard_map/ppermute | solution.py:23
  19.7 0.7 collective-permute-start.1
  20.4 1.0 collective-permute-start.2
  21.4 3.6 %collective-permute-start.3 = (bf16[6,4,40,128]{3,2,1,0:T(8,128)(2,1)}, bf16[6,4,40,128]{3,2,1,0:T(8,128)(2,1)}, u32[]{:S(2)}, u32[]{:S(2)}) collective-permute-start(bf16[6,4,40,128]{3,2,1,0:T(8,128)(2,1)} %get-tuple-element.41), channel_id=1, source_target_pairs={{16,32},{32,16},{48,64},{64,48},{80,96},{96,80},{17,33},{33,17},{4... | collective-permute-start | bytes 737288 | tf_op jit(solution)/shard_map/ppermute | solution.py:23
  25.0 0.0 copy-done.10
  25.0 0.0 copy-done.9
  25.0 0.0 copy-done.8
  25.0 0.0 copy-done.7
  25.0 0.0 copy-done.1
  25.1 0.0 copy-done
  25.1 0.4 ready.1
  25.4 0.0 copy-start.11
  25.4 0.7 copy-done.11
  26.2 0.7 copy-done.21
  26.9 0.0 copy-done.2
  26.9 0.0 copy-done.3
  26.9 0.0 copy-done.4
  26.9 0.0 copy-start.5
  26.9 0.0 copy-start.6
  26.9 2.9 %own.1 = (f32[28,48,128]{2,1,0:T(8,128)S(1)}, f32[26,48,128]{2,1,0:T(8,128)S(1)}) custom-call(bf16[2,30,40,128]{3,2,1,0:T(8,128)(2,1)S(1)} %copy-done.2, bf16[1,30,40,128]{3,2,1,0:T(8,128)(2,1)S(1)} %copy-done.4, bf16[2,30,40,128]{3,2,1,0:T(8,128)(2,1)S(1)} %copy-done.3, bf16[1152,384]{1,0:T(8,128)(2,1)S(1)} %get-tuple-element.30.refs_3_.refs_8_.refs_9_, ...), custom_call_target="tpu_custom_call" | custom-call | flops 4000000000 | bytes 8000000 | tf_op jit(solution)/shard_map/own/pallas_call | solution.py:475
  29.9 0.0 copy-done.13
  29.9 0.0 copy-done.16
  29.9 0.0 copy-start.19
  29.9 0.8 copy-done.19
  30.7 0.0 collective-permute-done.refs_4_
  30.7 0.0 collective-permute-done.1.refs_5_
  30.8 2.1 %collective-permute-start.5 = (bf16[192,128]{1,0:T(8,128)(2,1)S(1)}, bf16[192,128]{1,0:T(8,128)(2,1)S(1)}, u32[]{:S(2)}, u32[]{:S(2)}) collective-permute-start(bf16[192,128]{1,0:T(8,128)(2,1)S(1)} %get-tuple-element.57), channel_id=1, source_target_pairs={{16,32},{32,16},{48,64},{64,48},{80,96},{96,80},{17,33},{33,17},{4... | collective-permute-start | bytes 147464 | tf_op jit(solution)/shard_map/ppermute | solution.py:23
  32.9 0.1 collective-permute-start.4
  33.0 0.0 copy-done.5
  33.0 0.0 copy-done.6
  33.0 0.0 copy-start.14
  33.0 1.2 %copy-done.14 = bf16[1152,384]{1,0:T(8,128)(2,1)S(1)} copy-done((bf16[1152,384]{1,0:T(8,128)(2,1)S(1)}, bf16[1152,384]{1,0:T(8,128)(2,1)}, u32[]{:S(2)}) %copy-start.14) | copy-done | bytes 884760
  34.2 1.2 %copy-done.17 = bf16[1152,384]{1,0:T(8,128)(2,1)S(1)} copy-done((bf16[1152,384]{1,0:T(8,128)(2,1)S(1)}, bf16[1152,384]{1,0:T(8,128)(2,1)}, u32[]{:S(2)}) %copy-start.17) | copy-done | bytes 884760
  35.3 1.1 %copy-done.20 = f32[26,48,128]{2,1,0:T(8,128)S(1)} copy-done((f32[26,48,128]{2,1,0:T(8,128)S(1)}, f32[26,48,128]{2,1,0:T(8,128)}, u32[]{:S(2)}) %copy-start.20) | copy-done | bytes 639000
  36.4 2.1 %middle.1 = (bf16[6,30,48,128]{3,2,1,0:T(8,128)(2,1)S(1)}, f32[28,48,128]{2,1,0:T(8,128)S(1)}, bf16[28,48,128]{2,1,0:T(8,128)(2,1)S(1)}, bf16[26,48,128]{2,1,0:T(8,128)(2,1)S(1)}, bf16[26,48,384]{2,1,0:T(8,128)(2,1)S(1)}) custom-call(bf16[2,30,40,128]{3,2,1,0:T(8,128)(2,1)S(1)} %copy-done.2, bf16[1,30,40,128]{3,2,1,0:T(8,128)(2,1)S(1)} %copy-done.5, ...), custom_call_target="tpu_custom_call" | custom-call | flops 3000000000 | bytes 8000000 | tf_op jit(solution)/shard_map/middle/pallas_call | solution.py:475
  38.6 0.0 collective-permute-done.5.refs_8_
  38.6 0.0 collective-permute-done.4.refs_7_
  38.6 0.0 collective-permute-done.2.refs_5_
  38.6 0.0 collective-permute-done.3.refs_6_
  38.6 0.0 copy-done.15
  38.6 0.0 copy-done.18
  38.6 0.0 copy-done.22
  38.6 0.0 copy-start.12
  38.6 7.7 %rim.1 = (bf16[3584,128]{1,0:T(8,128)(2,1)S(1)}, bf16[3584,128]{1,0:T(8,128)(2,1)S(1)}, bf16[32,48,128]{2,1,0:T(8,128)(2,1)S(1)}) custom-call(bf16[6,30,48,128]{3,2,1,0:T(8,128)(2,1)S(1)} %get-tuple-element.35.refs_0_, f32[28,48,128]{2,1,0:T(8,128)S(1)} %get-tuple-element.36.refs_1_, bf16[28,48,128]{2,1,0:T(8,128)(2,1)S(1)} %get-tuple-element.37.refs_2_, ...), custom_call_target="tpu_custom_call" | custom-call | flops 5000000000 | bytes 8000000 | tf_op jit(solution)/shard_map/rim/pallas_call | solution.py:475
  46.3 0.7 collective-permute-start.6
  47.1 0.0 copy-done.12
  47.1 1.7 %input.1 = bf16[1,30,40,128]{3,2,1,0:T(8,128)(2,1)} custom-call(bf16[32,48,128]{2,1,0:T(8,128)(2,1)S(1)} %get-tuple-element.44.refs_0_, bf16[384,384]{1,0:T(8,128)(2,1)S(1)} %copy-done.12), custom_call_target="tpu_custom_call" | custom-call | flops 1000000000 | bytes 8000000 | tf_op jit(solution)/shard_map/input/pallas_call | solution.py:475
  48.7 0.4 collective-permute-done.6
  49.2 0.2 add_convert_fusion
  49.4 29.8 %all_to_all.10 = bf16[64,56,128]{2,1,0:T(8,128)(2,1)S(1)} all-to-all(bf16[64,56,128]{2,1,0:T(8,128)(2,1)S(1)} %bitcast.6), channel_id=1, replica_groups={{0,1,2,3,4,5,6,7,8,9,10,11,12,13,14,15,32,33,34,35,36,37,38,39,40,41,42..., dimensions={0} | all-to-all | bytes 1835008 | tf_op jit(solution)/shard_map/all_to_all | solution.py:559
  79.2 0.2 convert_reduce_fusion
  79.4 0.1 broadcast_in_dim.2
  79.5 19.7 %all_to_all.11 = bf16[64,56,128]{2,1,0:T(8,128)(2,1)S(1)} all-to-all(bf16[64,56,128]{2,1,0:T(8,128)(2,1)S(1)} %broadcast_in_dim.2), channel_id=1, replica_groups={{0,1,2,3,4,5,6,7,8,9,10,11,12,13,14,15,32,33,34,35,36,37,38,39,40,41,42..., dimensions={0} | all-to-all | bytes 1835008 | tf_op jit(solution)/shard_map/all_to_all | solution.py:559
  99.2 3.1 %collective-permute-start.7 = (bf16[3584,128]{1,0:T(8,128)(2,1)S(1)}, bf16[3584,128]{1,0:T(8,128)(2,1)S(1)}, u32[]{:S(2)}, u32[]{:S(2)}) collective-permute-start(bf16[3584,128]{1,0:T(8,128)(2,1)S(1)} %bitcast.4), channel_id=1, source_target_pairs={{0,16},{16,0},{32,48},{48,32},{64,80},{80,64},{96,112},{112,96},{1... | collective-permute-start | bytes 2752520 | tf_op jit(solution)/shard_map/ppermute | solution.py:565
  102.3 1.3 %place.2 = (f32[3456,128]{1,0:T(8,128)}, f32[3456,128]{1,0:T(8,128)}) custom-call(bf16[3584,128]{1,0:T(8,128)(2,1)S(1)} %bitcast.5), custom_call_target="tpu_custom_call" | custom-call | flops 2000000000 | bytes 8000000 | tf_op jit(solution)/shard_map/place/pallas_call | solution.py:475
  103.5 0.8 collective-permute-done.7.refs_0_
  104.4 1.3 %place.3 = (f32[3456,128]{1,0:T(8,128)}, f32[3456,128]{1,0:T(8,128)}) custom-call(bf16[3584,128]{1,0:T(8,128)(2,1)S(1)} %collective-permute-done.7.refs_0_, f32[3456,128]{1,0:T(8,128)} %get-tuple-element.49.refs_1_, f32[3456,128]{1,0:T(8,128)} %get-tuple-element.50.refs_2_), custom_call_target="tpu_custom_call", output_to_operand_aliasing={{0}: (1, {}), {1}: (2, {})} | custom-call | flops 2000000000 | bytes 8000000 | tf_op jit(solution)/shard_map/place/pallas_call | solution.py:475
  (15 shorter events, 0.1 us)
Async XLA Ops:
  0.6 24.4 %copy-start.10 = (f32[1,128]{1,0:T(1,128)S(1)}, f32[1,128]{1,0:T(1,128)}, u32[]{:S(2)}) copy-start(f32[1,128]{1,0:T(1,128)} %refs_5_.1) | copy-start | bytes 1540
  0.6 24.4 %copy-start.9 = (f32[1,128]{1,0:T(1,128)S(1)}, f32[1,128]{1,0:T(1,128)}, u32[]{:S(2)}) copy-start(f32[1,128]{1,0:T(1,128)} %refs_4_.1) | copy-start | bytes 1540
  0.7 24.4 %copy-start.8 = (f32[1,128]{1,0:T(1,128)S(1)}, f32[1,128]{1,0:T(1,128)}, u32[]{:S(2)}) copy-start(f32[1,128]{1,0:T(1,128)} %refs_3_.4) | copy-start | bytes 1540
  0.7 24.4 %copy-start.7 = (f32[1,128]{1,0:T(1,128)S(1)}, f32[1,128]{1,0:T(1,128)}, u32[]{:S(2)}) copy-start(f32[1,128]{1,0:T(1,128)} %refs_2_.5) | copy-start | bytes 1540
  0.7 24.4 %copy-start.1 = (bf16[3,3,3,128,128]{4,3,2,1,0:T(8,128)(2,1)S(1)}, bf16[3,3,3,128,128]{4,3,2,1,0:T(8,128)(2,1)}, u32[]{:S(2)}) copy-start(bf16[3,3,3,128,128]{4,3,2,1,0:T(8,128)(2,1)} %refs_1_.5) | copy-start | bytes 2654212
  0.7 24.4 %copy-start = (bf16[3,3,3,128,128]{4,3,2,1,0:T(8,128)(2,1)S(1)}, bf16[3,3,3,128,128]{4,3,2,1,0:T(8,128)(2,1)}, u32[]{:S(2)}) copy-start(bf16[3,3,3,128,128]{4,3,2,1,0:T(8,128)(2,1)} %refs_0_.5) | copy-start | bytes 2654212
  17.6 13.2 %collective-permute-start = (bf16[720,128]{1,0:T(8,128)(2,1)}, bf16[720,128]{1,0:T(8,128)(2,1)S(1)}, u32[]{:S(2)}, u32[]{:S(2)}) collective-permute-start(bf16[720,128]{1,0:T(8,128)(2,1)} %get-tuple-element.28), channel_id=1, source_target_pairs={{0,1},{1,0},{2,3},{3,2},{4,5},{5,4},{6,7},{7,6},{8,9},{9,8},{10,11... | collective-permute-start | bytes 552968 | tf_op jit(solution)/shard_map/ppermute | solution.py:23
  19.7 11.1 %collective-permute-start.1 = (bf16[720,128]{1,0:T(8,128)(2,1)}, bf16[720,128]{1,0:T(8,128)(2,1)S(1)}, u32[]{:S(2)}, u32[]{:S(2)}) collective-permute-start(bf16[720,128]{1,0:T(8,128)(2,1)} %get-tuple-element.29), channel_id=1, source_target_pairs={{1,2},{2,1},{3,4},{4,3},{5,6},{6,5},{7,8},{8,7},{9,10},{10,9},{11,... | collective-permute-start | bytes 552968 | tf_op jit(solution)/shard_map/ppermute | solution.py:23
  20.4 18.2 %collective-permute-start.2 = (bf16[6,4,40,128]{3,2,1,0:T(8,128)(2,1)}, bf16[6,4,40,128]{3,2,1,0:T(8,128)(2,1)}, u32[]{:S(2)}, u32[]{:S(2)}) collective-permute-start(bf16[6,4,40,128]{3,2,1,0:T(8,128)(2,1)} %get-tuple-element.40), channel_id=1, source_target_pairs={{0,16},{16,0},{32,48},{48,32},{64,80},{80,64},{96,112},{112,96},{1... | collective-permute-start | bytes 737288 | tf_op jit(solution)/shard_map/ppermute | solution.py:23
  21.4 5.5 %copy-start.2 = (bf16[2,30,40,128]{3,2,1,0:T(8,128)(2,1)S(1)}, bf16[2,30,40,128]{3,2,1,0:T(8,128)(2,1)}, u32[]{:S(2)}) copy-start(bf16[2,30,40,128]{3,2,1,0:T(8,128)(2,1)} %refs_0_.7) | copy-start | bytes 1843204
  21.4 5.5 %copy-start.3 = (bf16[2,30,40,128]{3,2,1,0:T(8,128)(2,1)S(1)}, bf16[2,30,40,128]{3,2,1,0:T(8,128)(2,1)}, u32[]{:S(2)}) copy-start(bf16[2,30,40,128]{3,2,1,0:T(8,128)(2,1)} %refs_2_.7) | copy-start | bytes 1843204
  21.4 5.5 %copy-start.4 = (bf16[1,30,40,128]{3,2,1,0:T(8,128)(2,1)S(1)}, bf16[1,30,40,128]{3,2,1,0:T(8,128)(2,1)}, u32[]{:S(2)}) copy-start(bf16[1,30,40,128]{3,2,1,0:T(8,128)(2,1)} %refs_1_.7) | copy-start | bytes 921604
  21.4 17.2 %collective-permute-start.3 = (bf16[6,4,40,128]{3,2,1,0:T(8,128)(2,1)}, bf16[6,4,40,128]{3,2,1,0:T(8,128)(2,1)}, u32[]{:S(2)}, u32[]{:S(2)}) collective-permute-start(bf16[6,4,40,128]{3,2,1,0:T(8,128)(2,1)} %get-tuple-element.41), channel_id=1, source_target_pairs={{16,32},{32,16},{48,64},{64,48},{80,96},{96,80},{17,33},{33,17},{4... | collective-permute-start | bytes 737288 | tf_op jit(solution)/shard_map/ppermute | solution.py:23
  25.4 0.7 copy-start.11
  26.2 0.7 copy-start.21
  26.9 3.0 %copy-start.13 = (bf16[1152,384]{1,0:T(8,128)(2,1)}, bf16[1152,384]{1,0:T(8,128)(2,1)S(1)}, u32[]{:S(2)}) copy-start(bf16[1152,384]{1,0:T(8,128)(2,1)S(1)} %get-tuple-element.30.refs_3_.refs_8_.refs_9_) | copy-start | bytes 2654212
  26.9 3.0 %copy-start.16 = (bf16[1152,384]{1,0:T(8,128)(2,1)}, bf16[1152,384]{1,0:T(8,128)(2,1)S(1)}, u32[]{:S(2)}) copy-start(bf16[1152,384]{1,0:T(8,128)(2,1)S(1)} %get-tuple-element.31.refs_4_.refs_9_.refs_10_) | copy-start | bytes 2654212
  26.9 6.1 %copy-start.5 = (bf16[1,30,40,128]{3,2,1,0:T(8,128)(2,1)S(1)}, bf16[1,30,40,128]{3,2,1,0:T(8,128)(2,1)}, u32[]{:S(2)}) copy-start(bf16[1,30,40,128]{3,2,1,0:T(8,128)(2,1)} %refs_1_.7) | copy-start | bytes 921604
  26.9 6.1 %copy-start.6 = (bf16[1,30,40,128]{3,2,1,0:T(8,128)(2,1)S(1)}, bf16[1,30,40,128]{3,2,1,0:T(8,128)(2,1)}, u32[]{:S(2)}) copy-start(bf16[1,30,40,128]{3,2,1,0:T(8,128)(2,1)} %refs_3_.5) | copy-start | bytes 921604
  29.9 0.8 copy-start.19
  30.8 7.8 %collective-permute-start.5 = (bf16[192,128]{1,0:T(8,128)(2,1)S(1)}, bf16[192,128]{1,0:T(8,128)(2,1)S(1)}, u32[]{:S(2)}, u32[]{:S(2)}) collective-permute-start(bf16[192,128]{1,0:T(8,128)(2,1)S(1)} %get-tuple-element.57), channel_id=1, source_target_pairs={{16,32},{32,16},{48,64},{64,48},{80,96},{96,80},{17,33},{33,17},{4... | collective-permute-start | bytes 147464 | tf_op jit(solution)/shard_map/ppermute | solution.py:23
  32.9 5.7 %collective-permute-start.4 = (bf16[192,128]{1,0:T(8,128)(2,1)S(1)}, bf16[192,128]{1,0:T(8,128)(2,1)S(1)}, u32[]{:S(2)}, u32[]{:S(2)}) collective-permute-start(bf16[192,128]{1,0:T(8,128)(2,1)S(1)} %get-tuple-element.58), channel_id=1, source_target_pairs={{0,16},{16,0},{32,48},{48,32},{64,80},{80,64},{96,112},{112,96},{1... | collective-permute-start | bytes 147464 | tf_op jit(solution)/shard_map/ppermute | solution.py:23
  33.0 1.2 %copy-start.14 = (bf16[1152,384]{1,0:T(8,128)(2,1)S(1)}, bf16[1152,384]{1,0:T(8,128)(2,1)}, u32[]{:S(2)}) copy-start(bf16[1152,384]{1,0:T(8,128)(2,1)} %copy-done.13) | copy-start | bytes 2654212
  34.2 1.2 %copy-start.17 = (bf16[1152,384]{1,0:T(8,128)(2,1)S(1)}, bf16[1152,384]{1,0:T(8,128)(2,1)}, u32[]{:S(2)}) copy-start(bf16[1152,384]{1,0:T(8,128)(2,1)} %copy-done.16) | copy-start | bytes 2654212
  35.3 1.1 %copy-start.20 = (f32[26,48,128]{2,1,0:T(8,128)S(1)}, f32[26,48,128]{2,1,0:T(8,128)}, u32[]{:S(2)}) copy-start(f32[26,48,128]{2,1,0:T(8,128)} %copy-done.19) | copy-start | bytes 1916932
  36.4 2.2 %copy-start.15 = (bf16[1152,384]{1,0:T(8,128)(2,1)S(1)}, bf16[1152,384]{1,0:T(8,128)(2,1)}, u32[]{:S(2)}) copy-start(bf16[1152,384]{1,0:T(8,128)(2,1)} %copy-done.13) | copy-start | bytes 2654212
  36.4 2.2 %copy-start.18 = (bf16[1152,384]{1,0:T(8,128)(2,1)S(1)}, bf16[1152,384]{1,0:T(8,128)(2,1)}, u32[]{:S(2)}) copy-start(bf16[1152,384]{1,0:T(8,128)(2,1)} %copy-done.16) | copy-start | bytes 2654212
  36.4 2.2 %copy-start.22 = (bf16[384,384]{1,0:T(8,128)(2,1)S(1)}, bf16[384,384]{1,0:T(8,128)(2,1)}, u32[]{:S(2)}) copy-start(bf16[384,384]{1,0:T(8,128)(2,1)} %copy-done.21) | copy-start | bytes 884740
  38.6 8.5 %copy-start.12 = (bf16[384,384]{1,0:T(8,128)(2,1)S(1)}, bf16[384,384]{1,0:T(8,128)(2,1)}, u32[]{:S(2)}) copy-start(bf16[384,384]{1,0:T(8,128)(2,1)} %copy-done.11) | copy-start | bytes 884740
  46.3 2.8 %collective-permute-start.6 = (bf16[3584,128]{1,0:T(8,128)(2,1)S(1)}, bf16[3584,128]{1,0:T(8,128)(2,1)S(1)}, u32[]{:S(2)}, u32[]{:S(2)}) collective-permute-start(bf16[3584,128]{1,0:T(8,128)(2,1)S(1)} %get-tuple-element.43), channel_id=1, source_target_pairs={{0,16},{16,0},{32,48},{48,32},{64,80},{80,64},{96,112},{112,96},{1... | collective-permute-start | bytes 2752520 | tf_op jit(solution)/shard_map/ppermute | solution.py:550
  99.2 5.2 %collective-permute-start.7 = (bf16[3584,128]{1,0:T(8,128)(2,1)S(1)}, bf16[3584,128]{1,0:T(8,128)(2,1)S(1)}, u32[]{:S(2)}, u32[]{:S(2)}) collective-permute-start(bf16[3584,128]{1,0:T(8,128)(2,1)S(1)} %bitcast.4), channel_id=1, source_target_pairs={{0,16},{16,0},{32,48},{48,32},{64,80},{80,64},{96,112},{112,96},{1... | collective-permute-start | bytes 2752520 | tf_op jit(solution)/shard_map/ppermute | solution.py:565

commit v3 on v2

--- a/solution.py
+++ b/solution.py
@@ -206,28 +206,18 @@
         )
     ]
     odd_row, odd_col = is_odd("ha"), is_odd("wa")
-    last = rows - RIM
-    near_at, far_at = jnp.where(odd_row, 0, last), jnp.where(odd_row, last, 0)
     for copy in copies:
         copy.start()
-    straight, frame = [], 0
-    for source in (cache_in_at, frames_in_at, cache_mid_at, cot_at):
-        size = source.shape[0]
-        for start, target in ((near_at, row_near), (far_at, row_far)):
-            straight.append(
-                pltpu.make_async_copy(
-                    source.at[:, pl.ds(start, RIM)],
-                    target.at[frame : frame + size],
-                    sems.at[4 + len(straight)],
-                )
-            )
-            straight[-1].start()
-        frame += size
     for copy in copies:
         copy.wait()
     sources = (
         (cache_in, 0), (cache_in, 1), (frames_in, 0), (cache_mid, 0), (cache_mid, 1), (cot, 0)
     )
+    last = rows - RIM
+    near_at, far_at = jnp.where(odd_row, 0, last), jnp.where(odd_row, last, 0)
+    for frame, (ref, i) in enumerate(sources):
+        row_near[frame] = ref[i, pl.ds(near_at, RIM)]
+        row_far[frame] = ref[i, pl.ds(far_at, RIM)]
     lanes = col_near.shape[-1]
     lower = lax.broadcasted_iota(jnp.int32, (rows, 2 * RIM, lanes), 1) < RIM
 
@@ -245,8 +235,19 @@
         far.append(jnp.where(odd_col, tails, heads))
     col_near[...] = jnp.stack(near, axis=1).reshape(-1, lanes).astype(BF)
     col_far[...] = jnp.stack(far, axis=1).reshape(-1, lanes).astype(BF)
-    for copy in straight:
-        copy.wait()
+
+
+def corner_kernel(col_near, col_far, near, far):
+    size = near.shape[0] // 2
+    last = col_near.shape[0] - size
+    odd = is_odd("ha")
+    for target, start in (
+        (near, jnp.where(odd, 0, last)),
+        (far, jnp.where(odd, last, 0)),
+    ):
+        at = pl.ds(pl.multiple_of(start, 16), size)
+        target[:size] = col_near[at]
+        target[size:] = col_far[at]
 
 
 def ready_kernel(
@@ -486,14 +487,13 @@
     fields = (cache_in, frames_in, cache_mid, cotangent)
     rim_rows, rim_cols = shaped(6, RIM, cols, chans), shaped(6 * rows * RIM, chans)
     row_near, row_far, col_near, col_far = call(
-        pack_kernel, "pack", (rim_rows, rim_rows, rim_cols, rim_cols), 60, 1e9, fields,
+        pack_kernel, "pack", (rim_rows, rim_rows, rim_cols, rim_cols), 53, 1e9, fields,
         in_specs=[anywhere] * 4,
-        out_specs=(anywhere, anywhere, inner, inner),
-        scratch_shapes=[pltpu.VMEM(v.shape, BF) for v in fields] + [pltpu.SemaphoreType.DMA((12,))],
+        scratch_shapes=[pltpu.VMEM(v.shape, BF) for v in fields] + [pltpu.SemaphoreType.DMA((4,))],
     )
     ahead, back = shaped(9 * chans, 3 * chans), shaped(3 * chans, 3 * chans)
     ahead_one, ahead_two, back_one, back_two, affine = call(
-        ready_kernel, "ready", (ahead, ahead, back, back, shaped(8, chans, dtype=F32)), 16, 2e9,
+        ready_kernel, "ready", (ahead, ahead, back, back, shaped(8, chans, dtype=F32)), 10, 2e9,
         (w_first, w_second, scale_first, shift_first, scale_second, shift_second), sizes=False,
     )
     part_one, part_two = call(
@@ -502,16 +502,19 @@
             shaped(rows - 2, full, chans, dtype=F32),
             shaped(rows - 4, full, chans, dtype=F32),
         ),
-        24, 4e9, (cache_in, frames_in, cache_mid, ahead_one, ahead_two),
+        12, 4e9, (cache_in, frames_in, cache_mid, ahead_one, ahead_two),
         scratch_shapes=[pltpu.VMEM((5, rows, full, chans), BF)],
     )
     col_near, col_far = trade("wa", col_near, col_far)
     row_near, row_far = trade("ha", row_near, row_far)
     size = 6 * RIM * RIM
-    head = jnp.concatenate([col_near[:size], col_far[:size]], axis=0)
-    tail = jnp.concatenate([col_near[-size:], col_far[-size:]], axis=0)
-    odd = is_odd("ha")
-    corner_near, corner_far = trade("ha", jnp.where(odd, head, tail), jnp.where(odd, tail, head))
+    corner_near, corner_far = trade(
+        "ha",
+        *call(
+            corner_kernel, "corner", [shaped(2 * size, chans)] * 2, 4, 1e8, (col_near, col_far),
+            sizes=False,
+        ),
+    )
 
     field, slope_mid, a_mid, d_mid, moved_mid = call(
         middle_kernel, "middle",
@@ -522,12 +525,12 @@
             shaped(rows - 4, full, chans),
             shaped(rows - 4, full, 3 * chans),
         ),
-        28, 3e9, (*fields, col_near, col_far, part_one, part_two, ahead_one, ahead_two, affine),
+        16, 3e9, (*fields, col_near, col_far, part_one, part_two, ahead_one, ahead_two, affine),
     )
     keep, send, d_one = call(
         rim_kernel, "rim",
         (shaped(share * chips, chans), shaped(share * chips, chans), shaped(rows + 2, full, chans)),
-        28, 5e9,
+        20, 5e9,
         (
             field, slope_mid, a_mid, d_mid, moved_mid, row_near, row_far, corner_near, corner_far,
             ahead_one, ahead_two, back_two, affine,
@@ -549,7 +552,7 @@
     pairs, _ = swaps("ha")
     got = lax.ppermute(send, "ha", pairs)
     (grad_input,) = call(
-        input_kernel, "input", (shaped(1, rows, cols, chans),), 12, 1e9, (d_one, back_one)
+        input_kernel, "input", (shaped(1, rows, cols, chans),), 8, 1e9, (d_one, back_one)
     )
     got, grad_input = lax.optimization_barrier((got, grad_input))
     chip_sum = (keep.astype(F32) + got.astype(F32)).astype(BF)
@@ -569,7 +572,7 @@
     def place(source, *given):
         return call(
             lambda *refs: place_kernel(parts, not given, *refs), "place",
-            [shaped(total, chans, dtype=F32)] * 2, 8, 2e9, (source, *given), sizes=False,
+            [shaped(total, chans, dtype=F32)] * 2, 6, 2e9, (source, *given), sizes=False,
             in_specs=[inner] + [anywhere] * len(given),
             out_specs=(anywhere, anywhere),
             scratch_shapes=[

time: 106 us -> 84.6 us (0.80)
  Pallas kernels: 34.1 us -> 18 us
  local copies, waits for them, and re-layouts: 5.89 us -> 0.16 us
  starting transfers between devices: 13.4 us -> 14.9 us
  blocking collectives: 49.5 us -> 48.1 us
    pallas_call x8 -> x9, Pallas kernels: 34.1 us -> 18 us  [call(): pl.pallas_call(body, out_shape=tuple(out_shape), cost_estimate=pl.CostEst...]
    unnamed x46 -> x20, local copies, waits for them, and re-layouts: 5.76 us -> 0.04 us
    ppermute x6, starting transfers between devices: 9.6 us -> 11.4 us  [trade(): return (lax.ppermute(near, axis, first), lax.ppermute(far, axis, second))]
    all_to_all x2, blocking collectives: 49.5 us -> 48.1 us  [spread_out(): lax.all_to_all(value.reshape(chips, share, chans), BOTH, 0, 0, axis_index...]
  transfers between devices with their start and end apart: 8 -> 8, of which waited for: 2 -> 2; matrix products, arithmetic and copies ran while one was open for 0% -> 0% of each run, Pallas kernels for 8% -> 10%
where the time goes in v3:
time: 84.6 us; the launch traced here: 84.4 us
  blocking collectives  48.1 us (57%)
  Pallas kernels  18 us (21%)
  starting transfers between devices  14.9 us (18%)
  waiting for transfers between devices  1.65 us (2%)
  between operations  1.08 us (1%)
    all_to_all x2, blocking collectives, spread_out(): lax.all_to_all(value.reshape(chips, share, chans), BOTH, 0, 0, axis_index...  48.1 us
    pallas_call x9, Pallas kernels, call(): pl.pallas_call(body, out_shape=tuple(out_shape), cost_estimate=pl.CostEst...  18 us
    ppermute x6, starting transfers between devices, trade(): return (lax.ppermute(near, axis, first), lax.ppermute(far, axis, second))  11.4 us
    ppermute x1, starting transfers between devices, per_device(): other = lax.ppermute(one, 'ha', pairs)  3.19 us
  transfers between devices with their start and end apart: 8, of which 2 were waited for; matrix products, arithmetic and copies ran while one was open for 0% of the time, Pallas kernels for 10%

profile of v3, /device:TPU:1, one launch (start us, length us, event | category | flops | bytes accessed | tf_op | source)
XLA Modules:
  0.0 84.4 jit_solution(11528514501435870464)
XLA Ops:
  0.6 0.0 copy-start.9
  0.6 0.0 copy-start.8
  0.7 0.0 copy-start.7
  0.7 0.0 copy-start.6
  0.7 0.0 copy-start.1
  0.7 0.0 copy-start
  0.7 1.8 %pack.1 = (bf16[6,4,40,128]{3,2,1,0:T(8,128)(2,1)S(1)}, bf16[6,4,40,128]{3,2,1,0:T(8,128)(2,1)S(1)}, bf16[720,128]{1,0:T(8,128)(2,1)S(1)}, bf16[720,128]{1,0:T(8,128)(2,1)S(1)}) custom-call(bf16[2,30,40,128]{3,2,1,0:T(8,128)(2,1)} %refs_0_.7, bf16[1,30,40,128]{3,2,1,0:T(8,128)(2,1)} %refs_1_.7, bf16[2,30,40,128]{3,2,1,0:T(8,128)(2,1)} %refs_2_.7, ...), custom_call_target="tpu_custom_call" | custom-call | flops 1000000000 | bytes 8000000 | tf_op jit(solution)/shard_map/pack/pallas_call | solution.py:476
  2.5 2.1 %collective-permute-start = (bf16[720,128]{1,0:T(8,128)(2,1)S(1)}, bf16[720,128]{1,0:T(8,128)(2,1)S(1)}, u32[]{:S(2)}, u32[]{:S(2)}) collective-permute-start(bf16[720,128]{1,0:T(8,128)(2,1)S(1)} %get-tuple-element.30), channel_id=1, source_target_pairs={{0,1},{1,0},{2,3},{3,2},{4,5},{5,4},{6,7},{7,6},{8,9},{9,8},{10,11... | collective-permute-start | bytes 552968 | tf_op jit(solution)/shard_map/ppermute | solution.py:23
  4.6 0.7 collective-permute-start.1
  5.3 1.0 %collective-permute-start.2 = (bf16[6,4,40,128]{3,2,1,0:T(8,128)(2,1)S(1)}, bf16[6,4,40,128]{3,2,1,0:T(8,128)(2,1)S(1)}, u32[]{:S(2)}, u32[]{:S(2)}) collective-permute-start(bf16[6,4,40,128]{3,2,1,0:T(8,128)(2,1)S(1)} %get-tuple-element.42), channel_id=1, source_target_pairs={{0,16},{16,0},{32,48},{48,32},{64,80},{80,64},{96,112},{112,96},{1... | collective-permute-start | bytes 737288 | tf_op jit(solution)/shard_map/ppermute | solution.py:23
  6.3 0.0 copy-start.2
  6.3 0.0 copy-start.3
  6.3 0.0 copy-start.4
  6.3 3.6 %collective-permute-start.3 = (bf16[6,4,40,128]{3,2,1,0:T(8,128)(2,1)S(1)}, bf16[6,4,40,128]{3,2,1,0:T(8,128)(2,1)S(1)}, u32[]{:S(2)}, u32[]{:S(2)}) collective-permute-start(bf16[6,4,40,128]{3,2,1,0:T(8,128)(2,1)S(1)} %get-tuple-element.43), channel_id=1, source_target_pairs={{16,32},{32,16},{48,64},{64,48},{80,96},{96,80},{17,33},{33,17},{4... | collective-permute-start | bytes 737288 | tf_op jit(solution)/shard_map/ppermute | solution.py:23
  9.9 0.0 copy-done.9
  9.9 0.0 copy-done.8
  9.9 0.0 copy-done.7
  9.9 0.0 copy-done.6
  10.0 0.0 copy-done.1
  10.0 0.0 copy-done
  10.0 0.4 ready.1
  10.3 0.0 copy-done.2
  10.3 0.0 copy-done.3
  10.4 0.0 copy-done.4
  10.4 0.0 copy-start.5
  10.4 2.9 %own.1 = (f32[28,48,128]{2,1,0:T(8,128)S(1)}, f32[26,48,128]{2,1,0:T(8,128)S(1)}) custom-call(bf16[2,30,40,128]{3,2,1,0:T(8,128)(2,1)S(1)} %copy-done.2, bf16[1,30,40,128]{3,2,1,0:T(8,128)(2,1)S(1)} %copy-done.4, bf16[2,30,40,128]{3,2,1,0:T(8,128)(2,1)S(1)} %copy-done.3, bf16[1152,384]{1,0:T(8,128)(2,1)S(1)} %get-tuple-element.32.refs_3_.refs_8_.refs_9_, ...), custom_call_target="tpu_custom_call" | custom-call | flops 4000000000 | bytes 8000000 | tf_op jit(solution)/shard_map/own/pallas_call | solution.py:476
  13.3 0.0 collective-permute-done.refs_4_.refs_0_
  13.3 0.0 collective-permute-done.1.refs_5_.refs_1_
  13.4 0.1 collective-permute-start.4
  13.5 3.9 %collective-permute-start.5 = (bf16[192,128]{1,0:T(8,128)(2,1)S(1)}, bf16[192,128]{1,0:T(8,128)(2,1)S(1)}, u32[]{:S(2)}, u32[]{:S(2)}) collective-permute-start(bf16[192,128]{1,0:T(8,128)(2,1)S(1)} %get-tuple-element.45), channel_id=1, source_target_pairs={{16,32},{32,16},{48,64},{64,48},{80,96},{96,80},{17,33},{33,17},{4... | collective-permute-start | bytes 147464 | tf_op jit(solution)/shard_map/ppermute | solution.py:23
  17.4 0.0 copy-done.5
  17.4 2.2 %middle.1 = (bf16[6,30,48,128]{3,2,1,0:T(8,128)(2,1)S(1)}, f32[28,48,128]{2,1,0:T(8,128)S(1)}, bf16[28,48,128]{2,1,0:T(8,128)(2,1)S(1)}, bf16[26,48,128]{2,1,0:T(8,128)(2,1)S(1)}, bf16[26,48,384]{2,1,0:T(8,128)(2,1)S(1)}) custom-call(bf16[2,30,40,128]{3,2,1,0:T(8,128)(2,1)S(1)} %copy-done.2, bf16[1,30,40,128]{3,2,1,0:T(8,128)(2,1)S(1)} %copy-done.4, ...), custom_call_target="tpu_custom_call" | custom-call | flops 3000000000 | bytes 8000000 | tf_op jit(solution)/shard_map/middle/pallas_call | solution.py:476
  19.6 0.0 collective-permute-done.4.refs_7_
  19.6 0.0 collective-permute-done.5.refs_8_
  19.6 0.0 collective-permute-done.2.refs_5_
  19.6 0.0 collective-permute-done.3.refs_6_
  19.6 6.6 %rim.1 = (bf16[3584,128]{1,0:T(8,128)(2,1)S(1)}, bf16[3584,128]{1,0:T(8,128)(2,1)S(1)}, bf16[32,48,128]{2,1,0:T(8,128)(2,1)S(1)}) custom-call(bf16[6,30,48,128]{3,2,1,0:T(8,128)(2,1)S(1)} %get-tuple-element.37.refs_0_, f32[28,48,128]{2,1,0:T(8,128)S(1)} %get-tuple-element.38.refs_1_, bf16[28,48,128]{2,1,0:T(8,128)(2,1)S(1)} %get-tuple-element.39.refs_2_, ...), custom_call_target="tpu_custom_call" | custom-call | flops 5000000000 | bytes 8000000 | tf_op jit(solution)/shard_map/rim/pallas_call | solution.py:476
  26.2 0.3 collective-permute-start.6
  26.5 1.7 %input.1 = bf16[1,30,40,128]{3,2,1,0:T(8,128)(2,1)} custom-call(bf16[32,48,128]{2,1,0:T(8,128)(2,1)S(1)} %get-tuple-element.48.refs_0_, bf16[384,384]{1,0:T(8,128)(2,1)S(1)} %get-tuple-element.49.refs_1_), custom_call_target="tpu_custom_call" | custom-call | flops 1000000000 | bytes 8000000 | tf_op jit(solution)/shard_map/input/pallas_call | solution.py:476
  28.2 0.8 collective-permute-done.6
  29.0 0.2 add_convert_fusion
  29.2 28.7 %all_to_all.10 = bf16[64,56,128]{2,1,0:T(8,128)(2,1)S(1)} all-to-all(bf16[64,56,128]{2,1,0:T(8,128)(2,1)S(1)} %bitcast.6), channel_id=1, replica_groups={{0,1,2,3,4,5,6,7,8,9,10,11,12,13,14,15,32,33,34,35,36,37,38,39,40,41,42..., dimensions={0} | all-to-all | bytes 1835008 | tf_op jit(solution)/shard_map/all_to_all | solution.py:562
  57.9 0.2 convert_reduce_fusion
  58.0 0.1 broadcast_in_dim.2
  58.2 19.5 %all_to_all.11 = bf16[64,56,128]{2,1,0:T(8,128)(2,1)S(1)} all-to-all(bf16[64,56,128]{2,1,0:T(8,128)(2,1)S(1)} %broadcast_in_dim.2), channel_id=1, replica_groups={{0,1,2,3,4,5,6,7,8,9,10,11,12,13,14,15,32,33,34,35,36,37,38,39,40,41,42..., dimensions={0} | all-to-all | bytes 1835008 | tf_op jit(solution)/shard_map/all_to_all | solution.py:562
  77.6 3.2 %collective-permute-start.7 = (bf16[3584,128]{1,0:T(8,128)(2,1)S(1)}, bf16[3584,128]{1,0:T(8,128)(2,1)S(1)}, u32[]{:S(2)}, u32[]{:S(2)}) collective-permute-start(bf16[3584,128]{1,0:T(8,128)(2,1)S(1)} %bitcast.4), channel_id=1, source_target_pairs={{0,16},{16,0},{32,48},{48,32},{64,80},{80,64},{96,112},{112,96},{1... | collective-permute-start | bytes 2752520 | tf_op jit(solution)/shard_map/ppermute | solution.py:568
  80.8 1.3 %place.2 = (f32[3456,128]{1,0:T(8,128)}, f32[3456,128]{1,0:T(8,128)}) custom-call(bf16[3584,128]{1,0:T(8,128)(2,1)S(1)} %bitcast.5), custom_call_target="tpu_custom_call" | custom-call | flops 2000000000 | bytes 8000000 | tf_op jit(solution)/shard_map/place/pallas_call | solution.py:476
  82.1 0.8 collective-permute-done.7.refs_0_
  82.9 1.3 %place.3 = (f32[3456,128]{1,0:T(8,128)}, f32[3456,128]{1,0:T(8,128)}) custom-call(bf16[3584,128]{1,0:T(8,128)(2,1)S(1)} %collective-permute-done.7.refs_0_, f32[3456,128]{1,0:T(8,128)} %get-tuple-element.53.refs_1_, f32[3456,128]{1,0:T(8,128)} %get-tuple-element.54.refs_2_), custom_call_target="tpu_custom_call", output_to_operand_aliasing={{0}: (1, {}), {1}: (2, {})} | custom-call | flops 2000000000 | bytes 8000000 | tf_op jit(solution)/shard_map/place/pallas_call | solution.py:476
  (2 shorter events, 0.0 us)
Async XLA Ops:
  0.6 9.3 %copy-start.9 = (f32[1,128]{1,0:T(1,128)S(1)}, f32[1,128]{1,0:T(1,128)}, u32[]{:S(2)}) copy-start(f32[1,128]{1,0:T(1,128)} %refs_5_.1) | copy-start | bytes 1540
  0.6 9.3 %copy-start.8 = (f32[1,128]{1,0:T(1,128)S(1)}, f32[1,128]{1,0:T(1,128)}, u32[]{:S(2)}) copy-start(f32[1,128]{1,0:T(1,128)} %refs_4_.1) | copy-start | bytes 1540
  0.7 9.3 %copy-start.7 = (f32[1,128]{1,0:T(1,128)S(1)}, f32[1,128]{1,0:T(1,128)}, u32[]{:S(2)}) copy-start(f32[1,128]{1,0:T(1,128)} %refs_3_.4) | copy-start | bytes 1540
  0.7 9.3 %copy-start.6 = (f32[1,128]{1,0:T(1,128)S(1)}, f32[1,128]{1,0:T(1,128)}, u32[]{:S(2)}) copy-start(f32[1,128]{1,0:T(1,128)} %refs_2_.5) | copy-start | bytes 1540
  0.7 9.3 %copy-start.1 = (bf16[3,3,3,128,128]{4,3,2,1,0:T(8,128)(2,1)S(1)}, bf16[3,3,3,128,128]{4,3,2,1,0:T(8,128)(2,1)}, u32[]{:S(2)}) copy-start(bf16[3,3,3,128,128]{4,3,2,1,0:T(8,128)(2,1)} %refs_1_.5) | copy-start | bytes 2654212
  0.7 9.3 %copy-start = (bf16[3,3,3,128,128]{4,3,2,1,0:T(8,128)(2,1)S(1)}, bf16[3,3,3,128,128]{4,3,2,1,0:T(8,128)(2,1)}, u32[]{:S(2)}) copy-start(bf16[3,3,3,128,128]{4,3,2,1,0:T(8,128)(2,1)} %refs_0_.5) | copy-start | bytes 2654212
  2.5 10.9 %collective-permute-start = (bf16[720,128]{1,0:T(8,128)(2,1)S(1)}, bf16[720,128]{1,0:T(8,128)(2,1)S(1)}, u32[]{:S(2)}, u32[]{:S(2)}) collective-permute-start(bf16[720,128]{1,0:T(8,128)(2,1)S(1)} %get-tuple-element.30), channel_id=1, source_target_pairs={{0,1},{1,0},{2,3},{3,2},{4,5},{5,4},{6,7},{7,6},{8,9},{9,8},{10,11... | collective-permute-start | bytes 552968 | tf_op jit(solution)/shard_map/ppermute | solution.py:23
  4.6 8.8 %collective-permute-start.1 = (bf16[720,128]{1,0:T(8,128)(2,1)S(1)}, bf16[720,128]{1,0:T(8,128)(2,1)S(1)}, u32[]{:S(2)}, u32[]{:S(2)}) collective-permute-start(bf16[720,128]{1,0:T(8,128)(2,1)S(1)} %get-tuple-element.31), channel_id=1, source_target_pairs={{1,2},{2,1},{3,4},{4,3},{5,6},{6,5},{7,8},{8,7},{9,10},{10,9},{11,... | collective-permute-start | bytes 552968 | tf_op jit(solution)/shard_map/ppermute | solution.py:23
  5.3 14.3 %collective-permute-start.2 = (bf16[6,4,40,128]{3,2,1,0:T(8,128)(2,1)S(1)}, bf16[6,4,40,128]{3,2,1,0:T(8,128)(2,1)S(1)}, u32[]{:S(2)}, u32[]{:S(2)}) collective-permute-start(bf16[6,4,40,128]{3,2,1,0:T(8,128)(2,1)S(1)} %get-tuple-element.42), channel_id=1, source_target_pairs={{0,16},{16,0},{32,48},{48,32},{64,80},{80,64},{96,112},{112,96},{1... | collective-permute-start | bytes 737288 | tf_op jit(solution)/shard_map/ppermute | solution.py:23
  6.3 4.0 %copy-start.2 = (bf16[2,30,40,128]{3,2,1,0:T(8,128)(2,1)S(1)}, bf16[2,30,40,128]{3,2,1,0:T(8,128)(2,1)}, u32[]{:S(2)}) copy-start(bf16[2,30,40,128]{3,2,1,0:T(8,128)(2,1)} %refs_0_.7) | copy-start | bytes 1843204
  6.3 4.1 %copy-start.3 = (bf16[2,30,40,128]{3,2,1,0:T(8,128)(2,1)S(1)}, bf16[2,30,40,128]{3,2,1,0:T(8,128)(2,1)}, u32[]{:S(2)}) copy-start(bf16[2,30,40,128]{3,2,1,0:T(8,128)(2,1)} %refs_2_.7) | copy-start | bytes 1843204
  6.3 4.1 %copy-start.4 = (bf16[1,30,40,128]{3,2,1,0:T(8,128)(2,1)S(1)}, bf16[1,30,40,128]{3,2,1,0:T(8,128)(2,1)}, u32[]{:S(2)}) copy-start(bf16[1,30,40,128]{3,2,1,0:T(8,128)(2,1)} %refs_1_.7) | copy-start | bytes 921604
  6.3 13.3 %collective-permute-start.3 = (bf16[6,4,40,128]{3,2,1,0:T(8,128)(2,1)S(1)}, bf16[6,4,40,128]{3,2,1,0:T(8,128)(2,1)S(1)}, u32[]{:S(2)}, u32[]{:S(2)}) collective-permute-start(bf16[6,4,40,128]{3,2,1,0:T(8,128)(2,1)S(1)} %get-tuple-element.43), channel_id=1, source_target_pairs={{16,32},{32,16},{48,64},{64,48},{80,96},{96,80},{17,33},{33,17},{4... | collective-permute-start | bytes 737288 | tf_op jit(solution)/shard_map/ppermute | solution.py:23
  10.4 7.0 %copy-start.5 = (bf16[1,30,40,128]{3,2,1,0:T(8,128)(2,1)S(1)}, bf16[1,30,40,128]{3,2,1,0:T(8,128)(2,1)}, u32[]{:S(2)}) copy-start(bf16[1,30,40,128]{3,2,1,0:T(8,128)(2,1)} %refs_3_.5) | copy-start | bytes 921604
  13.4 6.2 %collective-permute-start.4 = (bf16[192,128]{1,0:T(8,128)(2,1)S(1)}, bf16[192,128]{1,0:T(8,128)(2,1)S(1)}, u32[]{:S(2)}, u32[]{:S(2)}) collective-permute-start(bf16[192,128]{1,0:T(8,128)(2,1)S(1)} %get-tuple-element.44), channel_id=1, source_target_pairs={{0,16},{16,0},{32,48},{48,32},{64,80},{80,64},{96,112},{112,96},{1... | collective-permute-start | bytes 147464 | tf_op jit(solution)/shard_map/ppermute | solution.py:23
  13.5 6.1 %collective-permute-start.5 = (bf16[192,128]{1,0:T(8,128)(2,1)S(1)}, bf16[192,128]{1,0:T(8,128)(2,1)S(1)}, u32[]{:S(2)}, u32[]{:S(2)}) collective-permute-start(bf16[192,128]{1,0:T(8,128)(2,1)S(1)} %get-tuple-element.45), channel_id=1, source_target_pairs={{16,32},{32,16},{48,64},{64,48},{80,96},{96,80},{17,33},{33,17},{4... | collective-permute-start | bytes 147464 | tf_op jit(solution)/shard_map/ppermute | solution.py:23
  26.2 2.7 %collective-permute-start.6 = (bf16[3584,128]{1,0:T(8,128)(2,1)S(1)}, bf16[3584,128]{1,0:T(8,128)(2,1)S(1)}, u32[]{:S(2)}, u32[]{:S(2)}) collective-permute-start(bf16[3584,128]{1,0:T(8,128)(2,1)S(1)} %get-tuple-element.47), channel_id=1, source_target_pairs={{0,16},{16,0},{32,48},{48,32},{64,80},{80,64},{96,112},{112,96},{1... | collective-permute-start | bytes 2752520 | tf_op jit(solution)/shard_map/ppermute | solution.py:553
  77.6 5.3 %collective-permute-start.7 = (bf16[3584,128]{1,0:T(8,128)(2,1)S(1)}, bf16[3584,128]{1,0:T(8,128)(2,1)S(1)}, u32[]{:S(2)}, u32[]{:S(2)}) collective-permute-start(bf16[3584,128]{1,0:T(8,128)(2,1)S(1)} %bitcast.4), channel_id=1, source_target_pairs={{0,16},{16,0},{32,48},{48,32},{64,80},{80,64},{96,112},{112,96},{1... | collective-permute-start | bytes 2752520 | tf_op jit(solution)/shard_map/ppermute | solution.py:568

commit v4 on v3

--- a/solution.py
+++ b/solution.py
@@ -20,7 +20,8 @@
 
 def trade(axis, near, far):
     first, second = swaps(axis)
-    return lax.ppermute(near, axis, first), lax.ppermute(far, axis, second)
+    far = lax.ppermute(far, axis, second)
+    return lax.ppermute(near, axis, first), far
 
 
 def is_odd(axis):
@@ -557,6 +558,7 @@
     got, grad_input = lax.optimization_barrier((got, grad_input))
     chip_sum = (keep.astype(F32) + got.astype(F32)).astype(BF)
     cores = [[c for c in range(devices) if (c // lax.axis_size("wa")) % 2 == k] for k in range(2)]
+    cores = [group[::-1] for group in cores]
 
     def spread_out(value):
         return lax.all_to_all(

time: 84.6 us -> 81.7 us (0.966)
  blocking collectives: 48.1 us -> 45.8 us
    all_to_all x2, blocking collectives: 48.1 us -> 45.8 us  [spread_out(): lax.all_to_all(value.reshape(chips, share, chans), BOTH, 0, 0, axis_index...]
where the time goes in v4:
time: 81.7 us; the launch traced here: 81.5 us
  blocking collectives  45.8 us (56%)
  Pallas kernels  18 us (22%)
  starting transfers between devices  14.4 us (18%)
  waiting for transfers between devices  1.65 us (2%)
  between operations  1.08 us (1%)
    all_to_all x2, blocking collectives, spread_out(): lax.all_to_all(value.reshape(chips, share, chans), BOTH, 0, 0, axis_index...  45.8 us
    pallas_call x9, Pallas kernels, call(): pl.pallas_call(body, out_shape=tuple(out_shape), cost_estimate=pl.CostEst...  18 us
    ppermute x3, starting transfers between devices, trade(): far = lax.ppermute(far, axis, second)  8.18 us
    ppermute x3, starting transfers between devices, trade(): return (lax.ppermute(near, axis, first), far)  3.24 us
    ppermute x1, starting transfers between devices, per_device(): other = lax.ppermute(one, 'ha', pairs)  2.68 us
  transfers between devices with their start and end apart: 8, of which 2 were waited for; matrix products, arithmetic and copies ran while one was open for 0% of the time, Pallas kernels for 10%

profile of v4, /device:TPU:1, one launch (start us, length us, event | category | flops | bytes accessed | tf_op | source)
XLA Modules:
  0.0 81.5 jit_solution(9171155005709413800)
XLA Ops:
  0.6 0.0 copy-start.9
  0.6 0.0 copy-start.8
  0.7 0.0 copy-start.7
  0.7 0.0 copy-start.6
  0.7 0.0 copy-start.1
  0.7 0.0 copy-start
  0.7 1.8 %pack.1 = (bf16[6,4,40,128]{3,2,1,0:T(8,128)(2,1)S(1)}, bf16[6,4,40,128]{3,2,1,0:T(8,128)(2,1)S(1)}, bf16[720,128]{1,0:T(8,128)(2,1)S(1)}, bf16[720,128]{1,0:T(8,128)(2,1)S(1)}) custom-call(bf16[2,30,40,128]{3,2,1,0:T(8,128)(2,1)} %refs_0_.7, bf16[1,30,40,128]{3,2,1,0:T(8,128)(2,1)} %refs_1_.7, bf16[2,30,40,128]{3,2,1,0:T(8,128)(2,1)} %refs_2_.7, ...), custom_call_target="tpu_custom_call" | custom-call | flops 1000000000 | bytes 8000000 | tf_op jit(solution)/shard_map/pack/pallas_call | solution.py:477
  2.5 2.1 %collective-permute-start = (bf16[720,128]{1,0:T(8,128)(2,1)S(1)}, bf16[720,128]{1,0:T(8,128)(2,1)S(1)}, u32[]{:S(2)}, u32[]{:S(2)}) collective-permute-start(bf16[720,128]{1,0:T(8,128)(2,1)S(1)} %get-tuple-element.30), channel_id=1, source_target_pairs={{0,1},{1,0},{2,3},{3,2},{4,5},{5,4},{6,7},{7,6},{8,9},{9,8},{10,11... | collective-permute-start | bytes 552968 | tf_op jit(solution)/shard_map/ppermute | solution.py:24
  4.6 0.7 collective-permute-start.1
  5.3 1.0 %collective-permute-start.2 = (bf16[6,4,40,128]{3,2,1,0:T(8,128)(2,1)S(1)}, bf16[6,4,40,128]{3,2,1,0:T(8,128)(2,1)S(1)}, u32[]{:S(2)}, u32[]{:S(2)}) collective-permute-start(bf16[6,4,40,128]{3,2,1,0:T(8,128)(2,1)S(1)} %get-tuple-element.42), channel_id=1, source_target_pairs={{0,16},{16,0},{32,48},{48,32},{64,80},{80,64},{96,112},{112,96},{1... | collective-permute-start | bytes 737288 | tf_op jit(solution)/shard_map/ppermute | solution.py:24
  6.3 0.0 copy-start.2
  6.3 0.0 copy-start.3
  6.3 0.0 copy-start.4
  6.3 3.6 %collective-permute-start.3 = (bf16[6,4,40,128]{3,2,1,0:T(8,128)(2,1)S(1)}, bf16[6,4,40,128]{3,2,1,0:T(8,128)(2,1)S(1)}, u32[]{:S(2)}, u32[]{:S(2)}) collective-permute-start(bf16[6,4,40,128]{3,2,1,0:T(8,128)(2,1)S(1)} %get-tuple-element.43), channel_id=1, source_target_pairs={{16,32},{32,16},{48,64},{64,48},{80,96},{96,80},{17,33},{33,17},{4... | collective-permute-start | bytes 737288 | tf_op jit(solution)/shard_map/ppermute | solution.py:23
  9.9 0.0 copy-done.9
  9.9 0.0 copy-done.8
  9.9 0.0 copy-done.7
  9.9 0.0 copy-done.6
  10.0 0.0 copy-done.1
  10.0 0.0 copy-done
  10.0 0.4 ready.1
  10.3 0.0 copy-done.2
  10.3 0.0 copy-done.3
  10.4 0.0 copy-done.4
  10.4 0.0 copy-start.5
  10.4 2.9 %own.1 = (f32[28,48,128]{2,1,0:T(8,128)S(1)}, f32[26,48,128]{2,1,0:T(8,128)S(1)}) custom-call(bf16[2,30,40,128]{3,2,1,0:T(8,128)(2,1)S(1)} %copy-done.2, bf16[1,30,40,128]{3,2,1,0:T(8,128)(2,1)S(1)} %copy-done.4, bf16[2,30,40,128]{3,2,1,0:T(8,128)(2,1)S(1)} %copy-done.3, bf16[1152,384]{1,0:T(8,128)(2,1)S(1)} %get-tuple-element.32.refs_3_.refs_8_.refs_9_, ...), custom_call_target="tpu_custom_call" | custom-call | flops 4000000000 | bytes 8000000 | tf_op jit(solution)/shard_map/own/pallas_call | solution.py:477
  13.3 0.0 collective-permute-done.refs_4_.refs_0_
  13.3 0.0 collective-permute-done.1.refs_5_.refs_1_
  13.4 0.1 collective-permute-start.4
  13.5 3.9 %collective-permute-start.5 = (bf16[192,128]{1,0:T(8,128)(2,1)S(1)}, bf16[192,128]{1,0:T(8,128)(2,1)S(1)}, u32[]{:S(2)}, u32[]{:S(2)}) collective-permute-start(bf16[192,128]{1,0:T(8,128)(2,1)S(1)} %get-tuple-element.45), channel_id=1, source_target_pairs={{16,32},{32,16},{48,64},{64,48},{80,96},{96,80},{17,33},{33,17},{4... | collective-permute-start | bytes 147464 | tf_op jit(solution)/shard_map/ppermute | solution.py:23
  17.4 0.0 copy-done.5
  17.4 2.2 %middle.1 = (bf16[6,30,48,128]{3,2,1,0:T(8,128)(2,1)S(1)}, f32[28,48,128]{2,1,0:T(8,128)S(1)}, bf16[28,48,128]{2,1,0:T(8,128)(2,1)S(1)}, bf16[26,48,128]{2,1,0:T(8,128)(2,1)S(1)}, bf16[26,48,384]{2,1,0:T(8,128)(2,1)S(1)}) custom-call(bf16[2,30,40,128]{3,2,1,0:T(8,128)(2,1)S(1)} %copy-done.2, bf16[1,30,40,128]{3,2,1,0:T(8,128)(2,1)S(1)} %copy-done.4, ...), custom_call_target="tpu_custom_call" | custom-call | flops 3000000000 | bytes 8000000 | tf_op jit(solution)/shard_map/middle/pallas_call | solution.py:477
  19.6 0.0 collective-permute-done.4.refs_7_
  19.6 0.0 collective-permute-done.5.refs_8_
  19.6 0.0 collective-permute-done.2.refs_5_
  19.6 0.0 collective-permute-done.3.refs_6_
  19.6 6.6 %rim.1 = (bf16[3584,128]{1,0:T(8,128)(2,1)S(1)}, bf16[3584,128]{1,0:T(8,128)(2,1)S(1)}, bf16[32,48,128]{2,1,0:T(8,128)(2,1)S(1)}) custom-call(bf16[6,30,48,128]{3,2,1,0:T(8,128)(2,1)S(1)} %get-tuple-element.37.refs_0_, f32[28,48,128]{2,1,0:T(8,128)S(1)} %get-tuple-element.38.refs_1_, bf16[28,48,128]{2,1,0:T(8,128)(2,1)S(1)} %get-tuple-element.39.refs_2_, ...), custom_call_target="tpu_custom_call" | custom-call | flops 5000000000 | bytes 8000000 | tf_op jit(solution)/shard_map/rim/pallas_call | solution.py:477
  26.2 0.3 collective-permute-start.6
  26.5 1.7 %input.1 = bf16[1,30,40,128]{3,2,1,0:T(8,128)(2,1)} custom-call(bf16[32,48,128]{2,1,0:T(8,128)(2,1)S(1)} %get-tuple-element.48.refs_0_, bf16[384,384]{1,0:T(8,128)(2,1)S(1)} %get-tuple-element.49.refs_1_), custom_call_target="tpu_custom_call" | custom-call | flops 1000000000 | bytes 8000000 | tf_op jit(solution)/shard_map/input/pallas_call | solution.py:477
  28.2 0.8 collective-permute-done.6
  29.0 0.2 add_convert_fusion
  29.2 25.5 %all_to_all.10 = bf16[64,56,128]{2,1,0:T(8,128)(2,1)S(1)} all-to-all(bf16[64,56,128]{2,1,0:T(8,128)(2,1)S(1)} %bitcast.6), channel_id=1, replica_groups={{111,110,109,108,107,106,105,104,103,102,101,100,99,98,97,96,79,78,77,7..., dimensions={0} | all-to-all | bytes 1835008 | tf_op jit(solution)/shard_map/all_to_all | solution.py:564
  54.7 0.2 convert_reduce_fusion
  54.9 0.1 broadcast_in_dim.2
  55.0 20.3 %all_to_all.11 = bf16[64,56,128]{2,1,0:T(8,128)(2,1)S(1)} all-to-all(bf16[64,56,128]{2,1,0:T(8,128)(2,1)S(1)} %broadcast_in_dim.2), channel_id=1, replica_groups={{111,110,109,108,107,106,105,104,103,102,101,100,99,98,97,96,79,78,77,7..., dimensions={0} | all-to-all | bytes 1835008 | tf_op jit(solution)/shard_map/all_to_all | solution.py:564
  75.3 2.7 %collective-permute-start.7 = (bf16[3584,128]{1,0:T(8,128)(2,1)S(1)}, bf16[3584,128]{1,0:T(8,128)(2,1)S(1)}, u32[]{:S(2)}, u32[]{:S(2)}) collective-permute-start(bf16[3584,128]{1,0:T(8,128)(2,1)S(1)} %bitcast.4), channel_id=1, source_target_pairs={{0,16},{16,0},{32,48},{48,32},{64,80},{80,64},{96,112},{112,96},{1... | collective-permute-start | bytes 2752520 | tf_op jit(solution)/shard_map/ppermute | solution.py:570
  77.9 1.3 %place.2 = (f32[3456,128]{1,0:T(8,128)}, f32[3456,128]{1,0:T(8,128)}) custom-call(bf16[3584,128]{1,0:T(8,128)(2,1)S(1)} %bitcast.5), custom_call_target="tpu_custom_call" | custom-call | flops 2000000000 | bytes 8000000 | tf_op jit(solution)/shard_map/place/pallas_call | solution.py:477
  79.2 0.8 %collective-permute-done.7.refs_0_ = bf16[3584,128]{1,0:T(8,128)(2,1)S(1)} collective-permute-done((bf16[3584,128]{1,0:T(8,128)(2,1)S(1)}, bf16[3584,128]{1,0:T(8,128)(2,1)S(1)}, u32[]{:S(2)}, u32[]{:S(2)}) %collective-permute-start.7) | collective-permute-done | bytes 917536 | tf_op jit(solution)/shard_map/ppermute | solution.py:570
  80.0 1.3 %place.3 = (f32[3456,128]{1,0:T(8,128)}, f32[3456,128]{1,0:T(8,128)}) custom-call(bf16[3584,128]{1,0:T(8,128)(2,1)S(1)} %collective-permute-done.7.refs_0_, f32[3456,128]{1,0:T(8,128)} %get-tuple-element.53.refs_1_, f32[3456,128]{1,0:T(8,128)} %get-tuple-element.54.refs_2_), custom_call_target="tpu_custom_call", output_to_operand_aliasing={{0}: (1, {}), {1}: (2, {})} | custom-call | flops 2000000000 | bytes 8000000 | tf_op jit(solution)/shard_map/place/pallas_call | solution.py:477
  (2 shorter events, 0.0 us)
Async XLA Ops:
  0.6 9.3 %copy-start.9 = (f32[1,128]{1,0:T(1,128)S(1)}, f32[1,128]{1,0:T(1,128)}, u32[]{:S(2)}) copy-start(f32[1,128]{1,0:T(1,128)} %refs_5_.1) | copy-start | bytes 1540
  0.6 9.3 %copy-start.8 = (f32[1,128]{1,0:T(1,128)S(1)}, f32[1,128]{1,0:T(1,128)}, u32[]{:S(2)}) copy-start(f32[1,128]{1,0:T(1,128)} %refs_4_.1) | copy-start | bytes 1540
  0.7 9.3 %copy-start.7 = (f32[1,128]{1,0:T(1,128)S(1)}, f32[1,128]{1,0:T(1,128)}, u32[]{:S(2)}) copy-start(f32[1,128]{1,0:T(1,128)} %refs_3_.4) | copy-start | bytes 1540
  0.7 9.3 %copy-start.6 = (f32[1,128]{1,0:T(1,128)S(1)}, f32[1,128]{1,0:T(1,128)}, u32[]{:S(2)}) copy-start(f32[1,128]{1,0:T(1,128)} %refs_2_.5) | copy-start | bytes 1540
  0.7 9.3 %copy-start.1 = (bf16[3,3,3,128,128]{4,3,2,1,0:T(8,128)(2,1)S(1)}, bf16[3,3,3,128,128]{4,3,2,1,0:T(8,128)(2,1)}, u32[]{:S(2)}) copy-start(bf16[3,3,3,128,128]{4,3,2,1,0:T(8,128)(2,1)} %refs_1_.5) | copy-start | bytes 2654212
  0.7 9.3 %copy-start = (bf16[3,3,3,128,128]{4,3,2,1,0:T(8,128)(2,1)S(1)}, bf16[3,3,3,128,128]{4,3,2,1,0:T(8,128)(2,1)}, u32[]{:S(2)}) copy-start(bf16[3,3,3,128,128]{4,3,2,1,0:T(8,128)(2,1)} %refs_0_.5) | copy-start | bytes 2654212
  2.5 10.9 %collective-permute-start = (bf16[720,128]{1,0:T(8,128)(2,1)S(1)}, bf16[720,128]{1,0:T(8,128)(2,1)S(1)}, u32[]{:S(2)}, u32[]{:S(2)}) collective-permute-start(bf16[720,128]{1,0:T(8,128)(2,1)S(1)} %get-tuple-element.30), channel_id=1, source_target_pairs={{0,1},{1,0},{2,3},{3,2},{4,5},{5,4},{6,7},{7,6},{8,9},{9,8},{10,11... | collective-permute-start | bytes 552968 | tf_op jit(solution)/shard_map/ppermute | solution.py:24
  4.6 8.8 %collective-permute-start.1 = (bf16[720,128]{1,0:T(8,128)(2,1)S(1)}, bf16[720,128]{1,0:T(8,128)(2,1)S(1)}, u32[]{:S(2)}, u32[]{:S(2)}) collective-permute-start(bf16[720,128]{1,0:T(8,128)(2,1)S(1)} %get-tuple-element.31), channel_id=1, source_target_pairs={{1,2},{2,1},{3,4},{4,3},{5,6},{6,5},{7,8},{8,7},{9,10},{10,9},{11,... | collective-permute-start | bytes 552968 | tf_op jit(solution)/shard_map/ppermute | solution.py:23
  5.3 14.3 %collective-permute-start.2 = (bf16[6,4,40,128]{3,2,1,0:T(8,128)(2,1)S(1)}, bf16[6,4,40,128]{3,2,1,0:T(8,128)(2,1)S(1)}, u32[]{:S(2)}, u32[]{:S(2)}) collective-permute-start(bf16[6,4,40,128]{3,2,1,0:T(8,128)(2,1)S(1)} %get-tuple-element.42), channel_id=1, source_target_pairs={{0,16},{16,0},{32,48},{48,32},{64,80},{80,64},{96,112},{112,96},{1... | collective-permute-start | bytes 737288 | tf_op jit(solution)/shard_map/ppermute | solution.py:24
  6.3 4.0 %copy-start.2 = (bf16[2,30,40,128]{3,2,1,0:T(8,128)(2,1)S(1)}, bf16[2,30,40,128]{3,2,1,0:T(8,128)(2,1)}, u32[]{:S(2)}) copy-start(bf16[2,30,40,128]{3,2,1,0:T(8,128)(2,1)} %refs_0_.7) | copy-start | bytes 1843204
  6.3 4.1 %copy-start.3 = (bf16[2,30,40,128]{3,2,1,0:T(8,128)(2,1)S(1)}, bf16[2,30,40,128]{3,2,1,0:T(8,128)(2,1)}, u32[]{:S(2)}) copy-start(bf16[2,30,40,128]{3,2,1,0:T(8,128)(2,1)} %refs_2_.7) | copy-start | bytes 1843204
  6.3 4.1 %copy-start.4 = (bf16[1,30,40,128]{3,2,1,0:T(8,128)(2,1)S(1)}, bf16[1,30,40,128]{3,2,1,0:T(8,128)(2,1)}, u32[]{:S(2)}) copy-start(bf16[1,30,40,128]{3,2,1,0:T(8,128)(2,1)} %refs_1_.7) | copy-start | bytes 921604
  6.3 13.3 %collective-permute-start.3 = (bf16[6,4,40,128]{3,2,1,0:T(8,128)(2,1)S(1)}, bf16[6,4,40,128]{3,2,1,0:T(8,128)(2,1)S(1)}, u32[]{:S(2)}, u32[]{:S(2)}) collective-permute-start(bf16[6,4,40,128]{3,2,1,0:T(8,128)(2,1)S(1)} %get-tuple-element.43), channel_id=1, source_target_pairs={{16,32},{32,16},{48,64},{64,48},{80,96},{96,80},{17,33},{33,17},{4... | collective-permute-start | bytes 737288 | tf_op jit(solution)/shard_map/ppermute | solution.py:23
  10.4 7.0 %copy-start.5 = (bf16[1,30,40,128]{3,2,1,0:T(8,128)(2,1)S(1)}, bf16[1,30,40,128]{3,2,1,0:T(8,128)(2,1)}, u32[]{:S(2)}) copy-start(bf16[1,30,40,128]{3,2,1,0:T(8,128)(2,1)} %refs_3_.5) | copy-start | bytes 921604
  13.4 6.2 %collective-permute-start.4 = (bf16[192,128]{1,0:T(8,128)(2,1)S(1)}, bf16[192,128]{1,0:T(8,128)(2,1)S(1)}, u32[]{:S(2)}, u32[]{:S(2)}) collective-permute-start(bf16[192,128]{1,0:T(8,128)(2,1)S(1)} %get-tuple-element.44), channel_id=1, source_target_pairs={{0,16},{16,0},{32,48},{48,32},{64,80},{80,64},{96,112},{112,96},{1... | collective-permute-start | bytes 147464 | tf_op jit(solution)/shard_map/ppermute | solution.py:24
  13.5 6.1 %collective-permute-start.5 = (bf16[192,128]{1,0:T(8,128)(2,1)S(1)}, bf16[192,128]{1,0:T(8,128)(2,1)S(1)}, u32[]{:S(2)}, u32[]{:S(2)}) collective-permute-start(bf16[192,128]{1,0:T(8,128)(2,1)S(1)} %get-tuple-element.45), channel_id=1, source_target_pairs={{16,32},{32,16},{48,64},{64,48},{80,96},{96,80},{17,33},{33,17},{4... | collective-permute-start | bytes 147464 | tf_op jit(solution)/shard_map/ppermute | solution.py:23
  26.2 2.7 %collective-permute-start.6 = (bf16[3584,128]{1,0:T(8,128)(2,1)S(1)}, bf16[3584,128]{1,0:T(8,128)(2,1)S(1)}, u32[]{:S(2)}, u32[]{:S(2)}) collective-permute-start(bf16[3584,128]{1,0:T(8,128)(2,1)S(1)} %get-tuple-element.47), channel_id=1, source_target_pairs={{0,16},{16,0},{32,48},{48,32},{64,80},{80,64},{96,112},{112,96},{1... | collective-permute-start | bytes 2752520 | tf_op jit(solution)/shard_map/ppermute | solution.py:554
  75.3 4.8 %collective-permute-start.7 = (bf16[3584,128]{1,0:T(8,128)(2,1)S(1)}, bf16[3584,128]{1,0:T(8,128)(2,1)S(1)}, u32[]{:S(2)}, u32[]{:S(2)}) collective-permute-start(bf16[3584,128]{1,0:T(8,128)(2,1)S(1)} %bitcast.4), channel_id=1, source_target_pairs={{0,16},{16,0},{32,48},{48,32},{64,80},{80,64},{96,112},{112,96},{1... | collective-permute-start | bytes 2752520 | tf_op jit(solution)/shard_map/ppermute | solution.py:570

commit v5 on v4

--- a/solution.py
+++ b/solution.py
@@ -269,46 +269,38 @@
     )
 
 
-def own_kernel(
-    rows, cols, cache_in, frames_in, cache_mid, ahead_one, ahead_two, part_one, part_two, field
-):
-    block = [cache_in[0], cache_in[1], frames_in[0], cache_mid[0], cache_mid[1]]
+def own_kernel(rows, cols, cache_in, frames_in, ahead_one, part_one, field):
+    block = [cache_in[0], cache_in[1], frames_in[0]]
     none = jnp.zeros((rows, 2 * RIM, block[0].shape[-1]), F32)
     for i, value in enumerate(block):
         field[i] = jnp.concatenate([value.astype(F32), none], axis=1).astype(BF)
-    own = [Rows((RIM, Frame(field, i), rows)) for i in range(5)]
-    split = 6 * none.shape[-1]
-    for frames, weight, part, first in (
-        (own[:3], ahead_one[...], part_one, RIM + 1),
-        (own[3:], ahead_two[:split], part_two, RIM + 2),
-    ):
-        for start, count in cut(first, 2 * RIM + rows - first, 2):
-            part[start - first : start - first + count] = forward(frames, weight, [(start, count)])
+    own = [Rows((RIM, Frame(field, i), rows)) for i in range(3)]
+    first = RIM + 1
+    for start, count in cut(first, RIM + rows - 1, 2):
+        part_one[start - first : start - first + count] = forward(
+            own, ahead_one[...], [(start, count)]
+        )
 
 
 def middle_kernel(
-    rows, cols, cache_in, frames_in, cache_mid, cot, col_near, col_far, part_one, part_two,
+    rows, cols, cache_in, frames_in, cache_mid, cot, col_near, col_far, part_one,
     ahead_one, ahead_two, affine, field, slope_mid, a_mid, d_mid, moved_mid,
 ):
     block = [cache_in[0], cache_in[1], frames_in[0], cache_mid[0], cache_mid[1], cot[0]]
     frames, rims = join(block, col_near[...], col_far[...])
     for frame, value in enumerate(frames):
         field[frame] = value
-    split = 6 * affine.shape[-1]
     first = RIM + 1
     for start, count in cut(first, RIM + rows - 1, 2):
         at = slice(start - first, start - first + count)
         conv = part_one[at] + rim_forward(rims[:3], ahead_one[...], start, count, cols)
         a_mid[at], slope_mid[at] = first_layer(rows, cols, conv, affine, [(start, count)])
-    a_one, cotangent = Rows((first, a_mid, rows - 2)), Rows((RIM, Frame(field, 5), rows))
+    frames = [Rows((RIM, Frame(field, i), rows)) for i in (3, 4)] + [Rows((first, a_mid, rows - 2))]
+    cotangent = Rows((RIM, Frame(field, 5), rows))
     second = RIM + 2
     for start, count in cut(second, RIM + rows - 2, 2):
         at = slice(start - second, start - second + count)
-        conv = (
-            part_two[at]
-            + forward([a_one], ahead_two[split:], [(start, count)])
-            + rim_forward(rims[3:5], ahead_two[:split], start, count, cols)
-        )
+        conv = forward(frames, ahead_two[...], [(start, count)])
         value = second_layer(conv, cotangent, affine, [(start, count)])
         d_mid[at] = value.astype(BF)
         moved_mid[at] = spread(cols, value)
@@ -497,14 +489,10 @@
         ready_kernel, "ready", (ahead, ahead, back, back, shaped(8, chans, dtype=F32)), 10, 2e9,
         (w_first, w_second, scale_first, shift_first, scale_second, shift_second), sizes=False,
     )
-    part_one, part_two = call(
-        own_kernel, "own",
-        (
-            shaped(rows - 2, full, chans, dtype=F32),
-            shaped(rows - 4, full, chans, dtype=F32),
-        ),
-        12, 4e9, (cache_in, frames_in, cache_mid, ahead_one, ahead_two),
-        scratch_shapes=[pltpu.VMEM((5, rows, full, chans), BF)],
+    (part_one,) = call(
+        own_kernel, "own", (shaped(rows - 2, full, chans, dtype=F32),),
+        12, 3e9, (cache_in, frames_in, ahead_one),
+        scratch_shapes=[pltpu.VMEM((3, rows, full, chans), BF)],
     )
     col_near, col_far = trade("wa", col_near, col_far)
     row_near, row_far = trade("ha", row_near, row_far)
@@ -526,7 +514,7 @@
             shaped(rows - 4, full, chans),
             shaped(rows - 4, full, 3 * chans),
         ),
-        16, 3e9, (*fields, col_near, col_far, part_one, part_two, ahead_one, ahead_two, affine),
+        16, 3e9, (*fields, col_near, col_far, part_one, ahead_one, ahead_two, affine),
     )
     keep, send, d_one = call(
         rim_kernel, "rim",

time: 81.7 us -> 81.1 us (level)
  no operation moved by 1% of the time
where the time goes in v5:
time: 81.1 us; the launch traced here: 80.9 us
  blocking collectives  45.9 us (57%)
  Pallas kernels  17.5 us (22%)
  starting transfers between devices  14.2 us (18%)
  waiting for transfers between devices  1.65 us (2%)
  between operations  1.09 us (1%)
    all_to_all x2, blocking collectives, spread_out(): lax.all_to_all(value.reshape(chips, share, chans), BOTH, 0, 0, axis_index...  45.9 us
    pallas_call x9, Pallas kernels, call(): pl.pallas_call(body, out_shape=tuple(out_shape), cost_estimate=pl.CostEst...  17.5 us
    ppermute x3, starting transfers between devices, trade(): far = lax.ppermute(far, axis, second)  8.18 us
    ppermute x3, starting transfers between devices, trade(): return (lax.ppermute(near, axis, first), far)  3.24 us
    ppermute x1, starting transfers between devices, per_device(): other = lax.ppermute(one, 'ha', pairs)  2.68 us
  transfers between devices with their start and end apart: 8, of which 2 were waited for; matrix products, arithmetic and copies ran while one was open for 0% of the time, Pallas kernels for 10%

profile of v5, /device:TPU:1, one launch (start us, length us, event | category | flops | bytes accessed | tf_op | source)
XLA Modules:
  0.0 80.9 jit_solution(7015555904643197264)
XLA Ops:
  0.6 0.0 copy-start.9
  0.6 0.0 copy-start.8
  0.7 0.0 copy-start.7
  0.7 0.0 copy-start.6
  0.7 0.0 copy-start.1
  0.7 0.0 copy-start
  0.7 1.8 %pack.1 = (bf16[6,4,40,128]{3,2,1,0:T(8,128)(2,1)S(1)}, bf16[6,4,40,128]{3,2,1,0:T(8,128)(2,1)S(1)}, bf16[720,128]{1,0:T(8,128)(2,1)S(1)}, bf16[720,128]{1,0:T(8,128)(2,1)S(1)}) custom-call(bf16[2,30,40,128]{3,2,1,0:T(8,128)(2,1)} %refs_0_.7, bf16[1,30,40,128]{3,2,1,0:T(8,128)(2,1)} %refs_1_.7, bf16[2,30,40,128]{3,2,1,0:T(8,128)(2,1)} %refs_2_.5, ...), custom_call_target="tpu_custom_call" | custom-call | flops 1000000000 | bytes 8000000 | tf_op jit(solution)/shard_map/pack/pallas_call | solution.py:469
  2.5 2.1 %collective-permute-start = (bf16[720,128]{1,0:T(8,128)(2,1)S(1)}, bf16[720,128]{1,0:T(8,128)(2,1)S(1)}, u32[]{:S(2)}, u32[]{:S(2)}) collective-permute-start(bf16[720,128]{1,0:T(8,128)(2,1)S(1)} %get-tuple-element.28), channel_id=1, source_target_pairs={{0,1},{1,0},{2,3},{3,2},{4,5},{5,4},{6,7},{7,6},{8,9},{9,8},{10,11... | collective-permute-start | bytes 552968 | tf_op jit(solution)/shard_map/ppermute | solution.py:24
  4.6 0.7 collective-permute-start.1
  5.3 1.0 %collective-permute-start.2 = (bf16[6,4,40,128]{3,2,1,0:T(8,128)(2,1)S(1)}, bf16[6,4,40,128]{3,2,1,0:T(8,128)(2,1)S(1)}, u32[]{:S(2)}, u32[]{:S(2)}) collective-permute-start(bf16[6,4,40,128]{3,2,1,0:T(8,128)(2,1)S(1)} %get-tuple-element.38), channel_id=1, source_target_pairs={{0,16},{16,0},{32,48},{48,32},{64,80},{80,64},{96,112},{112,96},{1... | collective-permute-start | bytes 737288 | tf_op jit(solution)/shard_map/ppermute | solution.py:24
  6.3 0.0 copy-start.2
  6.3 0.0 copy-start.4
  6.3 3.6 %collective-permute-start.3 = (bf16[6,4,40,128]{3,2,1,0:T(8,128)(2,1)S(1)}, bf16[6,4,40,128]{3,2,1,0:T(8,128)(2,1)S(1)}, u32[]{:S(2)}, u32[]{:S(2)}) collective-permute-start(bf16[6,4,40,128]{3,2,1,0:T(8,128)(2,1)S(1)} %get-tuple-element.39), channel_id=1, source_target_pairs={{16,32},{32,16},{48,64},{64,48},{80,96},{96,80},{17,33},{33,17},{4... | collective-permute-start | bytes 737288 | tf_op jit(solution)/shard_map/ppermute | solution.py:23
  9.9 0.0 copy-done.9
  9.9 0.0 copy-done.8
  9.9 0.0 copy-done.7
  9.9 0.0 copy-done.6
  9.9 0.0 copy-done.1
  10.0 0.0 copy-done
  10.0 0.4 ready.1
  10.3 0.0 copy-done.2
  10.3 0.0 copy-done.4
  10.3 0.0 copy-start.3
  10.4 0.0 copy-start.5
  10.4 1.9 %own.1.refs_6_ = f32[28,48,128]{2,1,0:T(8,128)S(1)} custom-call(bf16[2,30,40,128]{3,2,1,0:T(8,128)(2,1)S(1)} %copy-done.2, bf16[1,30,40,128]{3,2,1,0:T(8,128)(2,1)S(1)} %copy-done.4, bf16[1152,384]{1,0:T(8,128)(2,1)S(1)} %get-tuple-element.30.refs_2_.refs_7_.refs_9_), custom_call_target="tpu_custom_call" | custom-call | flops 3000000000 | bytes 8000000 | tf_op jit(solution)/shard_map/own/pallas_call | solution.py:469
  12.3 0.0 collective-permute-done.refs_4_.refs_0_
  12.3 0.0 collective-permute-done.1.refs_5_.refs_1_
  12.4 0.1 collective-permute-start.4
  12.4 3.9 %collective-permute-start.5 = (bf16[192,128]{1,0:T(8,128)(2,1)S(1)}, bf16[192,128]{1,0:T(8,128)(2,1)S(1)}, u32[]{:S(2)}, u32[]{:S(2)}) collective-permute-start(bf16[192,128]{1,0:T(8,128)(2,1)S(1)} %get-tuple-element.41), channel_id=1, source_target_pairs={{16,32},{32,16},{48,64},{64,48},{80,96},{96,80},{17,33},{33,17},{4... | collective-permute-start | bytes 147464 | tf_op jit(solution)/shard_map/ppermute | solution.py:23
  16.4 0.0 copy-done.3
  16.4 0.0 copy-done.5
  16.4 2.6 %middle.1 = (bf16[6,30,48,128]{3,2,1,0:T(8,128)(2,1)S(1)}, f32[28,48,128]{2,1,0:T(8,128)S(1)}, bf16[28,48,128]{2,1,0:T(8,128)(2,1)S(1)}, bf16[26,48,128]{2,1,0:T(8,128)(2,1)S(1)}, bf16[26,48,384]{2,1,0:T(8,128)(2,1)S(1)}) custom-call(bf16[2,30,40,128]{3,2,1,0:T(8,128)(2,1)S(1)} %copy-done.2, bf16[1,30,40,128]{3,2,1,0:T(8,128)(2,1)S(1)} %copy-done.4, ...), custom_call_target="tpu_custom_call" | custom-call | flops 3000000000 | bytes 8000000 | tf_op jit(solution)/shard_map/middle/pallas_call | solution.py:469
  19.0 0.0 collective-permute-done.4.refs_7_
  19.0 0.0 collective-permute-done.5.refs_8_
  19.0 0.0 collective-permute-done.2.refs_5_
  19.0 0.0 collective-permute-done.3.refs_6_
  19.0 6.6 %rim.1 = (bf16[3584,128]{1,0:T(8,128)(2,1)S(1)}, bf16[3584,128]{1,0:T(8,128)(2,1)S(1)}, bf16[32,48,128]{2,1,0:T(8,128)(2,1)S(1)}) custom-call(bf16[6,30,48,128]{3,2,1,0:T(8,128)(2,1)S(1)} %get-tuple-element.33.refs_0_, f32[28,48,128]{2,1,0:T(8,128)S(1)} %get-tuple-element.34.refs_1_, bf16[28,48,128]{2,1,0:T(8,128)(2,1)S(1)} %get-tuple-element.35.refs_2_, ...), custom_call_target="tpu_custom_call" | custom-call | flops 5000000000 | bytes 8000000 | tf_op jit(solution)/shard_map/rim/pallas_call | solution.py:469
  25.7 0.1 collective-permute-start.6
  25.8 1.7 %input.1 = bf16[1,30,40,128]{3,2,1,0:T(8,128)(2,1)} custom-call(bf16[32,48,128]{2,1,0:T(8,128)(2,1)S(1)} %get-tuple-element.44.refs_0_, bf16[384,384]{1,0:T(8,128)(2,1)S(1)} %get-tuple-element.45.refs_1_), custom_call_target="tpu_custom_call" | custom-call | flops 1000000000 | bytes 8000000 | tf_op jit(solution)/shard_map/input/pallas_call | solution.py:469
  27.4 0.8 collective-permute-done.6
  28.2 0.2 add_convert_fusion
  28.5 25.6 %all_to_all.10 = bf16[64,56,128]{2,1,0:T(8,128)(2,1)S(1)} all-to-all(bf16[64,56,128]{2,1,0:T(8,128)(2,1)S(1)} %bitcast.6), channel_id=1, replica_groups={{111,110,109,108,107,106,105,104,103,102,101,100,99,98,97,96,79,78,77,7..., dimensions={0} | all-to-all | bytes 1835008 | tf_op jit(solution)/shard_map/all_to_all | solution.py:552
  54.1 0.2 convert_reduce_fusion
  54.3 0.1 broadcast_in_dim.2
  54.4 20.3 %all_to_all.11 = bf16[64,56,128]{2,1,0:T(8,128)(2,1)S(1)} all-to-all(bf16[64,56,128]{2,1,0:T(8,128)(2,1)S(1)} %broadcast_in_dim.2), channel_id=1, replica_groups={{111,110,109,108,107,106,105,104,103,102,101,100,99,98,97,96,79,78,77,7..., dimensions={0} | all-to-all | bytes 1835008 | tf_op jit(solution)/shard_map/all_to_all | solution.py:552
  74.7 2.7 %collective-permute-start.7 = (bf16[3584,128]{1,0:T(8,128)(2,1)S(1)}, bf16[3584,128]{1,0:T(8,128)(2,1)S(1)}, u32[]{:S(2)}, u32[]{:S(2)}) collective-permute-start(bf16[3584,128]{1,0:T(8,128)(2,1)S(1)} %bitcast.4), channel_id=1, source_target_pairs={{0,16},{16,0},{32,48},{48,32},{64,80},{80,64},{96,112},{112,96},{1... | collective-permute-start | bytes 2752520 | tf_op jit(solution)/shard_map/ppermute | solution.py:558
  77.4 1.3 %place.2 = (f32[3456,128]{1,0:T(8,128)}, f32[3456,128]{1,0:T(8,128)}) custom-call(bf16[3584,128]{1,0:T(8,128)(2,1)S(1)} %bitcast.5), custom_call_target="tpu_custom_call" | custom-call | flops 2000000000 | bytes 8000000 | tf_op jit(solution)/shard_map/place/pallas_call | solution.py:469
  78.6 0.8 %collective-permute-done.7.refs_0_ = bf16[3584,128]{1,0:T(8,128)(2,1)S(1)} collective-permute-done((bf16[3584,128]{1,0:T(8,128)(2,1)S(1)}, bf16[3584,128]{1,0:T(8,128)(2,1)S(1)}, u32[]{:S(2)}, u32[]{:S(2)}) %collective-permute-start.7) | collective-permute-done | bytes 917536 | tf_op jit(solution)/shard_map/ppermute | solution.py:558
  79.5 1.3 %place.3 = (f32[3456,128]{1,0:T(8,128)}, f32[3456,128]{1,0:T(8,128)}) custom-call(bf16[3584,128]{1,0:T(8,128)(2,1)S(1)} %collective-permute-done.7.refs_0_, f32[3456,128]{1,0:T(8,128)} %get-tuple-element.49.refs_1_, f32[3456,128]{1,0:T(8,128)} %get-tuple-element.50.refs_2_), custom_call_target="tpu_custom_call", output_to_operand_aliasing={{0}: (1, {}), {1}: (2, {})} | custom-call | flops 2000000000 | bytes 8000000 | tf_op jit(solution)/shard_map/place/pallas_call | solution.py:469
  (2 shorter events, 0.0 us)
Async XLA Ops:
  0.6 9.3 %copy-start.9 = (f32[1,128]{1,0:T(1,128)S(1)}, f32[1,128]{1,0:T(1,128)}, u32[]{:S(2)}) copy-start(f32[1,128]{1,0:T(1,128)} %refs_5_.1) | copy-start | bytes 1540
  0.6 9.3 %copy-start.8 = (f32[1,128]{1,0:T(1,128)S(1)}, f32[1,128]{1,0:T(1,128)}, u32[]{:S(2)}) copy-start(f32[1,128]{1,0:T(1,128)} %refs_4_.1) | copy-start | bytes 1540
  0.7 9.3 %copy-start.7 = (f32[1,128]{1,0:T(1,128)S(1)}, f32[1,128]{1,0:T(1,128)}, u32[]{:S(2)}) copy-start(f32[1,128]{1,0:T(1,128)} %refs_3_.4) | copy-start | bytes 1540
  0.7 9.3 %copy-start.6 = (f32[1,128]{1,0:T(1,128)S(1)}, f32[1,128]{1,0:T(1,128)}, u32[]{:S(2)}) copy-start(f32[1,128]{1,0:T(1,128)} %refs_2_.4) | copy-start | bytes 1540
  0.7 9.3 %copy-start.1 = (bf16[3,3,3,128,128]{4,3,2,1,0:T(8,128)(2,1)S(1)}, bf16[3,3,3,128,128]{4,3,2,1,0:T(8,128)(2,1)}, u32[]{:S(2)}) copy-start(bf16[3,3,3,128,128]{4,3,2,1,0:T(8,128)(2,1)} %refs_1_.5) | copy-start | bytes 2654212
  0.7 9.3 %copy-start = (bf16[3,3,3,128,128]{4,3,2,1,0:T(8,128)(2,1)S(1)}, bf16[3,3,3,128,128]{4,3,2,1,0:T(8,128)(2,1)}, u32[]{:S(2)}) copy-start(bf16[3,3,3,128,128]{4,3,2,1,0:T(8,128)(2,1)} %refs_0_.5) | copy-start | bytes 2654212
  2.5 9.8 %collective-permute-start = (bf16[720,128]{1,0:T(8,128)(2,1)S(1)}, bf16[720,128]{1,0:T(8,128)(2,1)S(1)}, u32[]{:S(2)}, u32[]{:S(2)}) collective-permute-start(bf16[720,128]{1,0:T(8,128)(2,1)S(1)} %get-tuple-element.28), channel_id=1, source_target_pairs={{0,1},{1,0},{2,3},{3,2},{4,5},{5,4},{6,7},{7,6},{8,9},{9,8},{10,11... | collective-permute-start | bytes 552968 | tf_op jit(solution)/shard_map/ppermute | solution.py:24
  4.6 7.7 %collective-permute-start.1 = (bf16[720,128]{1,0:T(8,128)(2,1)S(1)}, bf16[720,128]{1,0:T(8,128)(2,1)S(1)}, u32[]{:S(2)}, u32[]{:S(2)}) collective-permute-start(bf16[720,128]{1,0:T(8,128)(2,1)S(1)} %get-tuple-element.29), channel_id=1, source_target_pairs={{1,2},{2,1},{3,4},{4,3},{5,6},{6,5},{7,8},{8,7},{9,10},{10,9},{11,... | collective-permute-start | bytes 552968 | tf_op jit(solution)/shard_map/ppermute | solution.py:23
  5.3 13.8 %collective-permute-start.2 = (bf16[6,4,40,128]{3,2,1,0:T(8,128)(2,1)S(1)}, bf16[6,4,40,128]{3,2,1,0:T(8,128)(2,1)S(1)}, u32[]{:S(2)}, u32[]{:S(2)}) collective-permute-start(bf16[6,4,40,128]{3,2,1,0:T(8,128)(2,1)S(1)} %get-tuple-element.38), channel_id=1, source_target_pairs={{0,16},{16,0},{32,48},{48,32},{64,80},{80,64},{96,112},{112,96},{1... | collective-permute-start | bytes 737288 | tf_op jit(solution)/shard_map/ppermute | solution.py:24
  6.3 4.0 %copy-start.2 = (bf16[2,30,40,128]{3,2,1,0:T(8,128)(2,1)S(1)}, bf16[2,30,40,128]{3,2,1,0:T(8,128)(2,1)}, u32[]{:S(2)}) copy-start(bf16[2,30,40,128]{3,2,1,0:T(8,128)(2,1)} %refs_0_.7) | copy-start | bytes 1843204
  6.3 4.0 %copy-start.4 = (bf16[1,30,40,128]{3,2,1,0:T(8,128)(2,1)S(1)}, bf16[1,30,40,128]{3,2,1,0:T(8,128)(2,1)}, u32[]{:S(2)}) copy-start(bf16[1,30,40,128]{3,2,1,0:T(8,128)(2,1)} %refs_1_.7) | copy-start | bytes 921604
  6.3 12.7 %collective-permute-start.3 = (bf16[6,4,40,128]{3,2,1,0:T(8,128)(2,1)S(1)}, bf16[6,4,40,128]{3,2,1,0:T(8,128)(2,1)S(1)}, u32[]{:S(2)}, u32[]{:S(2)}) collective-permute-start(bf16[6,4,40,128]{3,2,1,0:T(8,128)(2,1)S(1)} %get-tuple-element.39), channel_id=1, source_target_pairs={{16,32},{32,16},{48,64},{64,48},{80,96},{96,80},{17,33},{33,17},{4... | collective-permute-start | bytes 737288 | tf_op jit(solution)/shard_map/ppermute | solution.py:23
  10.3 6.0 %copy-start.3 = (bf16[2,30,40,128]{3,2,1,0:T(8,128)(2,1)S(1)}, bf16[2,30,40,128]{3,2,1,0:T(8,128)(2,1)}, u32[]{:S(2)}) copy-start(bf16[2,30,40,128]{3,2,1,0:T(8,128)(2,1)} %refs_2_.5) | copy-start | bytes 1843204
  10.4 6.0 %copy-start.5 = (bf16[1,30,40,128]{3,2,1,0:T(8,128)(2,1)S(1)}, bf16[1,30,40,128]{3,2,1,0:T(8,128)(2,1)}, u32[]{:S(2)}) copy-start(bf16[1,30,40,128]{3,2,1,0:T(8,128)(2,1)} %refs_3_.5) | copy-start | bytes 921604
  12.4 6.7 %collective-permute-start.4 = (bf16[192,128]{1,0:T(8,128)(2,1)S(1)}, bf16[192,128]{1,0:T(8,128)(2,1)S(1)}, u32[]{:S(2)}, u32[]{:S(2)}) collective-permute-start(bf16[192,128]{1,0:T(8,128)(2,1)S(1)} %get-tuple-element.40), channel_id=1, source_target_pairs={{0,16},{16,0},{32,48},{48,32},{64,80},{80,64},{96,112},{112,96},{1... | collective-permute-start | bytes 147464 | tf_op jit(solution)/shard_map/ppermute | solution.py:24
  12.4 6.6 %collective-permute-start.5 = (bf16[192,128]{1,0:T(8,128)(2,1)S(1)}, bf16[192,128]{1,0:T(8,128)(2,1)S(1)}, u32[]{:S(2)}, u32[]{:S(2)}) collective-permute-start(bf16[192,128]{1,0:T(8,128)(2,1)S(1)} %get-tuple-element.41), channel_id=1, source_target_pairs={{16,32},{32,16},{48,64},{64,48},{80,96},{96,80},{17,33},{33,17},{4... | collective-permute-start | bytes 147464 | tf_op jit(solution)/shard_map/ppermute | solution.py:23
  25.7 2.6 %collective-permute-start.6 = (bf16[3584,128]{1,0:T(8,128)(2,1)S(1)}, bf16[3584,128]{1,0:T(8,128)(2,1)S(1)}, u32[]{:S(2)}, u32[]{:S(2)}) collective-permute-start(bf16[3584,128]{1,0:T(8,128)(2,1)S(1)} %get-tuple-element.43), channel_id=1, source_target_pairs={{0,16},{16,0},{32,48},{48,32},{64,80},{80,64},{96,112},{112,96},{1... | collective-permute-start | bytes 2752520 | tf_op jit(solution)/shard_map/ppermute | solution.py:542
  74.7 4.8 %collective-permute-start.7 = (bf16[3584,128]{1,0:T(8,128)(2,1)S(1)}, bf16[3584,128]{1,0:T(8,128)(2,1)S(1)}, u32[]{:S(2)}, u32[]{:S(2)}) collective-permute-start(bf16[3584,128]{1,0:T(8,128)(2,1)S(1)} %bitcast.4), channel_id=1, source_target_pairs={{0,16},{16,0},{32,48},{48,32},{64,80},{80,64},{96,112},{112,96},{1... | collective-permute-start | bytes 2752520 | tf_op jit(solution)/shard_map/ppermute | solution.py:558

commit v6 on v5

--- a/solution.py
+++ b/solution.py
@@ -358,15 +358,15 @@
     moved_one[rows + 2 : rows + 4] = edge
 
     def gradient(which, frames, moved):
-        lhs = jnp.concatenate([flat(frames[a].get(RIM - 1, rows + 2)) for a in range(3)], axis=1)
-        for b in range(3):
-            rhs = flat(moved.get(RIM - b, rows + 2))
+        rhs = jnp.concatenate([flat(moved.get(RIM - b, rows + 2)) for b in range(3)], axis=1)
+        for a in range(3):
+            lhs = flat(frames[a].get(RIM - 1, rows + 2))
             out = lax.dot_general(lhs, rhs, (((0,), (0,)), ((), ())), preferred_element_type=F32)
-            for a in range(3):
+            for b in range(3):
                 for c in range(3):
                     at = ((a * 3 + b) * 3 + c) * lanes
                     grads[which, at : at + lanes, :] = out[
-                        a * lanes : (a + 1) * lanes, c * lanes : (c + 1) * lanes
+                        :, (b * 3 + c) * lanes : (b * 3 + c + 1) * lanes
                     ].astype(BF)
 
         @pl.when(core == which)
@@ -495,6 +495,7 @@
         scratch_shapes=[pltpu.VMEM((3, rows, full, chans), BF)],
     )
     col_near, col_far = trade("wa", col_near, col_far)
+    row_near, part_one = lax.optimization_barrier((row_near, part_one))
     row_near, row_far = trade("ha", row_near, row_far)
     size = 6 * RIM * RIM
     corner_near, corner_far = trade(

time: 81.1 us -> 80.7 us (level)
  no operation moved by 1% of the time
where the time goes in v6:
time: 80.7 us; the launch traced here: 80.4 us
  blocking collectives  45.7 us (57%)
  Pallas kernels  17 us (21%)
  starting transfers between devices  14.3 us (18%)
  waiting for transfers between devices  1.64 us (2%)
  between operations  1.11 us (1%)
    all_to_all x2, blocking collectives, spread_out(): lax.all_to_all(value.reshape(chips, share, chans), BOTH, 0, 0, axis_index...  45.7 us
    pallas_call x9, Pallas kernels, call(): pl.pallas_call(body, out_shape=tuple(out_shape), cost_estimate=pl.CostEst...  17 us
    ppermute x3, starting transfers between devices, trade(): far = lax.ppermute(far, axis, second)  8.66 us
    ppermute x3, starting transfers between devices, trade(): return (lax.ppermute(near, axis, first), far)  2.75 us
    ppermute x1, starting transfers between devices, per_device(): other = lax.ppermute(one, 'ha', pairs)  2.68 us
  transfers between devices with their start and end apart: 8, of which 2 were waited for; matrix products, arithmetic and copies ran while one was open for 0% of the time, Pallas kernels for 10%

profile of v6, /device:TPU:1, one launch (start us, length us, event | category | flops | bytes accessed | tf_op | source)
XLA Modules:
  0.0 80.4 jit_solution(1822638896507735780)
XLA Ops:
  0.6 0.0 copy-start.9
  0.6 0.0 copy-start.8
  0.7 0.0 copy-start.7
  0.7 0.0 copy-start.6
  0.7 0.0 copy-start.1
  0.7 0.0 copy-start
  0.7 1.8 %pack.1 = (bf16[6,4,40,128]{3,2,1,0:T(8,128)(2,1)S(1)}, bf16[6,4,40,128]{3,2,1,0:T(8,128)(2,1)S(1)}, bf16[720,128]{1,0:T(8,128)(2,1)S(1)}, bf16[720,128]{1,0:T(8,128)(2,1)S(1)}) custom-call(bf16[2,30,40,128]{3,2,1,0:T(8,128)(2,1)} %refs_0_.7, bf16[1,30,40,128]{3,2,1,0:T(8,128)(2,1)} %refs_1_.7, bf16[2,30,40,128]{3,2,1,0:T(8,128)(2,1)} %refs_2_.5, ...), custom_call_target="tpu_custom_call" | custom-call | flops 1000000000 | bytes 8000000 | tf_op jit(solution)/shard_map/pack/pallas_call | solution.py:469
  2.5 2.1 %collective-permute-start = (bf16[720,128]{1,0:T(8,128)(2,1)S(1)}, bf16[720,128]{1,0:T(8,128)(2,1)S(1)}, u32[]{:S(2)}, u32[]{:S(2)}) collective-permute-start(bf16[720,128]{1,0:T(8,128)(2,1)S(1)} %get-tuple-element.30), channel_id=1, source_target_pairs={{0,1},{1,0},{2,3},{3,2},{4,5},{5,4},{6,7},{7,6},{8,9},{9,8},{10,11... | collective-permute-start | bytes 552968 | tf_op jit(solution)/shard_map/ppermute | solution.py:24
  4.6 0.7 collective-permute-start.1
  5.3 0.0 copy-start.2
  5.3 0.0 copy-start.4
  5.3 4.5 %collective-permute-start.3 = (bf16[6,4,40,128]{3,2,1,0:T(8,128)(2,1)S(1)}, bf16[6,4,40,128]{3,2,1,0:T(8,128)(2,1)S(1)}, u32[]{:S(2)}, u32[]{:S(2)}) collective-permute-start(bf16[6,4,40,128]{3,2,1,0:T(8,128)(2,1)S(1)} %get-tuple-element.43), channel_id=1, source_target_pairs={{16,32},{32,16},{48,64},{64,48},{80,96},{96,80},{17,33},{33,17},{4... | collective-permute-start | bytes 737288 | tf_op jit(solution)/shard_map/ppermute | solution.py:23
  9.8 0.0 copy-done.9
  9.8 0.0 copy-done.8
  9.8 0.0 copy-done.7
  9.8 0.0 copy-done.6
  9.8 0.0 copy-done.1
  9.9 0.0 copy-done
  9.9 0.4 ready.1
  10.2 0.0 copy-done.2
  10.2 0.0 copy-done.4
  10.3 0.0 copy-start.3
  10.3 0.0 copy-start.5
  10.3 1.9 %own.1.refs_6_ = f32[28,48,128]{2,1,0:T(8,128)S(1)} custom-call(bf16[2,30,40,128]{3,2,1,0:T(8,128)(2,1)S(1)} %copy-done.2, bf16[1,30,40,128]{3,2,1,0:T(8,128)(2,1)S(1)} %copy-done.4, bf16[1152,384]{1,0:T(8,128)(2,1)S(1)} %get-tuple-element.33.refs_2_.refs_7_.refs_9_), custom_call_target="tpu_custom_call" | custom-call | flops 3000000000 | bytes 8000000 | tf_op jit(solution)/shard_map/own/pallas_call | solution.py:469
  12.2 0.1 collective-permute-start.2
  12.3 0.0 collective-permute-done.refs_4_.refs_0_
  12.3 0.0 collective-permute-done.1.refs_5_.refs_1_
  12.4 0.5 collective-permute-start.4
  12.9 3.5 %collective-permute-start.5 = (bf16[192,128]{1,0:T(8,128)(2,1)S(1)}, bf16[192,128]{1,0:T(8,128)(2,1)S(1)}, u32[]{:S(2)}, u32[]{:S(2)}) collective-permute-start(bf16[192,128]{1,0:T(8,128)(2,1)S(1)} %get-tuple-element.45), channel_id=1, source_target_pairs={{16,32},{32,16},{48,64},{64,48},{80,96},{96,80},{17,33},{33,17},{4... | collective-permute-start | bytes 147464 | tf_op jit(solution)/shard_map/ppermute | solution.py:23
  16.4 0.0 copy-done.3
  16.4 0.0 copy-done.5
  16.4 2.6 %middle.1 = (bf16[6,30,48,128]{3,2,1,0:T(8,128)(2,1)S(1)}, f32[28,48,128]{2,1,0:T(8,128)S(1)}, bf16[28,48,128]{2,1,0:T(8,128)(2,1)S(1)}, bf16[26,48,128]{2,1,0:T(8,128)(2,1)S(1)}, bf16[26,48,384]{2,1,0:T(8,128)(2,1)S(1)}) custom-call(bf16[2,30,40,128]{3,2,1,0:T(8,128)(2,1)S(1)} %copy-done.2, bf16[1,30,40,128]{3,2,1,0:T(8,128)(2,1)S(1)} %copy-done.4, ...), custom_call_target="tpu_custom_call" | custom-call | flops 3000000000 | bytes 8000000 | tf_op jit(solution)/shard_map/middle/pallas_call | solution.py:469
  19.0 0.0 collective-permute-done.4.refs_7_
  19.0 0.0 collective-permute-done.5.refs_8_
  19.0 0.0 collective-permute-done.3.refs_6_
  19.0 0.0 collective-permute-done.2.refs_5_
  19.0 6.2 %rim.1 = (bf16[3584,128]{1,0:T(8,128)(2,1)S(1)}, bf16[3584,128]{1,0:T(8,128)(2,1)S(1)}, bf16[32,48,128]{2,1,0:T(8,128)(2,1)S(1)}) custom-call(bf16[6,30,48,128]{3,2,1,0:T(8,128)(2,1)S(1)} %get-tuple-element.37.refs_0_, f32[28,48,128]{2,1,0:T(8,128)S(1)} %get-tuple-element.38.refs_1_, bf16[28,48,128]{2,1,0:T(8,128)(2,1)S(1)} %get-tuple-element.39.refs_2_, ...), custom_call_target="tpu_custom_call" | custom-call | flops 5000000000 | bytes 8000000 | tf_op jit(solution)/shard_map/rim/pallas_call | solution.py:469
  25.2 0.3 collective-permute-start.6
  25.5 1.7 %input.1 = bf16[1,30,40,128]{3,2,1,0:T(8,128)(2,1)} custom-call(bf16[32,48,128]{2,1,0:T(8,128)(2,1)S(1)} %get-tuple-element.48.refs_0_, bf16[384,384]{1,0:T(8,128)(2,1)S(1)} %get-tuple-element.49.refs_1_), custom_call_target="tpu_custom_call" | custom-call | flops 1000000000 | bytes 8000000 | tf_op jit(solution)/shard_map/input/pallas_call | solution.py:469
  27.2 0.8 collective-permute-done.6
  28.0 0.2 add_convert_fusion
  28.2 25.5 %all_to_all.10 = bf16[64,56,128]{2,1,0:T(8,128)(2,1)S(1)} all-to-all(bf16[64,56,128]{2,1,0:T(8,128)(2,1)S(1)} %bitcast.6), channel_id=1, replica_groups={{111,110,109,108,107,106,105,104,103,102,101,100,99,98,97,96,79,78,77,7..., dimensions={0} | all-to-all | bytes 1835008 | tf_op jit(solution)/shard_map/all_to_all | solution.py:553
  53.7 0.2 convert_reduce_fusion
  53.8 0.1 broadcast_in_dim.2
  54.0 20.3 %all_to_all.11 = bf16[64,56,128]{2,1,0:T(8,128)(2,1)S(1)} all-to-all(bf16[64,56,128]{2,1,0:T(8,128)(2,1)S(1)} %broadcast_in_dim.2), channel_id=1, replica_groups={{111,110,109,108,107,106,105,104,103,102,101,100,99,98,97,96,79,78,77,7..., dimensions={0} | all-to-all | bytes 1835008 | tf_op jit(solution)/shard_map/all_to_all | solution.py:553
  74.2 2.7 %collective-permute-start.7 = (bf16[3584,128]{1,0:T(8,128)(2,1)S(1)}, bf16[3584,128]{1,0:T(8,128)(2,1)S(1)}, u32[]{:S(2)}, u32[]{:S(2)}) collective-permute-start(bf16[3584,128]{1,0:T(8,128)(2,1)S(1)} %bitcast.4), channel_id=1, source_target_pairs={{0,16},{16,0},{32,48},{48,32},{64,80},{80,64},{96,112},{112,96},{1... | collective-permute-start | bytes 2752520 | tf_op jit(solution)/shard_map/ppermute | solution.py:559
  76.9 1.3 %place.2 = (f32[3456,128]{1,0:T(8,128)}, f32[3456,128]{1,0:T(8,128)}) custom-call(bf16[3584,128]{1,0:T(8,128)(2,1)S(1)} %bitcast.5), custom_call_target="tpu_custom_call" | custom-call | flops 2000000000 | bytes 8000000 | tf_op jit(solution)/shard_map/place/pallas_call | solution.py:469
  78.2 0.8 %collective-permute-done.7.refs_0_ = bf16[3584,128]{1,0:T(8,128)(2,1)S(1)} collective-permute-done((bf16[3584,128]{1,0:T(8,128)(2,1)S(1)}, bf16[3584,128]{1,0:T(8,128)(2,1)S(1)}, u32[]{:S(2)}, u32[]{:S(2)}) %collective-permute-start.7) | collective-permute-done | bytes 917536 | tf_op jit(solution)/shard_map/ppermute | solution.py:559
  79.0 1.3 %place.3 = (f32[3456,128]{1,0:T(8,128)}, f32[3456,128]{1,0:T(8,128)}) custom-call(bf16[3584,128]{1,0:T(8,128)(2,1)S(1)} %collective-permute-done.7.refs_0_, f32[3456,128]{1,0:T(8,128)} %get-tuple-element.53.refs_1_, f32[3456,128]{1,0:T(8,128)} %get-tuple-element.54.refs_2_), custom_call_target="tpu_custom_call", output_to_operand_aliasing={{0}: (1, {}), {1}: (2, {})} | custom-call | flops 2000000000 | bytes 8000000 | tf_op jit(solution)/shard_map/place/pallas_call | solution.py:469
  (2 shorter events, 0.0 us)
Async XLA Ops:
  0.6 9.2 %copy-start.9 = (f32[1,128]{1,0:T(1,128)S(1)}, f32[1,128]{1,0:T(1,128)}, u32[]{:S(2)}) copy-start(f32[1,128]{1,0:T(1,128)} %refs_5_.1) | copy-start | bytes 1540
  0.6 9.2 %copy-start.8 = (f32[1,128]{1,0:T(1,128)S(1)}, f32[1,128]{1,0:T(1,128)}, u32[]{:S(2)}) copy-start(f32[1,128]{1,0:T(1,128)} %refs_4_.1) | copy-start | bytes 1540
  0.7 9.2 %copy-start.7 = (f32[1,128]{1,0:T(1,128)S(1)}, f32[1,128]{1,0:T(1,128)}, u32[]{:S(2)}) copy-start(f32[1,128]{1,0:T(1,128)} %refs_3_.4) | copy-start | bytes 1540
  0.7 9.2 %copy-start.6 = (f32[1,128]{1,0:T(1,128)S(1)}, f32[1,128]{1,0:T(1,128)}, u32[]{:S(2)}) copy-start(f32[1,128]{1,0:T(1,128)} %refs_2_.4) | copy-start | bytes 1540
  0.7 9.2 %copy-start.1 = (bf16[3,3,3,128,128]{4,3,2,1,0:T(8,128)(2,1)S(1)}, bf16[3,3,3,128,128]{4,3,2,1,0:T(8,128)(2,1)}, u32[]{:S(2)}) copy-start(bf16[3,3,3,128,128]{4,3,2,1,0:T(8,128)(2,1)} %refs_1_.5) | copy-start | bytes 2654212
  0.7 9.2 %copy-start = (bf16[3,3,3,128,128]{4,3,2,1,0:T(8,128)(2,1)S(1)}, bf16[3,3,3,128,128]{4,3,2,1,0:T(8,128)(2,1)}, u32[]{:S(2)}) copy-start(bf16[3,3,3,128,128]{4,3,2,1,0:T(8,128)(2,1)} %refs_0_.5) | copy-start | bytes 2654212
  2.5 9.8 %collective-permute-start = (bf16[720,128]{1,0:T(8,128)(2,1)S(1)}, bf16[720,128]{1,0:T(8,128)(2,1)S(1)}, u32[]{:S(2)}, u32[]{:S(2)}) collective-permute-start(bf16[720,128]{1,0:T(8,128)(2,1)S(1)} %get-tuple-element.30), channel_id=1, source_target_pairs={{0,1},{1,0},{2,3},{3,2},{4,5},{5,4},{6,7},{7,6},{8,9},{9,8},{10,11... | collective-permute-start | bytes 552968 | tf_op jit(solution)/shard_map/ppermute | solution.py:24
  4.6 7.7 %collective-permute-start.1 = (bf16[720,128]{1,0:T(8,128)(2,1)S(1)}, bf16[720,128]{1,0:T(8,128)(2,1)S(1)}, u32[]{:S(2)}, u32[]{:S(2)}) collective-permute-start(bf16[720,128]{1,0:T(8,128)(2,1)S(1)} %get-tuple-element.31), channel_id=1, source_target_pairs={{1,2},{2,1},{3,4},{4,3},{5,6},{6,5},{7,8},{8,7},{9,10},{10,9},{11,... | collective-permute-start | bytes 552968 | tf_op jit(solution)/shard_map/ppermute | solution.py:23
  5.3 5.0 %copy-start.2 = (bf16[2,30,40,128]{3,2,1,0:T(8,128)(2,1)S(1)}, bf16[2,30,40,128]{3,2,1,0:T(8,128)(2,1)}, u32[]{:S(2)}) copy-start(bf16[2,30,40,128]{3,2,1,0:T(8,128)(2,1)} %refs_0_.7) | copy-start | bytes 1843204
  5.3 5.0 %copy-start.4 = (bf16[1,30,40,128]{3,2,1,0:T(8,128)(2,1)S(1)}, bf16[1,30,40,128]{3,2,1,0:T(8,128)(2,1)}, u32[]{:S(2)}) copy-start(bf16[1,30,40,128]{3,2,1,0:T(8,128)(2,1)} %refs_1_.7) | copy-start | bytes 921604
  5.3 13.7 %collective-permute-start.3 = (bf16[6,4,40,128]{3,2,1,0:T(8,128)(2,1)S(1)}, bf16[6,4,40,128]{3,2,1,0:T(8,128)(2,1)S(1)}, u32[]{:S(2)}, u32[]{:S(2)}) collective-permute-start(bf16[6,4,40,128]{3,2,1,0:T(8,128)(2,1)S(1)} %get-tuple-element.43), channel_id=1, source_target_pairs={{16,32},{32,16},{48,64},{64,48},{80,96},{96,80},{17,33},{33,17},{4... | collective-permute-start | bytes 737288 | tf_op jit(solution)/shard_map/ppermute | solution.py:23
  10.3 6.1 %copy-start.3 = (bf16[2,30,40,128]{3,2,1,0:T(8,128)(2,1)S(1)}, bf16[2,30,40,128]{3,2,1,0:T(8,128)(2,1)}, u32[]{:S(2)}) copy-start(bf16[2,30,40,128]{3,2,1,0:T(8,128)(2,1)} %refs_2_.5) | copy-start | bytes 1843204
  10.3 6.1 %copy-start.5 = (bf16[1,30,40,128]{3,2,1,0:T(8,128)(2,1)S(1)}, bf16[1,30,40,128]{3,2,1,0:T(8,128)(2,1)}, u32[]{:S(2)}) copy-start(bf16[1,30,40,128]{3,2,1,0:T(8,128)(2,1)} %refs_3_.5) | copy-start | bytes 921604
  12.2 6.8 %collective-permute-start.2 = (bf16[6,4,40,128]{3,2,1,0:T(8,128)(2,1)S(1)}, bf16[6,4,40,128]{3,2,1,0:T(8,128)(2,1)S(1)}, u32[]{:S(2)}, u32[]{:S(2)}) collective-permute-start(bf16[6,4,40,128]{3,2,1,0:T(8,128)(2,1)S(1)} %get-tuple-element.42), channel_id=1, source_target_pairs={{0,16},{16,0},{32,48},{48,32},{64,80},{80,64},{96,112},{112,96},{1... | collective-permute-start | bytes 737288 | tf_op jit(solution)/shard_map/ppermute | solution.py:24
  12.4 6.7 %collective-permute-start.4 = (bf16[192,128]{1,0:T(8,128)(2,1)S(1)}, bf16[192,128]{1,0:T(8,128)(2,1)S(1)}, u32[]{:S(2)}, u32[]{:S(2)}) collective-permute-start(bf16[192,128]{1,0:T(8,128)(2,1)S(1)} %get-tuple-element.44), channel_id=1, source_target_pairs={{0,16},{16,0},{32,48},{48,32},{64,80},{80,64},{96,112},{112,96},{1... | collective-permute-start | bytes 147464 | tf_op jit(solution)/shard_map/ppermute | solution.py:24
  12.9 6.1 %collective-permute-start.5 = (bf16[192,128]{1,0:T(8,128)(2,1)S(1)}, bf16[192,128]{1,0:T(8,128)(2,1)S(1)}, u32[]{:S(2)}, u32[]{:S(2)}) collective-permute-start(bf16[192,128]{1,0:T(8,128)(2,1)S(1)} %get-tuple-element.45), channel_id=1, source_target_pairs={{16,32},{32,16},{48,64},{64,48},{80,96},{96,80},{17,33},{33,17},{4... | collective-permute-start | bytes 147464 | tf_op jit(solution)/shard_map/ppermute | solution.py:23
  25.2 2.7 %collective-permute-start.6 = (bf16[3584,128]{1,0:T(8,128)(2,1)S(1)}, bf16[3584,128]{1,0:T(8,128)(2,1)S(1)}, u32[]{:S(2)}, u32[]{:S(2)}) collective-permute-start(bf16[3584,128]{1,0:T(8,128)(2,1)S(1)} %get-tuple-element.47), channel_id=1, source_target_pairs={{0,16},{16,0},{32,48},{48,32},{64,80},{80,64},{96,112},{112,96},{1... | collective-permute-start | bytes 2752520 | tf_op jit(solution)/shard_map/ppermute | solution.py:543
  74.2 4.8 %collective-permute-start.7 = (bf16[3584,128]{1,0:T(8,128)(2,1)S(1)}, bf16[3584,128]{1,0:T(8,128)(2,1)S(1)}, u32[]{:S(2)}, u32[]{:S(2)}) collective-permute-start(bf16[3584,128]{1,0:T(8,128)(2,1)S(1)} %bitcast.4), channel_id=1, source_target_pairs={{0,16},{16,0},{32,48},{48,32},{64,80},{80,64},{96,112},{112,96},{1... | collective-permute-start | bytes 2752520 | tf_op jit(solution)/shard_map/ppermute | solution.py:559

commit v7 on v6

--- a/solution.py
+++ b/solution.py
@@ -238,8 +238,9 @@
     col_far[...] = jnp.stack(far, axis=1).reshape(-1, lanes).astype(BF)
 
 
-def corner_kernel(col_near, col_far, near, far):
-    size = near.shape[0] // 2
+def corner_kernel(row_near, col_near, col_far, near, far):
+    size = far.shape[0] // 2
+    near[2 * size :] = flat(row_near[...])
     last = col_near.shape[0] - size
     odd = is_odd("ha")
     for target, start in (
@@ -248,7 +249,7 @@
     ):
         at = pl.ds(pl.multiple_of(start, 16), size)
         target[:size] = col_near[at]
-        target[size:] = col_far[at]
+        target[size : 2 * size] = col_far[at]
 
 
 def ready_kernel(
@@ -307,29 +308,31 @@
 
 
 def rim_kernel(
-    rows, cols, field, slope_mid, a_mid, d_mid, moved_mid, row_near, row_far, corner_near, corner_far,
+    rows, cols, field, slope_mid, a_mid, d_mid, moved_mid, row_far, beside, corner_far,
     ahead_one, ahead_two, back_two, affine, keep, send, d_one,
     top, bottom, slope_rim, a_rim, d_rim, moved_rim, moved_one, grads, sems,
 ):
     lanes = affine.shape[-1]
     tall = rows + 2 * RIM
     core = lax.axis_index("ha") % 2
-    half = corner_near.shape[0] // 2
+    half = corner_far.shape[0] // 2
 
     def assemble(target, block, corner):
-        parts, _ = join([block[i] for i in range(6)], corner[:half], corner[half:])
+        parts, _ = join([block[i] for i in range(6)], corner[:half], corner[half : 2 * half])
         for frame, value in enumerate(parts):
             target[frame] = value
 
+    row_near = beside[2 * half :].reshape(row_far.shape)
+
     @pl.when(is_odd("ha"))
     def _():
-        assemble(top, row_near, corner_near)
+        assemble(top, row_near, beside)
         assemble(bottom, row_far, corner_far)
 
     @pl.when(jnp.logical_not(is_odd("ha")))
     def _():
         assemble(top, row_far, corner_far)
-        assemble(bottom, row_near, corner_near)
+        assemble(bottom, row_near, beside)
 
     whole = [
         Rows(
@@ -495,16 +498,18 @@
         scratch_shapes=[pltpu.VMEM((3, rows, full, chans), BF)],
     )
     col_near, col_far = trade("wa", col_near, col_far)
+    row_far = lax.ppermute(row_far, "ha", swaps("ha")[1])
     row_near, part_one = lax.optimization_barrier((row_near, part_one))
-    row_near, row_far = trade("ha", row_near, row_far)
     size = 6 * RIM * RIM
-    corner_near, corner_far = trade(
+    beside, corner_far = trade(
         "ha",
         *call(
-            corner_kernel, "corner", [shaped(2 * size, chans)] * 2, 4, 1e8, (col_near, col_far),
-            sizes=False,
+            corner_kernel, "corner",
+            (shaped(2 * size + 6 * RIM * cols, chans), shaped(2 * size, chans)), 4, 1e8,
+            (row_near, col_near, col_far), sizes=False,
         ),
     )
+    part_one, row_far = lax.optimization_barrier((part_one, row_far))
 
     field, slope_mid, a_mid, d_mid, moved_mid = call(
         middle_kernel, "middle",
@@ -522,7 +527,7 @@
         (shaped(share * chips, chans), shaped(share * chips, chans), shaped(rows + 2, full, chans)),
         20, 5e9,
         (
-            field, slope_mid, a_mid, d_mid, moved_mid, row_near, row_far, corner_near, corner_far,
+            field, slope_mid, a_mid, d_mid, moved_mid, row_far, beside, corner_far,
             ahead_one, ahead_two, back_two, affine,
         ),
         out_specs=(anywhere, anywhere, inner),

time: 80.7 us -> 80.6 us (level)
    ppermute x0 -> x1, starting transfers between devices: none -> 4.52 us  [per_device(): row_far = lax.ppermute(row_far, 'ha', swaps('ha')[1])]
    ppermute x3 -> x2, starting transfers between devices: 8.66 us -> 4.57 us  [trade(): far = lax.ppermute(far, axis, second)]
    ppermute x3 -> x2, starting transfers between devices: 2.75 us -> 2.21 us  [trade(): return (lax.ppermute(near, axis, first), far)]
  transfers between devices with their start and end apart: 8 -> 7, of which waited for: 2 -> 2; matrix products, arithmetic and copies ran while one was open for 0% -> 0% of each run, Pallas kernels for 10% -> 10%
where the time goes in v7:
time: 80.6 us; the launch traced here: 80.3 us
  blocking collectives  45.9 us (57%)
  Pallas kernels  17 us (21%)
  starting transfers between devices  14.1 us (17%)
  waiting for transfers between devices  1.65 us (2%)
  between operations  1.1 us (1%)
    all_to_all x2, blocking collectives, spread_out(): lax.all_to_all(value.reshape(chips, share, chans), BOTH, 0, 0, axis_index...  45.9 us
    pallas_call x9, Pallas kernels, call(): pl.pallas_call(body, out_shape=tuple(out_shape), cost_estimate=pl.CostEst...  17 us
    ppermute x2, starting transfers between devices, trade(): far = lax.ppermute(far, axis, second)  4.57 us
    ppermute x1, starting transfers between devices, per_device(): row_far = lax.ppermute(row_far, 'ha', swaps('ha')[1])  4.52 us
    ppermute x1, starting transfers between devices, per_device(): other = lax.ppermute(one, 'ha', pairs)  2.68 us
    ppermute x2, starting transfers between devices, trade(): return (lax.ppermute(near, axis, first), far)  2.21 us
  transfers between devices with their start and end apart: 7, of which 2 were waited for; matrix products, arithmetic and copies ran while one was open for 0% of the time, Pallas kernels for 10%

profile of v7, /device:TPU:1, one launch (start us, length us, event | category | flops | bytes accessed | tf_op | source)
XLA Modules:
  0.0 80.3 jit_solution(14599214869405402065)
XLA Ops:
  0.6 0.0 copy-start.9
  0.6 0.0 copy-start.8
  0.7 0.0 copy-start.7
  0.7 0.0 copy-start.6
  0.7 0.0 copy-start.1
  0.7 0.0 copy-start
  0.7 1.8 %pack.1 = (bf16[6,4,40,128]{3,2,1,0:T(8,128)(2,1)S(1)}, bf16[6,4,40,128]{3,2,1,0:T(8,128)(2,1)S(1)}, bf16[720,128]{1,0:T(8,128)(2,1)S(1)}, bf16[720,128]{1,0:T(8,128)(2,1)S(1)}) custom-call(bf16[2,30,40,128]{3,2,1,0:T(8,128)(2,1)} %refs_0_.7, bf16[1,30,40,128]{3,2,1,0:T(8,128)(2,1)} %refs_1_.7, bf16[2,30,40,128]{3,2,1,0:T(8,128)(2,1)} %refs_2_.5, ...), custom_call_target="tpu_custom_call" | custom-call | flops 1000000000 | bytes 8000000 | tf_op jit(solution)/shard_map/pack/pallas_call | solution.py:472
  2.5 2.1 %collective-permute-start = (bf16[720,128]{1,0:T(8,128)(2,1)S(1)}, bf16[720,128]{1,0:T(8,128)(2,1)S(1)}, u32[]{:S(2)}, u32[]{:S(2)}) collective-permute-start(bf16[720,128]{1,0:T(8,128)(2,1)S(1)} %get-tuple-element.32), channel_id=1, source_target_pairs={{0,1},{1,0},{2,3},{3,2},{4,5},{5,4},{6,7},{7,6},{8,9},{9,8},{10,11... | collective-permute-start | bytes 552968 | tf_op jit(solution)/shard_map/ppermute | solution.py:24
  4.6 0.7 collective-permute-start.1
  5.3 0.0 copy-start.2
  5.3 0.0 copy-start.4
  5.3 4.5 %collective-permute-start.2 = (bf16[6,4,40,128]{3,2,1,0:T(8,128)(2,1)S(1)}, bf16[6,4,40,128]{3,2,1,0:T(8,128)(2,1)S(1)}, u32[]{:S(2)}, u32[]{:S(2)}) collective-permute-start(bf16[6,4,40,128]{3,2,1,0:T(8,128)(2,1)S(1)} %get-tuple-element.37), channel_id=1, source_target_pairs={{16,32},{32,16},{48,64},{64,48},{80,96},{96,80},{17,33},{33,17},{4... | collective-permute-start | bytes 737288 | tf_op jit(solution)/shard_map/ppermute | solution.py:501
  9.8 0.0 copy-done.9
  9.8 0.0 copy-done.8
  9.8 0.0 copy-done.7
  9.8 0.0 copy-done.6
  9.8 0.0 copy-done.1
  9.9 0.0 copy-done
  9.9 0.4 ready.1
  10.2 0.0 copy-done.2
  10.2 0.0 copy-done.4
  10.3 0.0 copy-start.3
  10.3 0.0 copy-start.5
  10.3 1.9 %own.1.refs_6_ = f32[28,48,128]{2,1,0:T(8,128)S(1)} custom-call(bf16[2,30,40,128]{3,2,1,0:T(8,128)(2,1)S(1)} %copy-done.2, bf16[1,30,40,128]{3,2,1,0:T(8,128)(2,1)S(1)} %copy-done.4, bf16[1152,384]{1,0:T(8,128)(2,1)S(1)} %get-tuple-element.35.refs_2_.refs_7_.refs_8_), custom_call_target="tpu_custom_call" | custom-call | flops 3000000000 | bytes 8000000 | tf_op jit(solution)/shard_map/own/pallas_call | solution.py:472
  12.2 0.0 collective-permute-done.refs_4_.refs_1_
  12.2 0.0 collective-permute-done.1.refs_5_.refs_2_
  12.3 0.1 collective-permute-start.3
  12.4 3.9 %collective-permute-start.4 = (bf16[192,128]{1,0:T(8,128)(2,1)S(1)}, bf16[192,128]{1,0:T(8,128)(2,1)S(1)}, u32[]{:S(2)}, u32[]{:S(2)}) collective-permute-start(bf16[192,128]{1,0:T(8,128)(2,1)S(1)} %get-tuple-element.49), channel_id=1, source_target_pairs={{16,32},{32,16},{48,64},{64,48},{80,96},{96,80},{17,33},{33,17},{4... | collective-permute-start | bytes 147464 | tf_op jit(solution)/shard_map/ppermute | solution.py:23
  16.3 0.0 collective-permute-done.2.refs_5_
  16.3 0.0 copy-done.3
  16.3 0.0 copy-done.5
  16.3 2.6 %middle.1 = (bf16[6,30,48,128]{3,2,1,0:T(8,128)(2,1)S(1)}, f32[28,48,128]{2,1,0:T(8,128)S(1)}, bf16[28,48,128]{2,1,0:T(8,128)(2,1)S(1)}, bf16[26,48,128]{2,1,0:T(8,128)(2,1)S(1)}, bf16[26,48,384]{2,1,0:T(8,128)(2,1)S(1)}) custom-call(bf16[2,30,40,128]{3,2,1,0:T(8,128)(2,1)S(1)} %copy-done.2, bf16[1,30,40,128]{3,2,1,0:T(8,128)(2,1)S(1)} %copy-done.4, ...), custom_call_target="tpu_custom_call" | custom-call | flops 3000000000 | bytes 8000000 | tf_op jit(solution)/shard_map/middle/pallas_call | solution.py:472
  18.9 0.0 collective-permute-done.4.refs_7_
  18.9 0.0 collective-permute-done.3.refs_6_
  18.9 6.2 %rim.1 = (bf16[3584,128]{1,0:T(8,128)(2,1)S(1)}, bf16[3584,128]{1,0:T(8,128)(2,1)S(1)}, bf16[32,48,128]{2,1,0:T(8,128)(2,1)S(1)}) custom-call(bf16[6,30,48,128]{3,2,1,0:T(8,128)(2,1)S(1)} %get-tuple-element.41.refs_0_, f32[28,48,128]{2,1,0:T(8,128)S(1)} %get-tuple-element.42.refs_1_, bf16[28,48,128]{2,1,0:T(8,128)(2,1)S(1)} %get-tuple-element.43.refs_2_, ...), custom_call_target="tpu_custom_call" | custom-call | flops 5000000000 | bytes 8000000 | tf_op jit(solution)/shard_map/rim/pallas_call | solution.py:472
  25.1 0.1 collective-permute-start.5
  25.2 1.7 %input.1 = bf16[1,30,40,128]{3,2,1,0:T(8,128)(2,1)} custom-call(bf16[32,48,128]{2,1,0:T(8,128)(2,1)S(1)} %get-tuple-element.52.refs_0_, bf16[384,384]{1,0:T(8,128)(2,1)S(1)} %get-tuple-element.53.refs_1_), custom_call_target="tpu_custom_call" | custom-call | flops 1000000000 | bytes 8000000 | tf_op jit(solution)/shard_map/input/pallas_call | solution.py:472
  26.9 0.8 %collective-permute-done.5 = bf16[3584,128]{1,0:T(8,128)(2,1)S(1)} collective-permute-done((bf16[3584,128]{1,0:T(8,128)(2,1)S(1)}, bf16[3584,128]{1,0:T(8,128)(2,1)S(1)}, u32[]{:S(2)}, u32[]{:S(2)}) %collective-permute-start.5) | collective-permute-done | bytes 917536 | tf_op jit(solution)/shard_map/ppermute | solution.py:548
  27.7 0.2 add_convert_fusion
  27.9 25.7 %all_to_all.10 = bf16[64,56,128]{2,1,0:T(8,128)(2,1)S(1)} all-to-all(bf16[64,56,128]{2,1,0:T(8,128)(2,1)S(1)} %bitcast.6), channel_id=1, replica_groups={{111,110,109,108,107,106,105,104,103,102,101,100,99,98,97,96,79,78,77,7..., dimensions={0} | all-to-all | bytes 1835008 | tf_op jit(solution)/shard_map/all_to_all | solution.py:558
  53.6 0.2 convert_reduce_fusion
  53.7 0.1 broadcast_in_dim.2
  53.9 20.3 %all_to_all.11 = bf16[64,56,128]{2,1,0:T(8,128)(2,1)S(1)} all-to-all(bf16[64,56,128]{2,1,0:T(8,128)(2,1)S(1)} %broadcast_in_dim.2), channel_id=1, replica_groups={{111,110,109,108,107,106,105,104,103,102,101,100,99,98,97,96,79,78,77,7..., dimensions={0} | all-to-all | bytes 1835008 | tf_op jit(solution)/shard_map/all_to_all | solution.py:558
  74.1 2.7 %collective-permute-start.6 = (bf16[3584,128]{1,0:T(8,128)(2,1)S(1)}, bf16[3584,128]{1,0:T(8,128)(2,1)S(1)}, u32[]{:S(2)}, u32[]{:S(2)}) collective-permute-start(bf16[3584,128]{1,0:T(8,128)(2,1)S(1)} %bitcast.4), channel_id=1, source_target_pairs={{0,16},{16,0},{32,48},{48,32},{64,80},{80,64},{96,112},{112,96},{1... | collective-permute-start | bytes 2752520 | tf_op jit(solution)/shard_map/ppermute | solution.py:564
  76.8 1.3 %place.2 = (f32[3456,128]{1,0:T(8,128)}, f32[3456,128]{1,0:T(8,128)}) custom-call(bf16[3584,128]{1,0:T(8,128)(2,1)S(1)} %bitcast.5), custom_call_target="tpu_custom_call" | custom-call | flops 2000000000 | bytes 8000000 | tf_op jit(solution)/shard_map/place/pallas_call | solution.py:472
  78.1 0.8 %collective-permute-done.6.refs_0_ = bf16[3584,128]{1,0:T(8,128)(2,1)S(1)} collective-permute-done((bf16[3584,128]{1,0:T(8,128)(2,1)S(1)}, bf16[3584,128]{1,0:T(8,128)(2,1)S(1)}, u32[]{:S(2)}, u32[]{:S(2)}) %collective-permute-start.6) | collective-permute-done | bytes 917536 | tf_op jit(solution)/shard_map/ppermute | solution.py:564
  78.9 1.3 %place.3 = (f32[3456,128]{1,0:T(8,128)}, f32[3456,128]{1,0:T(8,128)}) custom-call(bf16[3584,128]{1,0:T(8,128)(2,1)S(1)} %collective-permute-done.6.refs_0_, f32[3456,128]{1,0:T(8,128)} %get-tuple-element.57.refs_1_, f32[3456,128]{1,0:T(8,128)} %get-tuple-element.58.refs_2_), custom_call_target="tpu_custom_call", output_to_operand_aliasing={{0}: (1, {}), {1}: (2, {})} | custom-call | flops 2000000000 | bytes 8000000 | tf_op jit(solution)/shard_map/place/pallas_call | solution.py:472
  (2 shorter events, 0.0 us)
Async XLA Ops:
  0.6 9.2 %copy-start.9 = (f32[1,128]{1,0:T(1,128)S(1)}, f32[1,128]{1,0:T(1,128)}, u32[]{:S(2)}) copy-start(f32[1,128]{1,0:T(1,128)} %refs_5_.1) | copy-start | bytes 1540
  0.6 9.2 %copy-start.8 = (f32[1,128]{1,0:T(1,128)S(1)}, f32[1,128]{1,0:T(1,128)}, u32[]{:S(2)}) copy-start(f32[1,128]{1,0:T(1,128)} %refs_4_.1) | copy-start | bytes 1540
  0.7 9.2 %copy-start.7 = (f32[1,128]{1,0:T(1,128)S(1)}, f32[1,128]{1,0:T(1,128)}, u32[]{:S(2)}) copy-start(f32[1,128]{1,0:T(1,128)} %refs_3_.4) | copy-start | bytes 1540
  0.7 9.2 %copy-start.6 = (f32[1,128]{1,0:T(1,128)S(1)}, f32[1,128]{1,0:T(1,128)}, u32[]{:S(2)}) copy-start(f32[1,128]{1,0:T(1,128)} %refs_2_.4) | copy-start | bytes 1540
  0.7 9.2 %copy-start.1 = (bf16[3,3,3,128,128]{4,3,2,1,0:T(8,128)(2,1)S(1)}, bf16[3,3,3,128,128]{4,3,2,1,0:T(8,128)(2,1)}, u32[]{:S(2)}) copy-start(bf16[3,3,3,128,128]{4,3,2,1,0:T(8,128)(2,1)} %refs_1_.5) | copy-start | bytes 2654212
  0.7 9.2 %copy-start = (bf16[3,3,3,128,128]{4,3,2,1,0:T(8,128)(2,1)S(1)}, bf16[3,3,3,128,128]{4,3,2,1,0:T(8,128)(2,1)}, u32[]{:S(2)}) copy-start(bf16[3,3,3,128,128]{4,3,2,1,0:T(8,128)(2,1)} %refs_0_.5) | copy-start | bytes 2654212
  2.5 9.7 %collective-permute-start = (bf16[720,128]{1,0:T(8,128)(2,1)S(1)}, bf16[720,128]{1,0:T(8,128)(2,1)S(1)}, u32[]{:S(2)}, u32[]{:S(2)}) collective-permute-start(bf16[720,128]{1,0:T(8,128)(2,1)S(1)} %get-tuple-element.32), channel_id=1, source_target_pairs={{0,1},{1,0},{2,3},{3,2},{4,5},{5,4},{6,7},{7,6},{8,9},{9,8},{10,11... | collective-permute-start | bytes 552968 | tf_op jit(solution)/shard_map/ppermute | solution.py:24
  4.6 7.6 %collective-permute-start.1 = (bf16[720,128]{1,0:T(8,128)(2,1)S(1)}, bf16[720,128]{1,0:T(8,128)(2,1)S(1)}, u32[]{:S(2)}, u32[]{:S(2)}) collective-permute-start(bf16[720,128]{1,0:T(8,128)(2,1)S(1)} %get-tuple-element.33), channel_id=1, source_target_pairs={{1,2},{2,1},{3,4},{4,3},{5,6},{6,5},{7,8},{8,7},{9,10},{10,9},{11,... | collective-permute-start | bytes 552968 | tf_op jit(solution)/shard_map/ppermute | solution.py:23
  5.3 5.0 %copy-start.2 = (bf16[2,30,40,128]{3,2,1,0:T(8,128)(2,1)S(1)}, bf16[2,30,40,128]{3,2,1,0:T(8,128)(2,1)}, u32[]{:S(2)}) copy-start(bf16[2,30,40,128]{3,2,1,0:T(8,128)(2,1)} %refs_0_.7) | copy-start | bytes 1843204
  5.3 5.0 %copy-start.4 = (bf16[1,30,40,128]{3,2,1,0:T(8,128)(2,1)S(1)}, bf16[1,30,40,128]{3,2,1,0:T(8,128)(2,1)}, u32[]{:S(2)}) copy-start(bf16[1,30,40,128]{3,2,1,0:T(8,128)(2,1)} %refs_1_.7) | copy-start | bytes 921604
  5.3 11.0 %collective-permute-start.2 = (bf16[6,4,40,128]{3,2,1,0:T(8,128)(2,1)S(1)}, bf16[6,4,40,128]{3,2,1,0:T(8,128)(2,1)S(1)}, u32[]{:S(2)}, u32[]{:S(2)}) collective-permute-start(bf16[6,4,40,128]{3,2,1,0:T(8,128)(2,1)S(1)} %get-tuple-element.37), channel_id=1, source_target_pairs={{16,32},{32,16},{48,64},{64,48},{80,96},{96,80},{17,33},{33,17},{4... | collective-permute-start | bytes 737288 | tf_op jit(solution)/shard_map/ppermute | solution.py:501
  10.3 6.0 %copy-start.3 = (bf16[2,30,40,128]{3,2,1,0:T(8,128)(2,1)S(1)}, bf16[2,30,40,128]{3,2,1,0:T(8,128)(2,1)}, u32[]{:S(2)}) copy-start(bf16[2,30,40,128]{3,2,1,0:T(8,128)(2,1)} %refs_2_.5) | copy-start | bytes 1843204
  10.3 6.0 %copy-start.5 = (bf16[1,30,40,128]{3,2,1,0:T(8,128)(2,1)S(1)}, bf16[1,30,40,128]{3,2,1,0:T(8,128)(2,1)}, u32[]{:S(2)}) copy-start(bf16[1,30,40,128]{3,2,1,0:T(8,128)(2,1)} %refs_3_.5) | copy-start | bytes 921604
  12.3 6.7 %collective-permute-start.3 = (bf16[1152,128]{1,0:T(8,128)(2,1)S(1)}, bf16[1152,128]{1,0:T(8,128)(2,1)S(1)}, u32[]{:S(2)}, u32[]{:S(2)}) collective-permute-start(bf16[1152,128]{1,0:T(8,128)(2,1)S(1)} %get-tuple-element.48), channel_id=1, source_target_pairs={{0,16},{16,0},{32,48},{48,32},{64,80},{80,64},{96,112},{112,96},{1... | collective-permute-start | bytes 884744 | tf_op jit(solution)/shard_map/ppermute | solution.py:24
  12.4 6.6 %collective-permute-start.4 = (bf16[192,128]{1,0:T(8,128)(2,1)S(1)}, bf16[192,128]{1,0:T(8,128)(2,1)S(1)}, u32[]{:S(2)}, u32[]{:S(2)}) collective-permute-start(bf16[192,128]{1,0:T(8,128)(2,1)S(1)} %get-tuple-element.49), channel_id=1, source_target_pairs={{16,32},{32,16},{48,64},{64,48},{80,96},{96,80},{17,33},{33,17},{4... | collective-permute-start | bytes 147464 | tf_op jit(solution)/shard_map/ppermute | solution.py:23
  25.1 2.6 %collective-permute-start.5 = (bf16[3584,128]{1,0:T(8,128)(2,1)S(1)}, bf16[3584,128]{1,0:T(8,128)(2,1)S(1)}, u32[]{:S(2)}, u32[]{:S(2)}) collective-permute-start(bf16[3584,128]{1,0:T(8,128)(2,1)S(1)} %get-tuple-element.51), channel_id=1, source_target_pairs={{0,16},{16,0},{32,48},{48,32},{64,80},{80,64},{96,112},{112,96},{1... | collective-permute-start | bytes 2752520 | tf_op jit(solution)/shard_map/ppermute | solution.py:548
  74.1 4.8 %collective-permute-start.6 = (bf16[3584,128]{1,0:T(8,128)(2,1)S(1)}, bf16[3584,128]{1,0:T(8,128)(2,1)S(1)}, u32[]{:S(2)}, u32[]{:S(2)}) collective-permute-start(bf16[3584,128]{1,0:T(8,128)(2,1)S(1)} %bitcast.4), channel_id=1, source_target_pairs={{0,16},{16,0},{32,48},{48,32},{64,80},{80,64},{96,112},{112,96},{1... | collective-permute-start | bytes 2752520 | tf_op jit(solution)/shard_map/ppermute | solution.py:564
